TPU v7x, 128 devices: a whole 4x4x4 slice. The times are simulated.
128 devices in a mesh: dp: 4 (over z_hi, core), fsdp: 32 (over z_lo, x, y).
Axes of the slice: x: 4, y: 4, z: 4 (z_hi: 2, z_lo: 2; z = z_hi * 2 + z_lo), core: 2. Of those that a mesh axis runs over, the one named last changes fastest.
Arguments:
- tokens: bfloat16 [2, 128, 128, 896], P(None, ('dp', 'fsdp')), may hold values from -6 to 6
- segments: int32 [2, 128, 128], P(None, ('dp', 'fsdp')), may hold values from 0 to 3, never falling along the last dimension, each value on 1 to 64 neighbouring positions
- w_query: bfloat16 [896, 896], P(('dp', 'fsdp')), may hold values from -0.1875 to 0.1875
- w_key: bfloat16 [896, 128], P(('dp', 'fsdp')), may hold values from -0.1875 to 0.1875
- w_value: bfloat16 [896, 128], P(('dp', 'fsdp')), may hold values from -0.1875 to 0.1875
- w_out: bfloat16 [896, 896], P(('dp', 'fsdp')), may hold values from -0.5 to 0.5
- w_gate: bfloat16 [896, 4864], P(('dp', 'fsdp')), may hold values from -0.1875 to 0.1875
- w_up: bfloat16 [896, 4864], P(('dp', 'fsdp')), may hold values from -0.1875 to 0.1875
- w_down: bfloat16 [4864, 896], P(('dp', 'fsdp')), may hold values from -0.078125 to 0.078125
- gains: bfloat16 [896, 2], P(('dp', 'fsdp')), may hold values from 0.099609375 to 1.8984375
- biases: bfloat16 [1152], P(('dp', 'fsdp')), may hold values from -3 to 3
- cotangent: bfloat16 [2, 128, 128, 896], P(None, ('dp', 'fsdp')), may hold values from -6 to 6
Outputs:
- block_out: bfloat16 [2, 128, 128, 896], P(None, ('dp', 'fsdp'))
- grad_tokens: bfloat16 [2, 128, 128, 896], P(None, ('dp', 'fsdp'))
- grad_query: float32 [896, 896], P(('dp', 'fsdp'))
- grad_key: float32 [896, 128], P(('dp', 'fsdp'))
- grad_value: float32 [896, 128], P(('dp', 'fsdp'))
- grad_outproj: float32 [896, 896], P(('dp', 'fsdp'))
- grad_gate: float32 [896, 4864], P(('dp', 'fsdp'))
- grad_up: float32 [896, 4864], P(('dp', 'fsdp'))
- grad_down: float32 [4864, 896], P(('dp', 'fsdp'))
- grad_gains: float32 [896, 2], P(('dp', 'fsdp'))
- grad_biases: float32 [1152], P(('dp', 'fsdp'))
Inputs may be any that keep to these rules, and one draw needn't show every extreme that they name: `segments`: within each sequence the document numbers never fall; each of the 4 documents holds 1 to half of 128 tokens.
All inputs are finite; a program needn't handle non-finite values.
Results may differ from a plain program's by a relative error of at most 0.017.
Values may be sent and summed in bfloat16 or wider, within the bound.
A program may use at most 256 MiB of HBM per device.

v0:
```python
import math

import jax
import jax.numpy as jnp
from jax import lax
from jax.sharding import PartitionSpec as P

HD = 64


EPSILON = 1e-06
THETA = 1000000.0
NEG_FILL = -1e30


def positions(segment_ids):
    last_axis = segment_ids.ndim - 1
    counter = lax.broadcasted_iota(jnp.int32, segment_ids.shape, last_axis)
    starts = jnp.concatenate(
        [
            jnp.ones(segment_ids.shape[:-1] + (1,), dtype=jnp.bool_),
            segment_ids[..., 1:] != segment_ids[..., :-1],
        ],
        axis=last_axis,
    )
    first_index = lax.cummax(jnp.where(starts, counter, 0), axis=last_axis)
    return counter - first_index


def rope_tables(position, head_size):
    half_size = head_size // 2
    exponent = jnp.arange(half_size, dtype=jnp.float32) * (2.0 / head_size)
    inverse = jnp.power(THETA, -exponent)
    angles = position.astype(jnp.float32)[..., None] * inverse
    cosine = jnp.cos(angles)
    sine = jnp.sin(angles)
    return (jnp.concatenate([cosine, cosine], axis=-1), jnp.concatenate([sine, sine], axis=-1))


def rotate(tensor, cosine, sine):
    half_size = tensor.shape[-1] // 2
    turned = jnp.concatenate([-tensor[..., half_size:], tensor[..., :half_size]], axis=-1)
    return tensor * cosine + turned * sine


def rotate_back(tensor, cosine, sine):
    half_size = tensor.shape[-1] // 2
    scaled = tensor * sine
    turned = jnp.concatenate([scaled[..., half_size:], -scaled[..., :half_size]], axis=-1)
    return tensor * cosine + turned


def attention_mask(segment_ids):
    length = segment_ids.shape[-1]
    row_index = lax.broadcasted_iota(jnp.int32, (length, length), 0)
    col_index = lax.broadcasted_iota(jnp.int32, (length, length), 1)
    same_doc = segment_ids[:, :, None] == segment_ids[:, None, :]
    return jnp.logical_and((col_index <= row_index)[None], same_doc)[:, None, None, :, :]


def score_block(queries, key_rot, allowed):
    raw_scores = jnp.einsum(
        "bqcrd,bkcd->bcrqk", queries, key_rot, preferred_element_type=jnp.float32
    ) * (1.0 / math.sqrt(HD))
    return jnp.where(allowed, raw_scores, NEG_FILL)


def times_transpose(left, right):
    return jnp.einsum("nf,df->nd", left, right, preferred_element_type=jnp.float32)


def outer_sum(left, right):
    return jnp.einsum("nd,nf->df", left, right, preferred_element_type=jnp.float32)


def norm_back(grad_normed, source, inv_root, gain):
    scaled = grad_normed * gain
    return inv_root * scaled - source * inv_root**3 * jnp.mean(
        scaled * source, axis=-1, keepdims=True
    )


def attention_core(normed, segment_ids, w_query, w_key, w_value, bias_q, bias_k, bias_v):
    seq_count, length = segment_ids.shape
    rows = seq_count * length
    q_heads = w_query.shape[1] // HD
    kv_heads = w_key.shape[1] // HD
    query_raw = jnp.dot(normed, w_query, preferred_element_type=jnp.float32) + bias_q.astype(
        jnp.float32
    )
    key_raw = jnp.dot(normed, w_key, preferred_element_type=jnp.float32) + bias_k.astype(
        jnp.float32
    )
    value_raw = jnp.dot(normed, w_value, preferred_element_type=jnp.float32) + bias_v.astype(
        jnp.float32
    )
    cosine, sine = rope_tables(positions(segment_ids), HD)
    cosine = cosine.reshape(rows, 1, HD)
    sine = sine.reshape(rows, 1, HD)
    queries = (
        rotate(query_raw.reshape(rows, q_heads, HD), cosine, sine)
        .astype(jnp.bfloat16)
        .reshape(seq_count, length, kv_heads, q_heads // kv_heads, HD)
    )
    key_rot = (
        rotate(key_raw.reshape(rows, kv_heads, HD), cosine, sine)
        .astype(jnp.bfloat16)
        .reshape(seq_count, length, kv_heads, HD)
    )
    values = value_raw.astype(jnp.bfloat16).reshape(seq_count, length, kv_heads, HD)
    allowed = attention_mask(segment_ids)
    scores = score_block(queries, key_rot, allowed)
    peak = jnp.max(scores, axis=-1, keepdims=True)
    shifted_exp = jnp.exp(scores - peak)
    totals = jnp.sum(shifted_exp, axis=-1, keepdims=True)
    soft_weights = shifted_exp / totals
    log_total = peak + jnp.log(totals)
    mixed = (
        jnp.einsum(
            "bcrqk,bkcd->bqcrd",
            soft_weights.astype(jnp.bfloat16),
            values,
            preferred_element_type=jnp.float32,
        )
        .astype(jnp.bfloat16)
        .reshape(rows, q_heads * HD)
    )
    return (mixed, (queries, key_rot, values, log_total, cosine, sine, allowed))


def attention_core_back(grad_mixed, saved, normed, w_query, w_key, w_value):
    queries, key_rot, values, log_total, cosine, sine, allowed = saved
    rows = normed.shape[0]
    q_heads = queries.shape[2] * queries.shape[3]
    kv_heads = key_rot.shape[2]
    grad_heads = grad_mixed.reshape(queries.shape)
    scores = score_block(queries, key_rot, allowed)
    soft_weights = jnp.where(allowed, jnp.exp(scores - log_total), 0.0)
    grad_soft = jnp.einsum(
        "bqcrd,bkcd->bcrqk", grad_heads, values, preferred_element_type=jnp.float32
    )
    inner_term = jnp.sum(soft_weights * grad_soft, axis=-1, keepdims=True)
    grad_scores = (soft_weights * (grad_soft - inner_term)).astype(jnp.bfloat16)
    scale = 1.0 / math.sqrt(HD)
    grad_queries = (
        jnp.einsum("bcrqk,bkcd->bqcrd", grad_scores, key_rot, preferred_element_type=jnp.float32)
        * scale
    )
    grad_keys = (
        jnp.einsum("bcrqk,bqcrd->bkcd", grad_scores, queries, preferred_element_type=jnp.float32)
        * scale
    )
    grad_values = jnp.einsum(
        "bcrqk,bqcrd->bkcd",
        soft_weights.astype(jnp.bfloat16),
        grad_heads,
        preferred_element_type=jnp.float32,
    )
    grad_qraw = (
        rotate_back(grad_queries.reshape(rows, q_heads, HD), cosine, sine)
        .reshape(rows, q_heads * HD)
        .astype(jnp.bfloat16)
    )
    grad_kraw = (
        rotate_back(grad_keys.reshape(rows, kv_heads, HD), cosine, sine)
        .reshape(rows, kv_heads * HD)
        .astype(jnp.bfloat16)
    )
    grad_vraw = grad_values.reshape(rows, kv_heads * HD).astype(jnp.bfloat16)
    grad_normed = (
        times_transpose(grad_qraw, w_query)
        + times_transpose(grad_kraw, w_key)
        + times_transpose(grad_vraw, w_value)
    )
    weight_grads = (
        outer_sum(normed, grad_qraw),
        outer_sum(normed, grad_kraw),
        outer_sum(normed, grad_vraw),
    )
    bias_grads = (
        jnp.sum(grad_qraw.astype(jnp.float32), axis=0),
        jnp.sum(grad_kraw.astype(jnp.float32), axis=0),
        jnp.sum(grad_vraw.astype(jnp.float32), axis=0),
    )
    return (grad_normed, weight_grads, bias_grads)


def run_batch(
    block_in,
    segment_ids,
    grad_out,
    attn_first,
    ffn_first,
    ffn_second,
    attn_second,
    gather_pair,
    sum_pair,
):
    seq_count, length, width = block_in.shape
    rows = seq_count * length
    w_query, w_key, w_value, w_out, gains, bias_q, bias_k, bias_v = attn_first()
    source = block_in.astype(jnp.float32).reshape(rows, width)
    inv_one = lax.rsqrt(jnp.mean(source * source, axis=-1, keepdims=True) + EPSILON)
    gain_one = gains[:, 0].astype(jnp.float32)
    gain_two = gains[:, 1].astype(jnp.float32)
    normed = gather_pair((source * inv_one * gain_one).astype(jnp.bfloat16))
    mixed, attn_saved = attention_core(
        normed, segment_ids, w_query, w_key, w_value, bias_q, bias_k, bias_v
    )
    resid = source + sum_pair(jnp.dot(mixed, w_out, preferred_element_type=jnp.float32))
    w_gate, w_up, w_down = ffn_first()
    inv_two = lax.rsqrt(jnp.mean(resid * resid, axis=-1, keepdims=True) + EPSILON)
    normed_two = gather_pair((resid * inv_two * gain_two).astype(jnp.bfloat16))
    gate_act = jnp.dot(normed_two, w_gate, preferred_element_type=jnp.float32)
    up_act = jnp.dot(normed_two, w_up, preferred_element_type=jnp.float32)
    hidden = (jax.nn.silu(gate_act) * up_act).astype(jnp.bfloat16)
    output = resid + sum_pair(jnp.dot(hidden, w_down, preferred_element_type=jnp.float32))
    grad_rows = grad_out.astype(jnp.float32).reshape(rows, width)
    w_gate, w_up, w_down = ffn_second()
    grad_branch = gather_pair(grad_rows.astype(jnp.bfloat16))
    grad_wdown = outer_sum(hidden, grad_branch)
    grad_hidden = times_transpose(grad_branch, w_down)
    sigmoid_gate = jax.nn.sigmoid(gate_act)
    grad_gateact = (
        grad_hidden * up_act * sigmoid_gate * (1.0 + gate_act * (1.0 - sigmoid_gate))
    ).astype(jnp.bfloat16)
    grad_upact = (grad_hidden * gate_act * sigmoid_gate).astype(jnp.bfloat16)
    grad_normed_two = sum_pair(
        times_transpose(grad_gateact, w_gate) + times_transpose(grad_upact, w_up)
    )
    gain_two_grad = jnp.sum(grad_normed_two * resid * inv_two, axis=0)
    grad_resid = grad_rows + norm_back(grad_normed_two, resid, inv_two, gain_two)
    w_query, w_key, w_value, w_out, gains, bias_q, bias_k, bias_v = attn_second()
    grad_attn = gather_pair(grad_resid.astype(jnp.bfloat16))
    grad_wout = outer_sum(mixed, grad_attn)
    grad_mixed = times_transpose(grad_attn, w_out).astype(jnp.bfloat16)
    grad_normed, qkv_grads, bias_grads = attention_core_back(
        grad_mixed, attn_saved, normed, w_query, w_key, w_value
    )
    grad_normed = sum_pair(grad_normed)
    gain_one_grad = jnp.sum(grad_normed * source * inv_one, axis=0)
    grad_input = grad_resid + norm_back(grad_normed, source, inv_one, gain_one)
    attn_grads = (
        qkv_grads + (grad_wout, jnp.stack([gain_one_grad, gain_two_grad], axis=1)) + bias_grads
    )
    ffn_grads = (outer_sum(normed_two, grad_gateact), outer_sum(normed_two, grad_upact), grad_wdown)
    return (
        output.astype(jnp.bfloat16).reshape(block_in.shape),
        grad_input.astype(jnp.bfloat16).reshape(block_in.shape),
        attn_grads,
        ffn_grads,
    )


def accumulate(running, update):
    if running is None:
        return update
    return jax.tree.map(jnp.add, running, update)


def same_rows(rows):
    return rows


def flat_rows(matrix, device_count):
    return matrix.reshape(8 * device_count, -1)


def owned_rows(summed, whole, device_count):
    return summed.reshape(whole.shape[0] // device_count, whole.shape[1])


def shards(
    tokens, segments, w_query, w_key, w_value, w_out, w_gate, w_up, w_down, gains, biases, cotangent
):
    micro_count = tokens.shape[0]
    q_width = w_query.shape[1]
    k_width = w_key.shape[1]

    def get_attention():
        gathered = (
            lax.all_gather(w_query, ("dp", "fsdp"), axis=0, tiled=True),
            lax.all_gather(w_key, ("dp", "fsdp"), axis=0, tiled=True),
            lax.all_gather(w_value, ("dp", "fsdp"), axis=0, tiled=True),
            lax.all_gather(w_out, ("dp", "fsdp"), axis=0, tiled=True),
            lax.all_gather(gains, ("dp", "fsdp"), axis=0, tiled=True),
            lax.all_gather(biases, ("dp", "fsdp"), axis=0, tiled=True),
        )
        bias_all = gathered[5]
        return (
            gathered[0],
            gathered[1],
            gathered[2],
            gathered[3],
            gathered[4],
            bias_all[:q_width],
            bias_all[q_width : q_width + k_width],
            bias_all[q_width + k_width :],
        )

    def get_ffn():
        return (
            lax.all_gather(w_gate, ("dp", "fsdp"), axis=0, tiled=True),
            lax.all_gather(w_up, ("dp", "fsdp"), axis=0, tiled=True),
            lax.all_gather(w_down, ("dp", "fsdp"), axis=0, tiled=True),
        )

    outputs_list = []
    grads_list = []
    attn_total = None
    ffn_total = None
    for micro_index in range(micro_count):
        result = run_batch(
            tokens[micro_index],
            segments[micro_index],
            cotangent[micro_index],
            get_attention,
            get_ffn,
            get_ffn,
            get_attention,
            same_rows,
            same_rows,
        )
        outputs_list.append(result[0])
        grads_list.append(result[1])
        attn_total = accumulate(attn_total, result[2])
        ffn_total = accumulate(ffn_total, result[3])
    grad_q, grad_k, grad_v, grad_wout, grad_gain, grad_bq, grad_bk, grad_bv = attn_total
    grad_g, grad_u, grad_d = ffn_total
    bias_grad = jnp.concatenate([grad_bq, grad_bk, grad_bv])
    device_count = lax.axis_size(("dp", "fsdp"))
    summed = (
        lax.psum_scatter(
            flat_rows(grad_q, device_count), ("dp", "fsdp"), scatter_dimension=0, tiled=True
        ),
        lax.psum_scatter(
            flat_rows(grad_k, device_count), ("dp", "fsdp"), scatter_dimension=0, tiled=True
        ),
        lax.psum_scatter(
            flat_rows(grad_v, device_count), ("dp", "fsdp"), scatter_dimension=0, tiled=True
        ),
        lax.psum_scatter(
            flat_rows(grad_wout, device_count), ("dp", "fsdp"), scatter_dimension=0, tiled=True
        ),
        lax.psum_scatter(
            flat_rows(grad_g, device_count), ("dp", "fsdp"), scatter_dimension=0, tiled=True
        ),
        lax.psum_scatter(
            flat_rows(grad_u, device_count), ("dp", "fsdp"), scatter_dimension=0, tiled=True
        ),
        lax.psum_scatter(
            flat_rows(grad_d, device_count), ("dp", "fsdp"), scatter_dimension=0, tiled=True
        ),
        lax.psum_scatter(grad_gain, ("dp", "fsdp"), scatter_dimension=0, tiled=True),
        lax.psum_scatter(bias_grad, ("dp", "fsdp"), scatter_dimension=0, tiled=True),
    )
    owned = (
        owned_rows(summed[0], grad_q, device_count),
        owned_rows(summed[1], grad_k, device_count),
        owned_rows(summed[2], grad_v, device_count),
        owned_rows(summed[3], grad_wout, device_count),
        owned_rows(summed[4], grad_g, device_count),
        owned_rows(summed[5], grad_u, device_count),
        owned_rows(summed[6], grad_d, device_count),
        summed[7],
        summed[8],
    )
    block_out = jnp.stack(outputs_list, axis=0)
    grad_tokens = jnp.stack(grads_list, axis=0)
    return (
        block_out,
        grad_tokens,
        owned[0],
        owned[1],
        owned[2],
        owned[3],
        owned[4],
        owned[5],
        owned[6],
        owned[7],
        owned[8],
    )


def solution(mesh):
    placed = (
        P(None, ("dp", "fsdp"), None, None),
        P(None, ("dp", "fsdp"), None),
        P(("dp", "fsdp"), None),
        P(("dp", "fsdp"), None),
        P(("dp", "fsdp"), None),
        P(("dp", "fsdp"), None),
        P(("dp", "fsdp"), None),
        P(("dp", "fsdp"), None),
        P(("dp", "fsdp"), None),
        P(("dp", "fsdp"), None),
        P(("dp", "fsdp")),
        P(None, ("dp", "fsdp"), None, None),
    )
    return jax.shard_map(
        shards,
        mesh=mesh,
        in_specs=placed,
        out_specs=(
            P(None, ("dp", "fsdp"), None, None),
            P(None, ("dp", "fsdp"), None, None),
            P(("dp", "fsdp"), None),
            P(("dp", "fsdp"), None),
            P(("dp", "fsdp"), None),
            P(("dp", "fsdp"), None),
            P(("dp", "fsdp"), None),
            P(("dp", "fsdp"), None),
            P(("dp", "fsdp"), None),
            P(("dp", "fsdp"), None),
            P(("dp", "fsdp")),
        ),
        check_vma=False,
    )
```

profile of v0, /device:TPU:1, one launch (start us, length us, event | category | flops | bytes accessed | tf_op | source)
XLA Modules:
  0.0 3816.3 jit_solution(17721975916544248482)
XLA Ops:
  12.3 277.5 %all-gather = bf16[128,7,2]{1,2,0:T(2,128)(2,1)S(1)} all-gather(bf16[1,7,2]{1,2,0:T(2,128)(2,1)} %bitcast.489), channel_id=1, replica_groups=mesh['dp'=4,'fsdp'=32] {'dp','fsdp'}, dimensions={0}, use_global_device_ids=true | all-gather | bytes 3612 | tf_op jit(solution)/shard_map/all_gather | solution.py:286
  290.0 298.8 %all-gather.2 = bf16[128,7,128]{2,1,0:T(8,128)(2,1)S(1)} all-gather(bf16[1,7,128]{2,1,0:T(8,128)(2,1)} %bitcast.487), channel_id=1, replica_groups=mesh['dp'=4,'fsdp'=32] {'dp','fsdp'}, dimensions={0}, use_global_device_ids=true | all-gather | bytes 231168 | tf_op jit(solution)/shard_map/all_gather | solution.py:283
  588.9 304.1 %all-gather.1 = bf16[128,7,128]{2,1,0:T(8,128)(2,1)S(1)} all-gather(bf16[1,7,128]{2,1,0:T(8,128)(2,1)} %bitcast.488), channel_id=1, replica_groups=mesh['dp'=4,'fsdp'=32] {'dp','fsdp'}, dimensions={0}, use_global_device_ids=true | all-gather | bytes 231168 | tf_op jit(solution)/shard_map/all_gather | solution.py:284
  893.3 124.7 %all-reduce = bf16[1152]{0:T(1024)(128)(2,1)S(1)} all-reduce(bf16[1152]{0:T(1024)(128)(2,1)S(1)} %dynamic-update-slice), channel_id=1, replica_groups=mesh['dp'=4,'fsdp'=32] {'dp','fsdp'}, use_global_device_ids=true, to_apply=%add | all-reduce | flops 1152 | bytes 4608
  1023.7 2.6 reshape.1124
  1029.2 2.6 reshape.1126
  1034.7 1.2 multiply_reduce_fusion.6
  1038.7 13.6 reshape.1128
  1052.4 200.6 %all-gather.20.cloned.1.call-done = bf16[128,7,4864]{2,1,0:T(8,128)(2,1)} async-done(((bf16[1,7,4864]{2,1,0:T(8,128)(2,1)}), bf16[128,7,4864]{2,1,0:T(8,128)(2,1)}) %all-gather.20.cloned.1.call-update) | async-done | bytes 8716304 | tf_op jit(solution)/shard_map/all_gather | solution.py:304
  1253.0 13.5 reshape.1130
  1266.5 6.5 fusion.144
  1273.0 2.9 fusion.143
  1276.0 294.8 %all-gather.22.cloned.1.call-done = bf16[128,38,896]{2,1,0:T(8,128)(2,1)} async-done(((bf16[1,38,896]{2,1,0:T(8,128)(2,1)}), bf16[128,38,896]{2,1,0:T(8,128)(2,1)}) %all-gather.22.cloned.1.call-update) | async-done | bytes 8716304 | tf_op jit(solution)/shard_map/all_gather | solution.py:305
  1570.8 13.4 reshape.1132
  1584.2 9.0 multiply_convert_fusion.2
  1593.3 6.7 fusion.147
  1600.2 4.2 multiply_reduce_fusion.3
  1604.4 2.9 fusion.146
  1607.3 2.9 fusion.145
  1610.8 9.3 multiply_convert_fusion
  1620.1 4.2 fusion.149
  1624.4 3.6 multiply_reduce_fusion.2
  1629.1 1.3 convolution_convert_fusion
  1630.4 1.8 copy.73
  1632.2 2.4 convert_reduce_fusion.2
  1634.5 1.3 multiply_reduce_fusion
  1638.1 1.3 convolution_convert_fusion.1
  1639.4 1.1 copy.69
  1641.6 1.2 multiply_reduce_fusion.1
  1644.4 2.2 fusion.95
  1647.3 1.1 reshape.1101
  1648.5 1.3 convert_reduce_fusion.5
  1650.1 1.2 convert_reduce_fusion.4
  1651.3 1.1 convolution_add_fusion.6
  1652.5 2.1 reshape.1099
  1654.7 4.3 convolution_add_fusion.3
  1659.0 5.9 reshape.1103
  1667.4 2.3 convolution_add_fusion.4
  1669.7 5.9 reshape.1097
  1676.6 3.8 fusion.152
  1680.3 10.2 convolution_add_fusion.1
  1690.5 23.5 reshape.1107
  1714.1 3.8 fusion.151
  1717.9 9.8 convolution_add_fusion.2
  1727.7 23.3 reshape.1105
  1752.0 3.8 fusion.85
  1755.8 9.8 convolution_add_fusion
  1765.6 22.9 reshape.1109
  1790.4 1.3 stack.27
  1794.5 1.5 fusion.105
  1797.3 1.2 convert_reduce_fusion
  1798.5 1.5 convert_reduce_fusion.1
  1800.0 1.1 fusion.67
  1801.2 1.1 fusion.64
  1804.4 1.2 fusion.37
  1805.7 68.4 %all-reduce.7 = (f32[896,2]{0,1:T(2,128)S(1)}, f32[1152]{0:T(1024)S(1)}) all-reduce(f32[896,2]{0,1:T(2,128)S(1)} %maximum_add_fusion.2, f32[1152]{0:T(1024)S(1)} %pad_maximum_fusion.6), channel_id=9, replica_groups=mesh['dp'=4,'fsdp'=32] {'dp','fsdp'}, use_global_device_ids=true, to_apply=%region_27.28.clone | all-reduce | flops 2944 | bytes 23552
  1875.4 5.5 fusion.7
  1882.1 1.5 fusion.6
  1891.2 571.8 %reduce-scatter.7.cloned.1.call-done = f32[8,4256]{1,0:T(8,128)} async-done(((f32[1024,4256]{1,0:T(8,128)}), f32[8,4256]{1,0:T(8,128)}) %reduce-scatter.7.cloned.1.call-update) | async-done | bytes 136208 | tf_op jit(solution)/shard_map/reduce_scatter | solution.py:348
  2463.0 1.7 reshape.1108
  2464.7 672.2 %reduce-scatter.5.cloned.1.call-done = f32[8,4256]{1,0:T(8,128)} async-done(((f32[1024,4256]{1,0:T(8,128)}), f32[8,4256]{1,0:T(8,128)}) %reduce-scatter.5.cloned.1.call-update) | async-done | bytes 136208 | tf_op jit(solution)/shard_map/reduce_scatter | solution.py:345
  3136.9 1.7 reshape.1106
  3138.6 668.9 %reduce-scatter.9.cloned.1.call-done = f32[8,4256]{1,0:T(8,128)} async-done(((f32[1024,4256]{1,0:T(8,128)}), f32[8,4256]{1,0:T(8,128)}) %reduce-scatter.9.cloned.1.call-update) | async-done | bytes 136208 | tf_op jit(solution)/shard_map/reduce_scatter | solution.py:351
  3807.5 1.7 reshape.1110
  (361 shorter events, 49.6 us)
Async XLA Ops:
  7.2 885.9 %copy-start.101 = (bf16[9]{0:T(256)(128)(2,1)S(1)}, bf16[9]{0:T(256)(128)(2,1)}, u32[]{:S(2)}) copy-start(bf16[9]{0:T(256)(128)(2,1)} %param.22) | copy-start | bytes 58
  7.2 1011.2 %copy-start.3 = (bf16[2,1,128,896]{3,2,1,0:T(8,128)(2,1)S(1)}, bf16[2,1,128,896]{3,2,1,0:T(8,128)(2,1)}, u32[]{:S(2)}) copy-start(bf16[2,1,128,896]{3,2,1,0:T(8,128)(2,1)} %param.12) | copy-start | bytes 1376260
  7.2 1016.5 %all-gather.14.cloned.1.call-start = ((), (), s32[]{:S(2)}) async-start(), calls=%async_computation.6 | async-start | bytes 1849344 | tf_op jit(solution)/shard_map/all_gather | solution.py:282
  7.9 1021.3 %all-gather.16.cloned.1.call-start = ((), (), s32[]{:S(2)}) async-start(), calls=%async_computation.7 | async-start | bytes 1849344 | tf_op jit(solution)/shard_map/all_gather | solution.py:285
  8.7 1030.0 %all-gather.18.cloned.1.call-start = ((), (), s32[]{:S(2)}) async-start(), calls=%async_computation.8 | async-start | bytes 10039296 | tf_op jit(solution)/shard_map/all_gather | solution.py:303
  9.4 1243.5 %all-gather.20.cloned.1.call-start = ((), (), s32[]{:S(2)}) async-start(), calls=%async_computation.9 | async-start | bytes 10039296 | tf_op jit(solution)/shard_map/all_gather | solution.py:304
  10.0 1560.8 %all-gather.22.cloned.1.call-start = ((), (), s32[]{:S(2)}) async-start(), calls=%async_computation.10 | async-start | bytes 9246720 | tf_op jit(solution)/shard_map/all_gather | solution.py:305
  10.6 1875.0 %all-reduce.11.cloned.1.call-start = ((), (), s32[]{:S(2)}) async-start(), calls=%async_computation.11 | async-start | bytes 16777216
  588.9 434.8 %copy-start.35 = (bf16[896,128]{1,0:T(8,128)(2,1)}, bf16[896,128]{1,0:T(8,128)(2,1)S(1)}, u32[]{:S(2)}) copy-start(bf16[896,128]{1,0:T(8,128)(2,1)S(1)} %reshape.1122) | copy-start | bytes 688132
  893.0 130.6 %copy-start.56 = (bf16[896,128]{1,0:T(8,128)(2,1)}, bf16[896,128]{1,0:T(8,128)(2,1)S(1)}, u32[]{:S(2)}) copy-start(bf16[896,128]{1,0:T(8,128)(2,1)S(1)} %reshape.1120) | copy-start | bytes 688132
  1018.3 646.6 %copy-start.52 = (f32[128,64]{0,1:T(8,128)}, f32[128,64]{0,1:T(8,128)S(1)}, u32[]{:S(2)}) copy-start(f32[128,64]{0,1:T(8,128)S(1)} %maximum_bitcast_fusion) | copy-start | bytes 98308
  1018.3 648.2 %copy-start.50 = (f32[128,64]{0,1:T(8,128)}, f32[128,64]{0,1:T(8,128)S(1)}, u32[]{:S(2)}) copy-start(f32[128,64]{0,1:T(8,128)S(1)} %maximum_bitcast_fusion.2) | copy-start | bytes 98308
  1019.2 8.6 copy-start.86
  1037.9 14.4 copy-start.91
  1038.7 234.3 %copy-start.18 = (bf16[128,896]{1,0:T(8,128)(2,1)}, bf16[128,896]{1,0:T(8,128)(2,1)S(1)}, u32[]{:S(2)}) copy-start(bf16[128,896]{1,0:T(8,128)(2,1)S(1)} %multiply_convert_fusion.9) | copy-start | bytes 688132
  1266.5 6.6 copy-start
  1570.8 29.3 slice-start.3
  1584.2 15.9 slice-start.4
  1584.2 15.9 slice-start.5
  1593.3 6.8 copy-start.30
  1593.3 6.8 copy-start.12
  1593.3 6.8 copy-start.15
  1593.3 6.8 copy-start.31
  1593.3 6.8 copy-start.92
  1600.1 7.1 slice-start
  1600.2 7.1 slice-start.1
  1620.1 4.2 copy-start.16
  1620.1 4.2 copy-start.32
  1624.3 3.7 copy-start.13
  1624.4 3.7 copy-start.47
  1628.1 4.1 copy-start.10
  1628.1 4.1 copy-start.71
  1628.1 4.1 copy-start.80
  1629.1 6.8 copy-start.24
  1629.1 5.4 copy-start.83
  1636.2 4.4 copy-start.8
  1636.2 4.4 copy-start.68
  1638.1 28.4 copy-start.20
  1641.6 5.0 copy-start.84
  1643.3 5.2 copy-start.61
  1644.4 20.6 copy-start.22
  1644.4 4.0 copy-start.72
  1648.5 18.1 copy-start.37
  1648.5 18.1 copy-start.39
  1649.8 4.9 copy-start.25
  1649.8 4.9 copy-start.55
  1654.7 10.2 copy-start.43
  1654.7 10.2 copy-start.44
  1675.6 787.4 %reduce-scatter.7.cloned.1.call-start = ((), (), s32[]{:S(2)}) async-start(), calls=%async_computation.4 | async-start | bytes 17965056 | tf_op jit(solution)/shard_map/reduce_scatter | solution.py:348
  1714.1 1422.9 %reduce-scatter.5.cloned.1.call-start = ((), (), s32[]{:S(2)}) async-start(), calls=%async_computation.3 | async-start | bytes 17965056 | tf_op jit(solution)/shard_map/reduce_scatter | solution.py:345
  1751.1 2056.5 %reduce-scatter.9.cloned.1.call-start = ((), (), s32[]{:S(2)}) async-start(), calls=%async_computation.5 | async-start | bytes 17965056 | tf_op jit(solution)/shard_map/reduce_scatter | solution.py:351
  1788.5 5.1 copy-start.51
  1788.5 6.0 copy-start.53
  1788.5 8.7 copy-start.38
  1788.5 8.7 copy-start.40
  1788.6 11.5 copy-start.23
  1788.6 12.6 copy-start.21
  1788.6 13.7 copy-start.2
  1803.5 71.8 %copy-start.14 = (f32[128,896]{1,0:T(8,128)S(1)}, f32[128,896]{1,0:T(8,128)}, u32[]{:S(2)}) copy-start(f32[128,896]{1,0:T(8,128)} %copy-done.11) | copy-start | bytes 1376260
  1803.5 77.4 %slice-start.6 = ((s8[8716288]{0:T(1024)(128)(4,1)}), s8[327680]{0:T(1024)(128)(4,1)S(1)}, s32[]{:S(2)}) async-start(s8[8716288]{0:T(1024)(128)(4,1)} %bitcast.444), calls=%async_computation.18 | async-start | bytes 655360
  1875.4 5.5 slice-start.7
  1875.4 6.4 slice-start.8
  1875.4 6.7 copy-start.6
  1875.4 6.7 copy-start.17
  (56 other events, 121.9 us)
Sparse Core Ops, SparseCore 0:
  9.7 302.4 all-gather.13
  314.0 298.3 all-gather.15
  614.1 319.1 all-gather.17
  934.8 318.1 all-gather.19
  1254.5 316.2 all-gather.21
  1675.8 162.4 all-reduce.10
  1840.8 622.1 reduce-scatter.6
  2465.4 671.4 reduce-scatter.4
  3139.4 668.0 reduce-scatter.8
where the time goes:
time: 3870 us; the launch traced here: 3820 us
  waiting for transfers between devices  2410 us (62%)
  blocking collectives  1070 us (28%)
  local copies, waits for them, and re-layouts  157 us (4%)
  matrix products  133 us (3%)
    reduce_scatter x1, waiting for transfers between devices, shards(): lax.psum_scatter(flat_rows(grad_g, device_count), ('dp', 'fsdp'), scatter...  672 us
    reduce_scatter x1, waiting for transfers between devices, shards(): lax.psum_scatter(flat_rows(grad_d, device_count), ('dp', 'fsdp'), scatter...  669 us
    reduce_scatter x1, waiting for transfers between devices, shards(): lax.psum_scatter(flat_rows(grad_u, device_count), ('dp', 'fsdp'), scatter...  572 us
    all_gather x1, blocking collectives, get_attention(): lax.all_gather(w_value, ('dp', 'fsdp'), axis=0, tiled=True)  304 us
    all_gather x1, blocking collectives, get_attention(): lax.all_gather(w_key, ('dp', 'fsdp'), axis=0, tiled=True)  299 us
    all_gather x1, waiting for transfers between devices, get_ffn(): lax.all_gather(w_down, ('dp', 'fsdp'), axis=0, tiled=True)  295 us
    all_gather x1, blocking collectives, get_attention(): lax.all_gather(gains, ('dp', 'fsdp'), axis=0, tiled=True)  277 us
    all_gather x1, waiting for transfers between devices, get_ffn(): lax.all_gather(w_up, ('dp', 'fsdp'), axis=0, tiled=True)  201 us
  transfers between devices with their start and end apart: 9, of which 5 were waited for; matrix products, arithmetic and copies ran while one was open for 5% of the time, Pallas kernels for 0%

commit v1 on v0

v1 whole, which is shorter than its diff:
```python
import functools
import math

import jax
import jax.numpy as jnp
import numpy as np
from jax import lax
from jax.experimental import pallas as pl
from jax.experimental.pallas import tpu as pltpu
from jax.sharding import PartitionSpec as P

HD = 64
EPSILON = 1e-06
THETA = 1000000.0
NEG_FILL = -1e30
MESH = pl.DeviceIdType.MESH
AXES = ("dp", "fsdp")
BF = jnp.bfloat16
F32 = jnp.float32

WCOLS = 7040
DROWS = 48
W_PARTS = ((0, 7), (7, 10), (17, 10), (27, 10), (37, 9), (46, 9))
D_PARTS = ((0, 2), (2, 1), (3, 1), (4, 1), (5, 1), (6, 1))
ORDER = tuple(
    tuple(2 * ((p % 3 + k // 2) % 3) + ((k % 2) ^ (p // 3)) for k in range(6)) for p in range(6)
)


def here():
    dp = lax.axis_index("dp")
    fs = lax.axis_index("fsdp")
    return (fs // 4) % 4, fs % 4, (dp // 2) * 2 + fs // 16, dp % 2


def device(x, y, z, core):
    return ((z // 2) * 2 + core, (z % 2) * 16 + x * 4 + y)


def gray_bits(v):
    high = v // 2
    low = (v % 2 + high) % 2
    return low, high


def flip(v, bit):
    if bit == 0:
        return v + 1 - 2 * (v % 2)
    return 3 - v


def partner(bit):
    x, y, z, core = here()
    axis, low = bit // 2, bit % 2
    place = [x, y, z]
    place[axis] = flip(place[axis], low)
    return device(*place, core)


def sibling():
    x, y, z, core = here()
    return device(x, y, z, 1 - core)


def my_bits():
    x, y, z, _ = here()
    bits = []
    for v in (x, y, z):
        low, high = gray_bits(v)
        bits += [low, high]
    return bits


def slot(bits, full):
    return tuple(slice(None) if b in full else bits[b] for b in (1, 0, 3, 2, 5, 4))


def greet():
    barrier = pltpu.get_barrier_semaphore()
    for b in range(6):
        pl.semaphore_signal(barrier, inc=1, device_id=partner(b), device_id_type=MESH)
    pl.semaphore_signal(barrier, inc=1, device_id=sibling(), device_id_type=MESH)
    pl.semaphore_wait(barrier, 7)


def pieces(wref, dref, index, p):
    wo, wn = W_PARTS[p]
    do, dn = D_PARTS[p]
    return (
        wref.at[index + (slice(None), pl.ds(wo * 128, wn * 128))],
        dref.at[index + (slice(None), pl.ds(do * 128, dn * 128))],
    )


def gather_kernel(pair, down, wide, tall, stage, slab, ss, rs, ws, wr, ds_, dr, ls):
    greet()
    bits = my_bits()
    swap = pltpu.make_async_remote_copy(
        src_ref=pair.at[1], dst_ref=stage, send_sem=ss, recv_sem=rs,
        device_id=sibling(), device_id_type=MESH)
    swap.start()
    mine = slot(bits, ())
    own_down = pltpu.make_async_copy(down, tall.at[mine], ls.at[0])
    own_down.start()
    swap.wait()
    slab[...] = pair[0] + stage[...]
    own_wide = pltpu.make_async_copy(slab, wide.at[mine], ls.at[1])
    own_wide.start()
    own_down.wait()
    own_wide.wait()
    sends = []
    copies = [None] * 6
    for k in range(6):
        for p in range(6):
            order = ORDER[p]
            if k > 0:
                for c in copies[p]:
                    c.wait_recv()
            index = slot(bits, order[:k])
            w, d = pieces(wide, tall, index, p)
            made = []
            for ref, a, b in ((w, ws, wr), (d, ds_, dr)):
                c = pltpu.make_async_remote_copy(
                    src_ref=ref, dst_ref=ref, send_sem=a.at[p, k], recv_sem=b.at[p, k],
                    device_id=partner(order[k]), device_id_type=MESH)
                c.start()
                made.append(c)
            copies[p] = made
            sends += made
    for p in range(6):
        for c in copies[p]:
            c.wait_recv()
    for c in sends:
        c.wait_send()


def gather_all(pair, down):
    dma = pltpu.SemaphoreType.DMA
    return pl.pallas_call(
        gather_kernel,
        out_shape=(
            jax.ShapeDtypeStruct((2,) * 6 + (16, WCOLS), BF),
            jax.ShapeDtypeStruct((2,) * 6 + (DROWS, 896), BF),
        ),
        in_specs=[pl.BlockSpec(memory_space=pltpu.VMEM)] * 2,
        out_specs=[pl.BlockSpec(memory_space=pl.ANY)] * 2,
        scratch_shapes=[
            pltpu.VMEM((16, WCOLS), BF), pltpu.VMEM((16, WCOLS), BF),
            dma, dma, dma((6, 6)), dma((6, 6)), dma((6, 6)), dma((6, 6)), dma((2,)),
        ],
        compiler_params=pltpu.CompilerParams(collective_id=0, has_side_effects=True,
                                             vmem_limit_bytes=32 * 2**20),
    )(pair, down)


def scatter_kernel(gw, gd, own_w, sib_w, out_d, accw, accd, rw, rd, slab,
                   ss, rs, ws, wr, ds_, dr, ls):
    greet()
    bits = my_bits()
    flipped = [1 - b for b in bits]

    def with_bit(k, order, value):
        b = list(bits)
        b[order[k]] = value
        return slot(b, order[:k])

    sends = []
    copies = {}

    def send(k, p):
        order = ORDER[p]
        src = (gw, gd) if k == 5 else (accw, accd)
        srcs = pieces(*src, with_bit(k, order, flipped[order[k]]), p)
        dsts = pieces(rw, rd, with_bit(k, order, bits[order[k]]), p)
        made = []
        for s, d, a, b in zip(srcs, dsts, (ws, ds_), (wr, dr)):
            c = pltpu.make_async_remote_copy(
                src_ref=s, dst_ref=d, send_sem=a.at[p, k], recv_sem=b.at[p, k],
                device_id=partner(order[k]), device_id_type=MESH)
            c.start()
            made.append(c)
        copies[p] = made
        sends.extend(made)

    for p in range(6):
        send(5, p)
    loads = []
    for p in range(6):
        order = ORDER[p]
        index = with_bit(5, order, bits[order[5]])
        for i, (s, d) in enumerate(zip(pieces(gw, gd, index, p), pieces(accw, accd, index, p))):
            c = pltpu.make_async_copy(s, d, ls.at[i, p])
            c.start()
            loads.append(c)
    for c in loads:
        c.wait()

    def add(k, p):
        order = ORDER[p]
        (wo, wn), (do, dn) = W_PARTS[p], D_PARTS[p]

        def body(n, carry):
            b = list(bits)
            for i in range(k):
                b[order[i]] = (n // 2**i) % 2
            here_at = slot(b, ())
            b[order[k]] = flipped[order[k]]
            there_at = slot(b, ())
            for acc, got, o, m in ((accw, rw, wo, wn), (accd, rd, do, dn)):
                cols = (slice(None), pl.ds(o * 128, m * 128))
                acc[here_at + cols] = (acc[here_at + cols].astype(F32)
                                       + got[there_at + cols].astype(F32)).astype(BF)
            return carry

        lax.fori_loop(0, 2**k, body, 0)

    for k in range(5, -1, -1):
        for p in range(6):
            for c in copies[p]:
                c.wait_recv()
            if k > 0:
                add(k, p)
                send(k - 1, p)
    mine = slot(bits, ())
    for p in range(6):
        order = ORDER[p]
        (wo, wn), (do, dn) = W_PARTS[p], D_PARTS[p]
        other = with_bit(0, order, flipped[order[0]])
        cols = (slice(None), pl.ds(wo * 128, wn * 128))
        total = accw[mine + cols].astype(F32) + rw[other + cols].astype(F32)
        own_w[cols] = total
        slab[cols] = total.astype(BF)
        cols = (slice(None), pl.ds(do * 128, dn * 128))
        out_d[cols] = accd[mine + cols].astype(F32) + rd[other + cols].astype(F32)
    swap = pltpu.make_async_remote_copy(
        src_ref=slab, dst_ref=sib_w, send_sem=ss, recv_sem=rs,
        device_id=sibling(), device_id_type=MESH)
    swap.start()
    for c in sends:
        c.wait_send()
    swap.wait()


def scatter_all(gw, gd):
    dma = pltpu.SemaphoreType.DMA
    return pl.pallas_call(
        scatter_kernel,
        out_shape=(
            jax.ShapeDtypeStruct((16, WCOLS), F32),
            jax.ShapeDtypeStruct((16, WCOLS), BF),
            jax.ShapeDtypeStruct((DROWS, 896), F32),
        ),
        in_specs=[pl.BlockSpec(memory_space=pl.ANY)] * 2,
        out_specs=[pl.BlockSpec(memory_space=pltpu.VMEM)] * 3,
        scratch_shapes=[
            pltpu.VMEM((2,) * 6 + (16, WCOLS), BF), pltpu.VMEM((2,) * 6 + (DROWS, 896), BF),
            pltpu.VMEM((2,) * 6 + (16, WCOLS), BF), pltpu.VMEM((2,) * 6 + (DROWS, 896), BF),
            pltpu.VMEM((16, WCOLS), BF),
            dma, dma, dma((6, 6)), dma((6, 6)), dma((6, 6)), dma((6, 6)), dma((2, 6)),
        ],
        compiler_params=pltpu.CompilerParams(collective_id=1, has_side_effects=True,
                                             vmem_limit_bytes=56 * 2**20),
    )(gw, gd)


def positions(segment_ids):
    counter = lax.broadcasted_iota(jnp.int32, segment_ids.shape, 1)
    starts = jnp.concatenate(
        [jnp.ones((segment_ids.shape[0], 1), jnp.bool_), segment_ids[:, 1:] != segment_ids[:, :-1]],
        axis=1)
    return counter - lax.cummax(jnp.where(starts, counter, 0), axis=1)


def rope_tables(position):
    exponent = jnp.arange(HD // 2, dtype=F32) * (2.0 / HD)
    angles = position.astype(F32)[..., None] * jnp.power(THETA, -exponent)
    cosine, sine = jnp.cos(angles), jnp.sin(angles)
    return jnp.concatenate([cosine] * 2, -1), jnp.concatenate([sine] * 2, -1)


def rotate(v, cosine, sine):
    turned = jnp.concatenate([-v[..., HD // 2:], v[..., :HD // 2]], axis=-1)
    return v * cosine + turned * sine


def rotate_back(v, cosine, sine):
    scaled = v * sine
    turned = jnp.concatenate([scaled[..., HD // 2:], -scaled[..., :HD // 2]], axis=-1)
    return v * cosine + turned


def dot(a, b, **kw):
    return jnp.dot(a, b, preferred_element_type=F32, **kw)


def dot_t(a, b):
    return jnp.einsum("nf,df->nd", a, b, preferred_element_type=F32)


def outer(a, b):
    return jnp.einsum("nd,nf->df", a, b, preferred_element_type=F32)


def norm_back(grad, source, inv, gain):
    scaled = grad * gain
    return inv * scaled - source * inv**3 * jnp.mean(scaled * source, axis=-1, keepdims=True)


def slot_numbers():
    gray = (0, 1, 3, 2)
    slots = np.zeros(128, np.int32)
    for n in range(128):
        dp, fs = n // 32, n % 32
        x, y, z, core = fs // 4 % 4, fs % 4, (dp // 2) * 2 + fs // 16, dp % 2
        slots[n] = ((gray[x] * 4 + gray[y]) * 4 + gray[z]) * 2 + core
    return slots


def shards(tokens, segments, w_query, w_key, w_value, w_out, w_gate, w_up, w_down, gains, biases,
           cotangent):
    core = lax.axis_index("dp") % 2
    swap = ((0, 1), (1, 0), (2, 3), (3, 2))
    slots = slot_numbers()
    spread_np = np.zeros((896, 1024), np.float32)
    for d in range(896):
        spread_np[d, slots[d // 7] * 8 + d % 7] = 1.0
    spread = jnp.asarray(spread_np, BF)

    def half(w, c):
        return lax.dynamic_index_in_dim(w.reshape(7, 2, 2, 1216), c, 2, keepdims=False).reshape(7, 2432)

    small = jnp.zeros((8, 128), BF).at[:7, :2].set(gains).at[0, 16:25].set(biases)[:7]
    rest = [w_query, w_key, w_value, w_out, small]

    def build(c):
        rows = jnp.concatenate([half(w_gate, c), half(w_up, c)] + rest, axis=1)
        return lax.dynamic_update_slice(jnp.zeros((16, WCOLS), BF), rows, (8 * core, 0))

    pair = jnp.stack([build(core), build(1 - core)])
    wide, tall = gather_all(pair, jnp.pad(w_down, ((0, DROWS - 38), (0, 0))))
    wide = wide.reshape(1024, WCOLS)
    wg, wu = wide[:, :2432], wide[:, 2432:4864]
    wqkv, wo = wide[:, 4864:6016], wide[:, 6016:6912]
    small = wide[:, 6912:]
    order = np.zeros(64, np.int32)
    gray = (0, 1, 3, 2)
    for s in range(64):
        z, x, y = s // 16, s // 4 % 4, s % 4
        order[s] = (gray[x] * 4 + gray[y]) * 4 + gray[z]
    back = np.argsort(order)
    wd = tall.reshape(64, DROWS, 896)[order, :38].reshape(2432, 896)
    gain = dot(spread, small[:, :2])
    bias = small.reshape(128, 8, 128)[slots, 0, 16:25].reshape(1152).astype(F32)

    seqs, length, width = 2, 128, 896
    rows = 256
    seg = segments.reshape(seqs, length)
    source = tokens.astype(F32).reshape(rows, width)
    inv_one = lax.rsqrt(jnp.mean(source * source, axis=-1, keepdims=True) + EPSILON)
    normed = (source * inv_one * gain[:, 0]).astype(BF)
    normed_s = dot(normed, spread).astype(BF)
    qkv = dot(normed_s, wqkv) + bias
    cosine, sine = rope_tables(positions(seg))
    cosine, sine = cosine.reshape(rows, 1, HD), sine.reshape(rows, 1, HD)
    queries = rotate(qkv[:, :896].reshape(rows, 14, HD), cosine, sine).astype(BF).reshape(
        seqs, length, 2, 7, HD)
    keys = rotate(qkv[:, 896:1024].reshape(rows, 2, HD), cosine, sine).astype(BF).reshape(
        seqs, length, 2, HD)
    values = qkv[:, 1024:].astype(BF).reshape(seqs, length, 2, HD)
    r = lax.broadcasted_iota(jnp.int32, (length, length), 0)
    c = lax.broadcasted_iota(jnp.int32, (length, length), 1)
    allowed = ((c <= r)[None] & (seg[:, :, None] == seg[:, None, :]))[:, None, None]
    scale = 1.0 / math.sqrt(HD)
    scores = jnp.einsum("bqcrd,bkcd->bcrqk", queries, keys, preferred_element_type=F32) * scale
    scores = jnp.where(allowed, scores, NEG_FILL)
    peak = jnp.max(scores, axis=-1, keepdims=True)
    e = jnp.exp(scores - peak)
    soft = e / jnp.sum(e, axis=-1, keepdims=True)
    softb = soft.astype(BF)
    mixed = jnp.einsum("bcrqk,bkcd->bqcrd", softb, values, preferred_element_type=F32).astype(
        BF).reshape(rows, 896)
    mixed_s = dot(mixed, spread).astype(BF)
    resid = source + dot(mixed_s, wo)
    inv_two = lax.rsqrt(jnp.mean(resid * resid, axis=-1, keepdims=True) + EPSILON)
    normed_two = (resid * inv_two * gain[:, 1]).astype(BF)
    dy = cotangent.reshape(rows, width)

    mine = jnp.concatenate([normed_two, dy], axis=1)
    other = lax.ppermute(mine, "dp", swap)
    both = jnp.concatenate([mine, other], axis=0)
    a2, eb = both[:, :896], both[:, 896:]
    a2s = dot(a2, spread).astype(BF)
    g = dot(a2s, wg)
    u = dot(a2s, wu)
    sig = jax.nn.sigmoid(g)
    hidden = (g * sig * u).astype(BF)
    part = dot(hidden, wd)
    dm = dot_t(eb, wd)
    dg = (dm * u * sig * (1.0 + g * (1.0 - sig))).astype(BF)
    du = (dm * g * sig).astype(BF)
    grad_d = outer(hidden, eb)
    grad_g = outer(a2s, dg)
    grad_u = outer(a2s, du)
    da2_s = dot_t(dg, wg) + dot_t(du, wu)
    sums = jnp.concatenate([part, da2_s], axis=1)
    sums = sums[:rows] + lax.ppermute(sums[rows:], "dp", swap)
    output = resid + sums[:, :896]
    unspread = spread.astype(F32).T
    da2 = dot(sums[:, 896:], unspread, precision=lax.Precision.HIGHEST)

    gain_two_grad = jnp.sum(da2 * resid * inv_two, axis=0)
    dy1 = dy.astype(F32) + norm_back(da2, resid, inv_two, gain[:, 1])
    f = dy1.astype(BF)
    grad_o = outer(mixed_s, f)
    do = dot(dot_t(f, wo).astype(BF), spread.T).astype(BF).reshape(seqs, length, 2, 7, HD)
    dp = jnp.einsum("bqcrd,bkcd->bcrqk", do, values, preferred_element_type=F32)
    ds = (soft * (dp - jnp.sum(soft * dp, axis=-1, keepdims=True))).astype(BF)
    dq = jnp.einsum("bcrqk,bkcd->bqcrd", ds, keys, preferred_element_type=F32) * scale
    dk = jnp.einsum("bcrqk,bqcrd->bkcd", ds, queries, preferred_element_type=F32) * scale
    dv = jnp.einsum("bcrqk,bqcrd->bkcd", softb, do, preferred_element_type=F32)
    dq0 = rotate_back(dq.reshape(rows, 14, HD), cosine, sine).reshape(rows, 896)
    dk0 = rotate_back(dk.reshape(rows, 2, HD), cosine, sine).reshape(rows, 128)
    dqkv = jnp.concatenate([dq0, dk0, dv.reshape(rows, 128)], axis=1).astype(BF)
    grad_qkv = outer(normed_s, dqkv)
    grad_bias = jnp.sum(dqkv.astype(F32), axis=0)
    da1 = dot(dot_t(dqkv, wqkv), unspread, precision=lax.Precision.HIGHEST)
    gain_one_grad = jnp.sum(da1 * source * inv_one, axis=0)
    grad_in = dy1 + norm_back(da1, source, inv_one, gain[:, 0])

    gain_grad = jnp.stack([gain_one_grad, gain_two_grad], axis=1).reshape(128, 7, 2)
    inverse = np.argsort(slots)
    small = jnp.zeros((128, 8, 128), F32)
    small = small.at[:, :7, :2].set(gain_grad[inverse])
    small = small.at[:, 0, 16:25].set(grad_bias.reshape(128, 9)[inverse]).reshape(1024, 128)
    gw = jnp.concatenate([grad_g, grad_u, grad_qkv, grad_o, small], axis=1).astype(BF)
    gd = jnp.pad(grad_d.astype(BF).reshape(64, 38, 896)[back], ((0, 0), (0, DROWS - 38), (0, 0)))
    own, sib, own_d = scatter_all(gw.reshape((2,) * 6 + (16, WCOLS)), gd.reshape((2,) * 6 + (DROWS, 896)))
    own = lax.dynamic_slice(own, (8 * core, 0), (7, WCOLS))
    sib = lax.dynamic_slice(sib, (8 * core, 0), (7, WCOLS)).astype(F32)

    def whole(a):
        first = jnp.where(core == 0, own[:, a:a + 2432], sib[:, a:a + 2432]).reshape(7, 2, 1216)
        second = jnp.where(core == 0, sib[:, a:a + 2432], own[:, a:a + 2432]).reshape(7, 2, 1216)
        return jnp.stack([first, second], axis=2).reshape(7, 4864)

    both = own[:, 4864:] + sib[:, 4864:]
    return (
        output.astype(BF).reshape(tokens.shape),
        grad_in.astype(BF).reshape(tokens.shape),
        both[:, :896], both[:, 896:1024], both[:, 1024:1152], both[:, 1152:2048],
        whole(0), whole(2432), own_d[:38],
        both[:, 2048:2050], both[0, 2064:2073],
    )


def solution(mesh):
    row = P(AXES, None)
    batch = P(None, AXES, None, None)
    return jax.shard_map(
        shards, mesh=mesh,
        in_specs=(batch, P(None, AXES, None)) + (row,) * 8 + (P(AXES), batch),
        out_specs=(batch, batch) + (row,) * 8 + (P(AXES),),
        check_vma=False,
    )
```

time: 3870 us -> 788 us (0.20); the launches traced: 3820 us -> 774 us
  waiting for transfers between devices: 2410 us -> 0.01 us
  blocking collectives: 1070 us -> 0 us
  local copies, waits for them, and re-layouts: 157 us -> 470 us
  Pallas kernels: 0 us -> 185 us
  matrix products: 133 us -> 78.2 us
    reduce_scatter x3 -> x0, waiting for transfers between devices: 1910 us -> none  [the longest x1 672 us: shards(): lax.psum_scatter(flat_rows(grad_g, device_count), ('dp', 'fsdp'), scatter...]
    all_gather x3 -> x0, blocking collectives: 880 us -> none  [the longest x1 304 us: get_attention(): lax.all_gather(w_value, ('dp', 'fsdp'), axis=0, tiled=True)]
    all_gather x5 -> x0, waiting for transfers between devices: 495 us -> none  [the longest x1 295 us: get_ffn(): lax.all_gather(w_down, ('dp', 'fsdp'), axis=0, tiled=True)]
    gather x0 -> x518, local copies, waits for them, and re-layouts: none -> 366 us
    unnamed x2 -> x0, blocking collectives: 193 us -> none
    pallas_call x0 -> x2, Pallas kernels: none -> 185 us  [the longest x1 97.1 us: scatter_all(): pl.pallas_call(scatter_kernel, out_shape=(jax.ShapeDtypeStruct((16, WCOLS...]
    reshape x14 -> x19, local copies, waits for them, and re-layouts: 92.6 us -> 34.2 us  [the longest x2 13.7 us: shards(): wd = tall.reshape(64, DROWS, 896)[order, :38].reshape(2432, 896)]
    dot_general x54 -> x26, matrix products: 133 us -> 75.3 us  [the longest x12 35.5 us: dot(): return jnp.dot(a, b, preferred_element_type=F32, **kw)]
  transfers between devices with their start and end apart: 9 -> 2, of which waited for: 5 -> 0; matrix products, arithmetic and copies ran while one was open for 5% -> 8% of each run, Pallas kernels for 0% -> 0%
where the time goes in v1:
time: 788 us; the launch traced here: 774 us
  local copies, waits for them, and re-layouts  470 us (60%)
  Pallas kernels  185 us (23%)
  matrix products  78.2 us (10%)
  other arithmetic  35.2 us (4%)
    gather x512, local copies, waits for them, and re-layouts  338 us
    pallas_call x1, Pallas kernels, scatter_all(): pl.pallas_call(scatter_kernel, out_shape=(jax.ShapeDtypeStruct((16, WCOLS...  97.1 us
    pallas_call x1, Pallas kernels, gather_all(): pl.pallas_call(gather_kernel, out_shape=(jax.ShapeDtypeStruct((2,) * 6 +...  87.5 us
    dot_general x12, matrix products, dot(): return jnp.dot(a, b, preferred_element_type=F32, **kw)  35.5 us
    scatter x1, local copies, waits for them, and re-layouts, shards(): small.at[:, 0, 16:25].set(grad_bias.reshape(128, 9)[inverse])  23.4 us
    unnamed x137, local copies, waits for them, and re-layouts  22.7 us
    gather x2, local copies, waits for them, and re-layouts, shards(): wd = tall.reshape(64, DROWS, 896)[order, :38].reshape(2432, 896)  19.8 us
    dot_general x4, matrix products, dot_t(): return jnp.einsum('nf,df->nd', a, b, preferred_element_type=F32)  17.7 us
  transfers between devices with their start and end apart: 2, of which 0 were waited for; matrix products, arithmetic and copies ran while one was open for 8% of the time, Pallas kernels for 0%

profile of v1, /device:TPU:1, one launch (start us, length us, event | category | flops | bytes accessed | tf_op | source)
XLA Modules:
  0.0 773.6 jit_solution(14089407937363015348)
XLA Ops:
  7.1 2.7 broadcast_select_fusion.1
  15.5 87.5 %shard_map.293 = (bf16[2,2,2,2,2,2,16,7040]{7,6,5,4,3,2,1,0:T(8,128)(2,1)S(1)}, bf16[2,2,2,2,2,2,48,896]{7,6,5,4,3,2,1,0:T(8,128)(2,1)S(1)}) custom-call(bf16[2,16,7040]{2,1,0:T(8,128)(2,1)S(1)} %pad_maximum_fusion.5.pair, bf16[48,896]{1,0:T(8,128)(2,1)S(1)} %pad.28.down), custom_call_target="tpu_custom_call" | custom-call | tf_op jit(solution)/shard_map/pallas_call | solution.py:139
  105.4 4.4 copy-done.1
  109.7 338.7 %while.5 = (s32[]{:T(128)}, bf16[128,8,128]{2,1,0:T(8,128)(2,1)S(1)}, s32[128,3]{0,1:T(4,128)S(1)}, bf16[128,9]{1,0:T(8,128)(2,1)S(1)}, s32[]{:T(128)}, /*index=5*/s32[]{:T(128)}) while((s32[]{:T(128)}, bf16[128,8,128]{2,1,0:T(8,128)(2,1)S(1)}, s32[128,3]{0,1:T(4,128)S(1)}, bf16[128,9]{1,0:T(8,128)(2,1)S(1)}, s32[]{:T(128)}, ...), condition=%wide.while_cond.4, body=%wide.while_body.4.sunk | while | flops 2 | bytes 217 | solution.py:353
  110.3 2.0 dynamic-slice_bitcast_fusion.2
  115.6 2.0 dynamic-slice_bitcast_fusion.2
  120.9 2.0 dynamic-slice_bitcast_fusion.2
  123.6 2.0 dynamic-slice_bitcast_fusion.2
  126.2 2.0 dynamic-slice_bitcast_fusion.2
  128.9 2.0 dynamic-slice_bitcast_fusion.2
  131.5 2.0 dynamic-slice_bitcast_fusion.2
  134.2 2.0 dynamic-slice_bitcast_fusion.2
  136.8 2.0 dynamic-slice_bitcast_fusion.2
  139.4 2.0 dynamic-slice_bitcast_fusion.2
  142.1 2.0 dynamic-slice_bitcast_fusion.2
  144.7 2.0 dynamic-slice_bitcast_fusion.2
  147.4 2.0 dynamic-slice_bitcast_fusion.2
  150.0 2.0 dynamic-slice_bitcast_fusion.2
  155.3 2.0 dynamic-slice_bitcast_fusion.2
  160.6 2.0 dynamic-slice_bitcast_fusion.2
  165.9 2.0 dynamic-slice_bitcast_fusion.2
  171.2 2.0 dynamic-slice_bitcast_fusion.2
  173.8 2.0 dynamic-slice_bitcast_fusion.2
  176.5 2.0 dynamic-slice_bitcast_fusion.2
  179.1 2.0 dynamic-slice_bitcast_fusion.2
  181.8 2.0 dynamic-slice_bitcast_fusion.2
  184.4 2.0 dynamic-slice_bitcast_fusion.2
  187.1 2.0 dynamic-slice_bitcast_fusion.2
  448.6 2.5 convolution_add_fusion
  458.2 2.1 concatenate.105
  468.0 2.6 fusion.45
  470.7 3.0 fusion.104
  476.7 2.5 multiply_reduce_fusion.2
  481.4 3.4 collective-permute-start
  485.4 6.4 copy.239
  491.8 12.9 %gather_fusion = bf16[64,38,896]{2,0,1:T(8,128)(2,1)} fusion(bf16[64,48,896]{2,0,1:T(8,128)(2,1)} %copy.239, s32[64]{0:T(128)S(1)} %copy-done.20), kind=kCustom, calls=%fused_computation | custom fusion | bytes 8716800 | tf_op jit(solution)/shard_map/gather | solution.py:351
  504.7 6.9 copy.240
  511.6 7.3 reshape.503
  524.4 7.3 fusion.3
  531.8 4.6 fusion.7
  536.4 9.3 %multiply_convert_fusion.2 = (bf16[512,2432]{1,0:T(8,128)(2,1)}, bf16[512,2432]{1,0:T(8,128)(2,1)}, bf16[512,2432]{1,0:T(8,128)(2,1)}) fusion(f32[512,2432]{1,0:T(8,128)} %fusion.3, f32[512,2432]{1,0:T(8,128)} %fusion.7, bf16[2432,896]{1,0:T(8,128)(2,1)S(1)} %bitcast.241, bf16[512,1792]{1,0:T(8,128)(2,1)} %copy-done.22), kind=kOutput, calls=%fused_computation.12 | convolution fusion | flops 2251292672 | bytes 22708224 | tf_op jit(solution)/shard_map/nf,df->nd/dot_general | solution.py:297
  545.7 6.0 fusion.109
  551.7 4.9 convolution_convert_fusion.2
  556.6 2.9 fusion.1
  559.5 2.9 fusion.22
  564.4 7.3 reshape.514
  571.7 5.5 gather_fusion.3
  577.2 5.3 pad.29
  582.5 3.1 convolution_convert_fusion.1
  587.3 4.6 convolution_convert_fusion
  591.9 3.3 constant_dynamic-update-slice_fusion.17
  595.5 3.2 fusion.13
  600.8 2.3 subtract_add_fusion
  603.2 3.9 convolution_convert_fusion.9
  607.1 2.9 reshape.577
  611.9 2.1 fusion.35
  621.3 2.6 fusion.9
  624.0 2.3 convolution_convert_fusion.3
  626.2 2.0 convolution_convert_fusion.4
  628.5 3.4 fusion.55
  635.2 3.5 constant_dynamic-update-slice_fusion.16
  640.3 2.1 broadcast_select_fusion
  642.4 23.4 %scatter.19 = bf16[128,8,128]{2,1,0:T(8,128)(2,1)S(1)} dynamic-update-slice(bf16[128,8,128]{2,1,0:T(8,128)(2,1)S(1)} %scatter.16, bf16[128,1,9]{2,1,0:T(2,128)(2,1)S(1)} %broadcast_select_fusion, s32[]{:T(128)} %constant.168.clone.1, s32[]{:T(128)} %bitcast.3, s32[]{:T(128)} %bitcast.4) | dynamic-update-slice | bytes 4612 | tf_op jit(solution)/shard_map/scatter | solution.py:434
  666.5 97.1 %shard_map.294 = (f32[16,7040]{1,0:T(8,128)}, bf16[16,7040]{1,0:T(8,128)(2,1)}, f32[48,896]{1,0:T(8,128)}) custom-call(bf16[2,2,2,2,2,2,16,7040]{7,6,5,4,3,2,1,0:T(8,128)(2,1)} %constant_dynamic-update-slice_fusion.14.gw, bf16[2,2,2,2,2,2,48,896]{7,6,5,4,3,2,1,0:T(8,128)(2,1)} %bitcast.232), custom_call_target="tpu_custom_call" | custom-call | tf_op jit(solution)/shard_map/pallas_call | solution.py:246
  (746 shorter events, 360.9 us)
Async XLA Ops:
  0.6 102.4 %copy-start.2 = (bf16[896,1024]{1,0:T(8,128)(2,1)S(1)}, bf16[896,1024]{1,0:T(8,128)(2,1)}, u32[]{:S(2)}) copy-start(bf16[896,1024]{1,0:T(8,128)(2,1)} %constant.189.clone) | copy-start | bytes 5505028
  0.7 14.8 %copy-start.31 = (bf16[38,896]{1,0:T(8,128)(2,1)S(1)}, bf16[38,896]{1,0:T(8,128)(2,1)}, u32[]{:S(2)}) copy-start(bf16[38,896]{1,0:T(8,128)(2,1)} %param.38) | copy-start | bytes 204292
  0.7 14.1 %copy-start.40 = (s32[2]{0:T(128)}, s32[2]{0:T(128)S(1)}, u32[]{:S(2)}) copy-start(s32[2]{0:T(128)S(1)} %iota_multiply_fusion) | copy-start | bytes 28
  14.2 89.5 %copy-start.12 = (bf16[2,1,128,896]{3,2,1,0:T(8,128)(2,1)S(1)}, bf16[2,1,128,896]{3,2,1,0:T(8,128)(2,1)}, u32[]{:S(2)}) copy-start(bf16[2,1,128,896]{3,2,1,0:T(8,128)(2,1)} %param.30) | copy-start | bytes 1376260
  103.0 2.4 copy-start
  103.0 6.8 copy-start.1
  103.6 1.8 copy-start.34
  105.4 345.8 %copy-start.25 = (bf16[256,1024]{1,0:T(8,128)(2,1)}, bf16[256,1024]{1,0:T(8,128)(2,1)S(1)}, u32[]{:S(2)}) copy-start(bf16[256,1024]{1,0:T(8,128)(2,1)S(1)} %convolution_convert_fusion.7) | copy-start | bytes 1572868
  448.6 4.9 copy-start.37
  451.2 1.6 copy-start.27
  457.2 7.7 %slice-start.6 = ((f32[256,1152]{1,0:T(8,128)}), f32[256,128]{1,0:T(8,128)S(1)}, s32[]{:S(2)}) async-start(f32[256,1152]{1,0:T(8,128)} %copy-done.27), calls=%async_computation.6 | async-start | bytes 262144 | tf_op jit(solution)/shard_map/slice | solution.py:367
  458.2 9.8 %copy-start.16 = (f32[2,128,2,7,64]{1,0,4,3,2:T(2,128)S(1)}, f32[2,128,2,7,64]{1,0,4,3,2:T(2,128)}, u32[]{:S(2)}) copy-start(f32[2,128,2,7,64]{1,0,4,3,2:T(2,128)} %reshape.498) | copy-start | bytes 2752516
  464.4 0.8 copy-start.38
  470.6 3.1 copy-start.32
  473.7 1.8 copy-start.35
  476.7 2.7 copy-start.18
  476.7 3.6 copy-start.14
  479.2 119.5 %copy-start.8 = (f32[256,896]{1,0:T(8,128)}, f32[256,896]{1,0:T(8,128)S(1)}, u32[]{:S(2)}) copy-start(f32[256,896]{1,0:T(8,128)S(1)} %get-tuple-element.206) | copy-start | bytes 2752516
  479.2 5.5 copy-start.41
  479.3 5.5 copy-start.47
  479.5 0.9 copy-start.13
  481.4 39.0 %collective-permute-start = (bf16[256,1792]{1,0:T(8,128)(2,1)}, bf16[256,1792]{1,0:T(8,128)(2,1)}, u32[]{:S(2)}, u32[]{:S(2)}) collective-permute-start(bf16[256,1792]{1,0:T(8,128)(2,1)} %pad_maximum_fusion.2), channel_id=1, source_target_pairs={{0,32},{32,0},{64,96},{96,64},{1,33},{33,1},{65,97},{97,65},{2,34}... | collective-permute-start | bytes 2752520 | tf_op jit(solution)/shard_map/ppermute | solution.py:389
  485.4 6.4 copy-start.20
  511.6 7.3 copy-start.45
  511.6 7.3 copy-start.46
  511.6 7.9 %copy-start.39 = (s32[2,128]{1,0:T(2,128)S(1)}, s32[2,128]{1,0:T(2,128)}, u32[]{:S(2)}) copy-start(s32[2,128]{1,0:T(2,128)} %copy-done.38) | copy-start | bytes 3076
  511.6 7.9 %copy-start.44 = (f32[32]{0:T(128)S(1)}, f32[32]{0:T(128)}, u32[]{:S(2)}) copy-start(f32[32]{0:T(128)} %negate_power_fusion) | copy-start | bytes 388
  521.9 1.2 copy-start.22
  523.1 8.6 %slice-start = ((s8[14417920]{0:T(1024)(128)(4,1)}), s8[4194304]{0:T(1024)(128)(4,1)S(1)}, s32[]{:S(2)}) async-start(s8[14417920]{0:T(1024)(128)(4,1)} %bitcast.227), calls=%async_computation | async-start | bytes 8388608
  524.4 7.4 copy-start.53
  524.4 7.4 slice-start.1
  524.4 7.4 slice-start.2
  524.4 7.4 slice-start.3
  524.4 12.0 %slice-start.4 = ((s8[4358144]{0:T(1024)(128)(4,1)}), s8[4194304]{0:T(1024)(128)(4,1)S(1)}, s32[]{:S(2)}) async-start(s8[4358144]{0:T(1024)(128)(4,1)} %bitcast.240), calls=%async_computation.4 | async-start | bytes 8388608
  531.8 4.6 slice-start.5
  545.7 6.0 copy-start.23
  545.7 6.0 copy-start.52
  551.7 10.8 %copy-start.10 = (f32[512,896]{1,0:T(8,128)}, f32[512,896]{1,0:T(8,128)S(1)}, u32[]{:S(2)}) copy-start(f32[512,896]{1,0:T(8,128)S(1)} %fusion.109) | copy-start | bytes 5505028
  551.7 4.9 copy-start.48
  556.6 2.9 copy-start.50
  562.5 1.9 copy-start.4
  564.4 30.9 %collective-permute-start.1 = (f32[256,1920]{1,0:T(8,128)}, f32[256,1920]{1,0:T(8,128)}, u32[]{:S(2)}, u32[]{:S(2)}) collective-permute-start(f32[256,1920]{1,0:T(8,128)} %pad_maximum_fusion), channel_id=1, source_target_pairs={{0,32},{32,0},{64,96},{96,64},{1,33},{33,1},{65,97},{97,65},{2,34}... | collective-permute-start | bytes 5898248 | tf_op jit(solution)/shard_map/ppermute | solution.py:406
  577.2 5.3 copy-start.51
  577.2 5.3 copy-start.54
  585.6 1.7 copy-start.49
  591.9 3.3 copy-start.5
  591.9 3.6 copy-start.11
  595.2 7.9 %copy-start.3 = (bf16[2,2,2,2,2,2,16,7040]{7,6,5,4,3,2,1,0:T(8,128)(2,1)}, bf16[2,2,2,2,2,2,16,7040]{7,6,5,4,3,2,1,0:T(8,128)(2,1)S(1)}, u32[]{:S(2)}) copy-start(bf16[2,2,2,2,2,2,16,7040]{7,6,5,4,3,2,1,0:T(8,128)(2,1)S(1)} %constant_dynamic-update-slice_fusion.17) | copy-start | bytes 43253764
  598.8 2.0 copy-start.15
  603.2 3.9 copy-start.6
  611.9 2.2 copy-start.21
  611.9 2.2 copy-start.33
  611.9 2.1 copy-start.36
  614.6 1.0 copy-start.24
  619.6 1.4 copy-start.28
  619.6 1.4 copy-start.29
  621.3 2.6 copy-start.26
  623.9 2.3 copy-start.7
  624.0 2.3 copy-start.19
  635.2 3.5 copy-start.9
  666.5 100.9 %copy-start.43 = (f32[256]{0:T(256)S(1)}, f32[256]{0:T(256)}, u32[]{:S(2)}) copy-start(f32[256]{0:T(256)} %get-tuple-element.146) | copy-start | bytes 3076
  763.6 7.4 copy-start.30
  763.6 8.7 %copy-start.17 = (f32[256,896]{1,0:T(8,128)S(1)}, f32[256,896]{1,0:T(8,128)}, u32[]{:S(2)}) copy-start(f32[256,896]{1,0:T(8,128)} %get-tuple-element.210) | copy-start | bytes 2752516
  763.6 8.7 %copy-start.42 = (f32[256]{0:T(256)S(1)}, f32[256]{0:T(256)}, u32[]{:S(2)}) copy-start(f32[256]{0:T(256)} %multiply_multiply_fusion) | copy-start | bytes 3076

commit v2 on v1

v2 whole, which is shorter than its diff:
```python
import functools

import jax
import jax.numpy as jnp
import numpy as np
from jax import lax
from jax.experimental import pallas as pl
from jax.experimental.pallas import tpu as pltpu
from jax.sharding import PartitionSpec as P

EPSILON = 1e-06
THETA = 1000000.0
NEG_FILL = -1e30
MESH = pl.DeviceIdType.MESH
AXES = ("dp", "fsdp")
BF = jnp.bfloat16
F32 = jnp.float32
GRAY = (0, 1, 3, 2)

FFN_WAVES = (
    ((0, 2), (2, 2), (4, 2), (6, 2), (8, 2), (10, 2)),
    ((12, 2), (14, 2), (16, 2), (18, 2), (20, 2), (22, 2)),
    ((24, 3), (27, 2), (29, 2), (31, 3), (34, 2), (36, 2)),
)
ATT_WAVE = ((38, 2), (40, 2), (42, 2), (44, 2), (46, 2), (48, 2))
DOWN_WAVE = ((0, 4), (4, 3), (7, 4), (11, 3), (14, 4), (18, 3))
WAVES = (ATT_WAVE, DOWN_WAVE) + FFN_WAVES
ATT, DOWN, FFN = 0, 1, 2
UNITS, TALL = 50, 21
ORDER = tuple(
    tuple(2 * ((p % 3 + k // 2) % 3) + ((k % 2) ^ (p // 3)) for k in range(6)) for p in range(6)
)


def here():
    dp = lax.axis_index("dp")
    fs = lax.axis_index("fsdp")
    return (fs // 4) % 4, fs % 4, (dp // 2) * 2 + fs // 16, dp % 2


def device(x, y, z, core):
    return ((z // 2) * 2 + core, (z % 2) * 16 + x * 4 + y)


def gray_bits(v):
    high = v // 2
    low = (v % 2 + high) % 2
    return low, high


def flip(v, bit):
    if bit == 0:
        return v + 1 - 2 * (v % 2)
    return 3 - v


def partner(bit):
    x, y, z, core = here()
    axis, low = bit // 2, bit % 2
    place = [x, y, z]
    place[axis] = flip(place[axis], low)
    return device(*place, core)


def sibling():
    x, y, z, core = here()
    return device(x, y, z, 1 - core)


def my_bits():
    x, y, z, _ = here()
    bits = []
    for v in (x, y, z):
        low, high = gray_bits(v)
        bits += [low, high]
    return bits


DIMS = (1, 0, 3, 2, 5, 4)


def slot(bits, full, skip=None):
    return tuple(slice(None) if b in full else bits[b] for b in DIMS if b != skip)


def dot(a, b):
    return lax.dot_general(a, b, (((1,), (0,)), ((), ())), preferred_element_type=F32)


def dot_t(a, b):
    return lax.dot_general(a, b, (((1,), (1,)), ((), ())), preferred_element_type=F32)


def layer_kernel(
    pair, down, x_own, e_own, seg_own, spread, spread_o, pack, unpack, brow, freq,
    out_ref, gtok_ref, own_ref, sib_ref,
    u_buf, t_buf, u_got, t_got, wd, x_all, e_all, seg_all, stage, a1s, a2s, a2st, qkv, o_s,
    y1, ypart, yrec, da2, darec, mrec, arec, cosine, sine, gain, bias, slab,
    ag_recv, rs_recv, sends_sem, credit, sib_send, sib_recv, loc_sem,
):
    _, _, _, core = here()
    bits = my_bits()
    flipped = [1 - b for b in bits]
    sib = sibling()
    peers = [partner(b) for b in range(6)]

    barrier = pltpu.get_barrier_semaphore()
    for b in range(6):
        pl.semaphore_signal(barrier, inc=1, device_id=peers[b], device_id_type=MESH)
    pl.semaphore_signal(barrier, inc=1, device_id=sib, device_id_type=MESH)
    pl.semaphore_wait(barrier, 7)

    def to_sibling(src, dst, i):
        return pltpu.make_async_remote_copy(
            src_ref=src, dst_ref=dst, send_sem=sib_send.at[i], recv_sem=sib_recv.at[i],
            device_id=sib, device_id_type=MESH)

    swap_pair = to_sibling(pair.at[1], stage, 0)
    swap_pair.start()
    own = pl.ds(pl.multiple_of(core * 256, 256), 256)
    swap_seg = to_sibling(seg_own, seg_all.at[core], 1)
    swap_x = to_sibling(x_own, x_all.at[own], 2)
    swap_e = to_sibling(e_own, e_all.at[own], 3)
    for c in (swap_seg, swap_x, swap_e):
        c.start()
    locals_ = [
        pltpu.make_async_copy(seg_own, seg_all.at[core], loc_sem.at[0]),
        pltpu.make_async_copy(x_own, x_all.at[own], loc_sem.at[1]),
        pltpu.make_async_copy(e_own, e_all.at[own], loc_sem.at[2]),
    ]
    for c in locals_:
        c.start()

    def bufs(w):
        return (t_buf, t_got) if w == DOWN else (u_buf, u_got)

    def ag_copy(w, k, p):
        start, n = WAVES[w][p]
        order = ORDER[p]
        ref = bufs(w)[0].at[(pl.ds(start, n),) + slot(bits, order[:k])]
        return pltpu.make_async_remote_copy(
            src_ref=ref, dst_ref=ref, send_sem=sends_sem.at[w, p, k],
            recv_sem=ag_recv.at[w, p, k], device_id=peers[order[k]], device_id_type=MESH)

    def ag(w, k):
        for p in range(6):
            if k > 0:
                ag_copy(w, k - 1, p).wait_recv()
            ag_copy(w, k, p).start()

    def ag_done(w):
        for p in range(6):
            ag_copy(w, 5, p).wait_recv()
        for p in range(6):
            for k in range(6):
                ag_copy(w, k, p).wait_send()

    def rs_copy(w, k, p):
        start, n = WAVES[w][p]
        order = ORDER[p]
        acc, got = bufs(w)
        b = list(bits)
        b[order[k]] = flipped[order[k]]
        src = acc.at[(pl.ds(start, n),) + slot(b, order[:k])]
        if k == 5:
            dst = got.at[pl.ds(start, n)]
        else:
            b = list(bits)
            b[order[5]] = flipped[order[5]]
            dst = acc.at[(pl.ds(start, n),) + slot(b, order[:k])]
        return pltpu.make_async_remote_copy(
            src_ref=src, dst_ref=dst, send_sem=sends_sem.at[w, p, k],
            recv_sem=rs_recv.at[w, p, k], device_id=peers[order[k]], device_id_type=MESH)

    def rs_add(w, k, p):
        start, n = WAVES[w][p]
        order = ORDER[p]
        acc, got = bufs(w)
        here_at = slot(bits, order[:k])
        b = list(bits)
        b[order[5]] = flipped[order[5]]
        b[order[k]] = flipped[order[k]]
        there_at = slot(b, order[:k])

        def one(u):
            add = got[u] if k == 5 else acc[(u,) + there_at]
            acc[(u,) + here_at] = acc[(u,) + here_at] + add

        if k >= 3:
            @pl.loop(0, n)
            def _(i):
                one(start + i)
        else:
            for i in range(n):
                one(start + i)

    def rs(w, k):
        if k == 4:
            for p in range(6):
                rs_copy(w, 5, p).wait_send()
            for b in range(6):
                pl.semaphore_signal(credit.at[w, b], inc=1, device_id=peers[b],
                                    device_id_type=MESH)
        for p in range(6):
            if k < 5:
                rs_copy(w, k + 1, p).wait_recv()
                rs_add(w, k + 1, p)
            if k == 4:
                pl.semaphore_wait(credit.at[w, ORDER[p][4]], 1)
            rs_copy(w, k, p).start()

    def rs_end(w):
        acc, _ = bufs(w)
        base = UNITS if w == DOWN else 0
        for p in range(6):
            start, n = WAVES[w][p]
            order = ORDER[p]
            rs_copy(w, 0, p).wait_recv()
            b = list(bits)
            b[order[5]] = flipped[order[5]]
            b[order[0]] = flipped[order[0]]
            units = pl.ds(start, n)
            total = (acc[(units,) + slot(bits, ())].astype(F32)
                     + acc[(units,) + slot(b, ())].astype(F32))
            own_ref[pl.ds(base + start, n)] = total
            if w != DOWN:
                slab[units] = total.astype(BF)
        for p in range(6):
            for k in range(5):
                rs_copy(w, k, p).wait_send()

    def last_swap(w):
        start = WAVES[w][0][0]
        n = sum(m for _, m in WAVES[w])
        return to_sibling(slab.at[pl.ds(start, n)], sib_ref.at[pl.ds(start, n)], 16 + w)

    def rows(s):
        return pl.ds(pl.multiple_of(s * 128, 128), 128)

    def unit(u):
        return u_buf[u].reshape(1024, 128)

    mine = slot(bits, ())
    t_buf[(slice(None),) + mine] = down[...]
    swap_pair.wait()
    u_buf[(slice(None),) + mine] = pair[0] + stage[...]
    ag(ATT, 0)
    ag(DOWN, 0)
    ag(ATT, 1)
    ag(FFN, 0)
    ag(ATT, 2)
    ag(DOWN, 1)
    ag(ATT, 3)
    ag(DOWN, 2)
    ag(ATT, 4)
    for c in locals_:
        c.wait()
    for c in (swap_seg, swap_x, swap_e):
        c.wait()
    ag(ATT, 5)

    causal = (lax.broadcasted_iota(jnp.int32, (128, 128), 1)
              <= lax.broadcasted_iota(jnp.int32, (128, 128), 0))

    def allowed(s):
        line = seg_all[s // 2, pl.ds(s % 2, 1), :]
        across = jnp.broadcast_to(line, (128, 128))
        return jnp.logical_and(causal, across == across.T)

    for s in range(4):
        place = jnp.sum(allowed(s).astype(F32), axis=1, keepdims=True) - 1.0
        angle = place * freq[0:1, :]
        cosine[rows(s), :] = jnp.cos(angle)
        sine[rows(s), :] = jnp.sin(angle)
    ag(DOWN, 3)
    ag(FFN, 1)
    ag_done(ATT)
    ag(DOWN, 4)
    ag(FFN, 2)

    small = unit(42).T
    gain[...] = dot_t(small[64:80], spread[...])[0:8]
    hit = (lax.broadcasted_iota(jnp.int32, (1024, 640), 0) == brow[core, 0:1, :]).astype(BF)
    picked = dot(small[80:96], hit)
    choose = lax.broadcasted_iota(jnp.int32, (16, 640), 0) == brow[core, 1:2, :]
    bias[...] = jnp.broadcast_to(
        jnp.sum(jnp.where(choose, picked, 0.0), axis=0, keepdims=True), (8, 640))

    def inv_root(v):
        return lax.rsqrt(jnp.mean(v * v, axis=-1, keepdims=True) + EPSILON)

    @pl.loop(0, 4)
    def _(s):
        v = x_all[rows(s), :].astype(F32)
        a1 = (v * inv_root(v) * gain[0:1, :]).astype(BF)
        a1s[rows(s), :] = dot(a1, spread[...]).astype(BF)

    ag(FFN + 1, 0)
    ag(FFN, 3)
    lane = lax.broadcasted_iota(jnp.int32, (128, 640), 1)
    first = lane % 64 < 32
    turns = lane < 512

    def wide(ref, s):
        return jnp.concatenate([ref[rows(s), :]] * 5, axis=1)

    w_qkv = jnp.concatenate([unit(38 + i) for i in range(5)], axis=1)
    for s in range(4):
        raw = dot(a1s[rows(s), :], w_qkv) + bias[0:1, :]
        turned = jnp.where(first, -pltpu.roll(raw, 608, 1), pltpu.roll(raw, 32, 1))
        turned = raw * wide(cosine, s) + turned * wide(sine, s)
        qkv[rows(s), :] = jnp.where(turns, turned, raw).astype(BF)
    ag(DOWN, 5)
    ag(FFN + 1, 1)

    def heads(v):
        return jnp.concatenate([v[:, 64 * h:64 * h + 64] for h in range(7)], axis=0)

    def unheads(v):
        return jnp.concatenate([v[128 * h:128 * h + 128, :] for h in range(7)], axis=1)

    def attend(s):
        q7 = heads(qkv[rows(s), 0:448])
        k = qkv[rows(s), 448:512]
        v = qkv[rows(s), 512:576]
        score = dot_t(q7, k) * 0.125
        ok = allowed(s)
        score = jnp.where(jnp.concatenate([ok] * 7, axis=0), score, NEG_FILL)
        e = jnp.exp(score - jnp.max(score, axis=-1, keepdims=True))
        soft = e / jnp.sum(e, axis=-1, keepdims=True)
        return q7, k, v, soft

    def w_out():
        return jnp.concatenate(
            [u_buf[43 + i, :, :, :, :, core].reshape(512, 128) for i in range(7)], axis=1)

    def y_swap(s):
        return to_sibling(ypart.at[rows(s)], yrec.at[rows(s)], 4 + s)

    @pl.loop(0, 4)
    def _(s):
        _, _, v, soft = attend(s)
        o = unheads(dot(soft.astype(BF), v)).astype(BF)
        os = dot(o, spread_o[core]).astype(BF)
        o_s[rows(s), :] = os
        ypart[rows(s), :] = dot(os, w_out())
        y_swap(s).start()
    ag(FFN, 4)
    ag(FFN + 1, 2)

    ag_done(DOWN)
    ag(FFN, 5)
    ag(FFN + 1, 3)
    ag(FFN + 2, 0)

    def slab_place(s):
        z, x, y = s // 16, s // 4 % 4, s % 4
        b = []
        for v in (x, y, z):
            low, high = gray_bits(v)
            b += [low, high]
        return slot(b, ())

    @pl.loop(0, 8)
    def _(g):
        lines = []
        for i in range(8):
            at = slab_place(g * 8 + i)
            for r in range(3):
                lines.append(jnp.concatenate(
                    [t_buf[(3 * c + r,) + at] for c in range(7)], axis=1))
        block = jnp.concatenate(lines, axis=0)
        wd[pl.ds(pl.multiple_of(g * 304, 16), 304), :] = dot(pack[...], block).astype(BF)

    ag(FFN + 1, 4)
    ag(FFN + 2, 1)

    @pl.loop(0, 4)
    def _(s):
        y_swap(s).wait()
        v = x_all[rows(s), :].astype(F32) + (ypart[rows(s), :] + yrec[rows(s), :])
        y1[rows(s), :] = v
        a2 = (v * inv_root(v) * gain[1:2, :]).astype(BF)
        a2s[rows(s), :] = dot(a2, spread[...]).astype(BF)
        ypart[rows(s), :] = jnp.zeros((128, 896), F32)
        da2[rows(s), :] = jnp.zeros((128, 1024), F32)

    ag(FFN + 1, 5)
    ag(FFN + 2, 2)
    a2st[...] = a2s[...].T
    ag(FFN + 2, 3)

    def ffn(gates, ups, row, n):
        width = 128 * n
        w = jnp.concatenate([unit(i) for i in gates + ups], axis=1)
        both = dot(a2s[...], w)
        g, u = both[:, :width], both[:, width:]
        at = pl.ds(pl.multiple_of(row, 128), width)
        w_d = wd[at, :]
        dm = dot_t(e_all[...], w_d)
        sig = 1.0 / (1.0 + jnp.exp(-g))
        silu = g * sig
        m = (silu * u).astype(BF)
        dg = (dm * u * sig * (1.0 + g * (1.0 - sig))).astype(BF)
        du = (dm * silu).astype(BF)
        dgu = jnp.concatenate([dg, du], axis=1)
        ypart[...] += dot(m, w_d)
        da2[...] += dot_t(dgu, w)
        wd[at, :] = dot(m.T, e_all[...]).astype(BF)
        for part, places in ((dg, gates), (du, ups)):
            grads = dot(a2st[...], part).astype(BF)
            for i, place in enumerate(places):
                u_buf[place] = grads[:, 128 * i:128 * i + 128].reshape((2,) * 6 + (16, 128))

    ag_done(FFN)

    @pl.loop(0, 9)
    def _(i):
        def at(t, *acts):
            @pl.when(i == t)
            def _():
                for f, a in acts:
                    f(*a)

        at(1, (ag, (FFN + 2, 4)))
        at(2, (ag, (FFN + 2, 5)))
        at(3, (rs, (FFN, 5)), (ag_done, (FFN + 1,)))
        at(4, (rs, (FFN, 4)))
        at(5, (rs, (FFN, 3)))
        at(6, (rs, (FFN + 1, 5)), (ag_done, (FFN + 2,)))
        at(7, (rs, (FFN, 2)), (rs, (FFN + 1, 4)))
        at(8, (rs, (FFN, 1)), (rs, (FFN + 1, 3)))
        g = 12 * (i // 3) + 2 * (i % 3) + (i + 1) // 8
        u = g + 6 + i // 6
        ffn([g, g + 1], [u, u + 1], i * 256, 2)

    ffn([26], [33], 2304, 1)
    rs(FFN + 2, 5)
    rs(FFN, 0)
    rs(FFN + 1, 2)

    other = pl.ds(pl.multiple_of((1 - core) * 256, 256), 256)
    out_swap = to_sibling(ypart.at[other], mrec, 8)
    out_swap.start()

    def unspread(v):
        high = v.astype(BF)
        low = (v - high.astype(F32)).astype(BF)
        return dot_t(high, spread[...]) + dot_t(low, spread[...])

    def da_swap(s):
        return to_sibling(yrec.at[rows(s)], darec.at[rows(s)], 9 + s)

    @pl.loop(0, 4)
    def _(s):
        yrec[rows(s), :] = unspread(da2[rows(s), :])
        da_swap(s).start()

    @pl.loop(0, 8)
    def _(g):
        block = dot(unpack[...], wd[pl.ds(pl.multiple_of(g * 304, 16), 304), :]).astype(BF)
        for i in range(8):
            at = slab_place(g * 8 + i)
            for r in range(3):
                for c in range(7):
                    t_buf[(3 * c + r,) + at] = block[48 * i + 16 * r:48 * i + 16 * r + 16,
                                                     128 * c:128 * c + 128]

    rs(DOWN, 5)
    rs_end(FFN)
    last_swap(FFN).start()
    rs(FFN + 1, 1)
    rs(FFN + 2, 4)
    out_swap.wait()
    for s in range(2):
        at = pl.ds(pl.multiple_of(core * 256 + 128 * s, 128), 128)
        out_ref[pl.ds(128 * s, 128), :] = (
            y1[at, :] + (ypart[at, :] + mrec[pl.ds(128 * s, 128), :])).astype(BF)

    gain_grads = gain.at[pl.ds(2, 2)]
    gain_grads[...] = jnp.zeros((2, 896), F32)

    @pl.loop(0, 4)
    def _(s):
        da_swap(s).wait()
        da = yrec[rows(s), :] + darec[rows(s), :]
        v = y1[rows(s), :]
        r = inv_root(v)

        @pl.when(s // 2 == core)
        def _():
            gain[3:4, :] += jnp.sum(da * v * r, axis=0, keepdims=True)

        w = da * gain[1:2, :]
        dy = (e_all[rows(s), :].astype(F32) + r * w
              - v * (r * r * r) * jnp.mean(w * v, axis=-1, keepdims=True))
        darec[rows(s), :] = dy
        f = dy.astype(BF)
        a2s[rows(s), 0:896] = f
        ds_ = dot_t(f, w_out()).astype(BF)
        a2s[rows(s), 896:1024] = jnp.zeros((128, 128), BF)
        a2st[rows(s), 0:448] = dot_t(ds_, spread_o[core]).astype(BF)

    rs(DOWN, 4)
    rs(FFN + 1, 0)
    rs(FFN + 2, 3)
    o_grad = dot(o_s[...].T, a2s[:, 0:896]).astype(BF)
    for i in range(7):
        part = o_grad[:, 128 * i:128 * i + 128].reshape((2,) * 5 + (16, 128))
        u_buf[43 + i, :, :, :, :, core] = part
        u_buf[43 + i, :, :, :, :, 1 - core] = jnp.zeros_like(part)
    rs_end(FFN + 1)
    last_swap(FFN + 1).start()
    rs(DOWN, 3)
    rs(FFN + 2, 2)

    bias[...] = jnp.zeros((8, 640), F32)

    @pl.loop(0, 4)
    def _(s):
        q7, k, v, soft = attend(s)
        do7 = heads(a2st[rows(s), 0:448])
        dp = dot_t(do7, v)
        ds_ = (soft * (dp - jnp.sum(soft * dp, axis=-1, keepdims=True))).astype(BF)
        dq = unheads(dot(ds_, k)) * 0.125
        dk = dot(ds_.T, q7) * 0.125
        dv = dot(soft.astype(BF).T, do7)
        raw = jnp.concatenate([dq, dk, dv, jnp.zeros((128, 64), F32)], axis=1)
        scaled = raw * wide(sine, s)
        turned = jnp.where(first, pltpu.roll(scaled, 608, 1), -pltpu.roll(scaled, 32, 1))
        grad = jnp.where(turns, raw * wide(cosine, s) + turned, raw).astype(BF)
        qkv[rows(s), :] = grad
        bias[0:1, :] += jnp.sum(grad.astype(F32), axis=0, keepdims=True)

    rs(DOWN, 2)
    rs(FFN + 2, 1)
    w_qkv = jnp.concatenate([unit(38 + i) for i in range(5)], axis=1)
    da2[...] = dot_t(qkv[...], w_qkv)

    @pl.loop(0, 4)
    def _(s):
        yrec[rows(s), :] = unspread(da2[rows(s), :])

    a_swap = to_sibling(yrec.at[other], arec, 13)
    a_swap.start()
    rs(DOWN, 1)
    rs(FFN + 2, 0)
    a2st[...] = a1s[...].T
    for i in range(4):
        part = dot(a2st[...], qkv[:, 128 * i:128 * i + 128])
        u_buf[38 + i] = part.astype(BF).reshape((2,) * 6 + (16, 128))
    a_swap.wait()
    for s in range(2):
        at = pl.ds(pl.multiple_of(core * 256 + 128 * s, 128), 128)
        da = yrec[at, :] + arec[pl.ds(128 * s, 128), :]
        v = x_all[at, :].astype(F32)
        r = inv_root(v)
        gain[2:3, :] += jnp.sum(da * v * r, axis=0, keepdims=True)
        w = da * gain[0:1, :]
        gtok_ref[pl.ds(128 * s, 128), :] = (
            darec[at, :] + r * w
            - v * (r * r * r) * jnp.mean(w * v, axis=-1, keepdims=True)).astype(BF)
    top = dot(jnp.concatenate([gain[2:4, :], jnp.zeros((14, 896), F32)], axis=0).astype(BF),
              spread[...])
    spot = jnp.where(choose, jnp.broadcast_to(bias[0:1, :], (16, 640)), 0.0).astype(BF)
    hit = (lax.broadcasted_iota(jnp.int32, (1024, 640), 0) == brow[core, 0:1, :]).astype(BF)
    low = dot_t(spot, hit)
    small = jnp.concatenate(
        [jnp.zeros((64, 1024), F32), top, low, jnp.zeros((32, 1024), F32)], axis=0).T
    part = dot(a2st[...], qkv[:, 512:640]) + small
    u_buf[42] = part.astype(BF).reshape((2,) * 6 + (16, 128))
    rs(ATT, 5)
    rs(DOWN, 0)
    rs_end(FFN + 2)
    last_swap(FFN + 2).start()
    rs(ATT, 4)
    rs_end(DOWN)
    for k in (3, 2, 1, 0):
        rs(ATT, k)
    rs_end(ATT)
    last_swap(ATT).start()
    for w in (ATT, FFN, FFN + 1, FFN + 2):
        last_swap(w).wait()


def layer(pair, down, x, e, seg, spread, spread_o, pack, unpack, brow, freq):
    dma = pltpu.SemaphoreType.DMA
    vm = pltpu.VMEM
    return pl.pallas_call(
        layer_kernel,
        out_shape=(
            jax.ShapeDtypeStruct((256, 896), BF),
            jax.ShapeDtypeStruct((256, 896), BF),
            jax.ShapeDtypeStruct((UNITS + TALL, 16, 128), F32),
            jax.ShapeDtypeStruct((UNITS, 16, 128), BF),
        ),
        in_specs=[pl.BlockSpec(memory_space=vm)] * 2 + [pl.BlockSpec(memory_space=pl.ANY)] * 2
        + [pl.BlockSpec(memory_space=vm)] * 7,
        out_specs=[pl.BlockSpec(memory_space=vm)] * 4,
        scratch_shapes=[
            vm((UNITS,) + (2,) * 6 + (16, 128), BF), vm((TALL,) + (2,) * 6 + (16, 128), BF),
            vm((UNITS,) + (2,) * 5 + (16, 128), BF), vm((TALL,) + (2,) * 5 + (16, 128), BF),
            vm((2432, 896), BF), vm((512, 896), BF), vm((512, 896), BF), vm((2, 8, 128), F32),
            vm((UNITS, 16, 128), BF), vm((512, 1024), BF), vm((512, 1024), BF),
            vm((1024, 512), BF), vm((512, 640), BF), vm((512, 512), BF),
            vm((512, 896), F32), vm((512, 896), F32), vm((512, 896), F32), vm((512, 1024), F32),
            vm((512, 896), F32), vm((256, 896), F32), vm((256, 896), F32), vm((512, 128), F32), vm((512, 128), F32),
            vm((8, 896), F32), vm((8, 640), F32), vm((UNITS, 16, 128), BF),
            dma((5, 6, 6)), dma((5, 6, 6)), dma((5, 6, 6)), pltpu.SemaphoreType.REGULAR((5, 6)),
            dma((21,)), dma((21,)), dma((3,)),
        ],
        compiler_params=pltpu.CompilerParams(collective_id=0, has_side_effects=True,
                                             vmem_limit_bytes=60 * 2**20),
    )(pair, down, x, e, seg, spread, spread_o, pack, unpack, brow, freq)


def constants():
    slots = np.zeros(128, np.int32)
    for n in range(128):
        dp, fs = n // 32, n % 32
        x, y, z, core = fs // 4 % 4, fs % 4, (dp // 2) * 2 + fs // 16, dp % 2
        slots[n] = ((GRAY[x] * 4 + GRAY[y]) * 4 + GRAY[z]) * 2 + core
    spread = np.zeros((896, 1024), np.float32)
    for d in range(896):
        spread[d, slots[d // 7] * 8 + d % 7] = 1.0
    spread_o = np.zeros((2, 448, 512), np.float32)
    for c in range(2):
        part = spread[448 * c:448 * c + 448].reshape(448, 16, 2, 32)
        spread_o[c] = part[:, :, c].reshape(448, 512)
    unpack = np.zeros((384, 304), np.float32)
    for a in range(8):
        for r in range(38):
            unpack[48 * a + r, 38 * a + r] = 1.0
    brow = np.full((2, 8, 640), -1, np.int32)
    for c in range(2):
        for i in range(576):
            if i < 448:
                nat = 448 * c + i
            elif i < 512:
                nat = 896 + 64 * c + i - 448
            else:
                nat = 1024 + 64 * c + i - 512
            brow[c, 0, i] = slots[nat // 9] * 8
            brow[c, 1, i] = nat % 9
    freq = THETA ** (-2.0 * (np.arange(128) % 32) / 64.0)
    freq = np.broadcast_to(freq.astype(np.float32), (8, 128))
    return (jnp.asarray(spread, BF), jnp.asarray(spread_o, BF), jnp.asarray(unpack.T, BF),
            jnp.asarray(unpack, BF), jnp.asarray(brow), jnp.asarray(freq))


def shards(tokens, segments, w_query, w_key, w_value, w_out, w_gate, w_up, w_down, gains, biases,
           cotangent):
    core = lax.axis_index("dp") % 2

    def pick(w, parts, c):
        cut = w.reshape(7, -1, 2, w.shape[1] // (2 * parts))
        return lax.dynamic_index_in_dim(cut, c, 2, keepdims=False).reshape(7, -1)

    small = jnp.concatenate(
        [gains, jnp.zeros((7, 14), BF), jnp.pad(biases[None], ((0, 6), (0, 0))),
         jnp.zeros((7, 39), BF)], axis=1)

    def build(c):
        g, u = pick(w_gate, 2, c), pick(w_up, 2, c)
        cols = [g[:, :768], u[:, :768], g[:, 768:1536], u[:, 768:1536],
                g[:, 1536:1792], g[:, 2304:], g[:, 1792:2304],
                u[:, 1536:1792], u[:, 2304:], u[:, 1792:2304],
                pick(w_query, 1, c), pick(w_key, 1, c), pick(w_value, 1, c), small, w_out]
        cols = jnp.concatenate(cols, axis=1)
        cols = lax.dynamic_update_slice(jnp.zeros((16, UNITS * 128), BF), cols, (8 * core, 0))
        return cols.reshape(16, UNITS, 128).transpose(1, 0, 2)

    pair = jnp.stack([build(core), build(1 - core)])
    down = jnp.pad(w_down, ((0, 10), (0, 0))).reshape(3, 16, 7, 128).transpose(2, 0, 1, 3)
    seg = jnp.pad(segments.reshape(2, 128).astype(F32), ((0, 6), (0, 0)))
    block_out, grad_in, own, sib = layer(
        pair, down.reshape(TALL, 16, 128), tokens.reshape(256, 896), cotangent.reshape(256, 896),
        seg, *constants())

    def lines(a):
        a = lax.dynamic_slice(a, (0, 8 * core, 0), (UNITS, 7, 128))
        return a.transpose(1, 0, 2).reshape(7, UNITS * 128).astype(F32)

    mine, theirs = lines(own[:UNITS]), lines(sib)
    zero, one = jnp.where(core == 0, mine, theirs), jnp.where(core == 0, theirs, mine)

    def columns(a, up):
        o = 128 * up
        return [a[:, 6 * o:6 * o + 768], a[:, 1536 + 6 * o:2304 + 6 * o]] + [
            a[:, 3072 + 7 * o:3072 + 7 * o + 896]]

    def whole(up):
        both = []
        for a in (zero, one):
            f0, f1, f2 = columns(a, up)
            f2 = jnp.concatenate([f2[:, :256], f2[:, 384:], f2[:, 256:384]], axis=1)
            both.append(jnp.concatenate([f0, f1, f2], axis=1).reshape(7, 2, 1216))
        return jnp.stack(both, axis=2).reshape(7, 4864)

    def halves(a, n):
        return jnp.concatenate([zero[:, a:a + n], one[:, a:a + n]], axis=1)

    q0 = 38 * 128
    both = mine[:, q0 + 576:] + theirs[:, q0 + 576:]
    grad_d = own[UNITS:].reshape(7, 48, 128)[:, :38].transpose(1, 0, 2).reshape(38, 896)
    return (
        block_out.reshape(tokens.shape), grad_in.reshape(tokens.shape),
        halves(q0, 448), halves(q0 + 448, 64), halves(q0 + 512, 64), both[:, 64:960],
        whole(0), whole(1), grad_d, both[:, :2], both[0, 16:25],
    )


def solution(mesh):
    row = P(AXES, None)
    batch = P(None, AXES, None, None)
    return jax.shard_map(
        shards, mesh=mesh,
        in_specs=(batch, P(None, AXES, None)) + (row,) * 8 + (P(AXES), batch),
        out_specs=(batch, batch) + (row,) * 8 + (P(AXES),),
        check_vma=False,
    )
```

time: 788 us -> 244 us (0.31); the launches traced: 774 us -> 244 us
  local copies, waits for them, and re-layouts: 470 us -> 20.3 us
  matrix products: 78.2 us -> 0 us
  Pallas kernels: 185 us -> 219 us
  other arithmetic: 35.2 us -> 3.82 us
    gather x518 -> x0, local copies, waits for them, and re-layouts: 366 us -> none
    dot_general x26 -> x0, matrix products: 75.3 us -> none  [the longest x12 35.5 us: dot(): return jnp.dot(a, b, preferred_element_type=F32, **kw)]
    pallas_call x2 -> x1, Pallas kernels: 185 us -> 219 us  [layer(): pl.pallas_call(layer_kernel, out_shape=(jax.ShapeDtypeStruct((256, 896),...]
    reshape x19 -> x14, local copies, waits for them, and re-layouts: 34.2 us -> 6.79 us  [the longest x5 4.38 us: pick(): cut = w.reshape(7, -1, 2, w.shape[1] // (2 * parts))]
    scatter x4 -> x0, local copies, waits for them, and re-layouts: 25 us -> none  [the longest x1 23.4 us: shards(): small.at[:, 0, 16:25].set(grad_bias.reshape(128, 9)[inverse])]
    unnamed x137 -> x31, local copies, waits for them, and re-layouts: 22.7 us -> 3.75 us
    another operation x13 -> x2, other arithmetic: 9.15 us -> 0.13 us  [whole(): return jnp.stack(both, axis=2).reshape(7, 4864)]
  transfers between devices with their start and end apart: 2 -> 0, of which waited for: 0 -> 0; matrix products, arithmetic and copies ran while one was open for 8% -> 0% of each run, Pallas kernels for 0% -> 0%
where the time goes in v2:
time: 244 us
  Pallas kernels  219 us (90%)
  local copies, waits for them, and re-layouts  20.3 us (8%)
  other arithmetic  3.82 us (2%)
    pallas_call x1, Pallas kernels, layer(): pl.pallas_call(layer_kernel, out_shape=(jax.ShapeDtypeStruct((256, 896),...  219 us

profile of v2, /device:TPU:1, one launch (start us, length us, event | category | flops | bytes accessed | tf_op | source)
XLA Modules:
  0.0 244.0 jit_solution(10443322146254816086)
XLA Ops:
  0.6 0.0 copy-start.4
  0.7 0.0 copy-start.3
  0.7 0.7 convert_bitcast_fusion.1
  1.4 0.7 pad.12
  2.1 0.8 copy.53
  2.8 0.6 pad.14.seg_own
  3.4 0.8 reshape.132
  4.2 0.8 reshape.134
  5.0 0.8 reshape.130
  5.9 1.0 reshape.126
  6.9 1.0 reshape.128
  7.9 1.0 dynamic-slice_reduce_fusion.2
  8.9 0.1 reshape.129
  9.1 0.1 reshape.138
  9.3 0.1 reshape.137
  9.4 0.0 copy-start.5
  9.5 0.8 concatenate.31
  10.3 0.1 reshape.127
  10.5 0.0 copy-done.4
  10.5 0.1 concatenate.30
  10.6 0.0 copy-done.3
  10.6 0.1 reshape.143
  10.7 0.7 copy.62
  11.4 0.5 dynamic_update_slice.7
  12.0 0.5 dynamic_update_slice.6
  12.6 0.8 pad_maximum_fusion.pair
  13.4 0.0 copy-done.5
  13.4 0.6 jit_solution_.3.freq
  14.0 218.7 %shard_map.257 = (bf16[256,896]{1,0:T(8,128)(2,1)}, bf16[256,896]{1,0:T(8,128)(2,1)}, f32[71,16,128]{2,1,0:T(8,128)}, bf16[50,16,128]{2,1,0:T(8,128)(2,1)}) custom-call(bf16[2,50,16,128]{3,2,1,0:T(8,128)(2,1)} %pad_maximum_fusion.pair, bf16[21,16,128]{2,1,0:T(8,128)(2,1)} %bitcast.81, bf16[256,896]{1,0:T(8,128)(2,1)} %bitcast.76, bf16[256,896]{1,0:T(8,128)(2,1)} %bitcast.77, ...), custom_call_target="tpu_custom_call" | custom-call | tf_op jit(solution)/shard_map/pallas_call | solution.py:589
  232.7 0.0 copy-start.2
  232.7 1.0 slice.228
  233.7 1.0 slice.198
  234.8 0.7 copy.83
  235.5 0.0 copy-done.2
  235.5 0.1 fusion.1
  235.6 0.0 copy-start.1
  235.6 0.1 slice_add_fusion
  235.7 0.6 slice_bitcast_fusion
  236.3 0.7 slice.260
  237.0 0.6 copy.69
  237.6 0.1 fusion.2
  237.7 0.1 fusion.3
  237.8 0.7 pad_maximum_fusion.5
  238.4 0.7 pad_maximum_fusion.4
  239.1 0.7 pad_maximum_fusion.3
  239.8 0.0 copy-start
  239.9 0.1 stack_reshape.14
  240.0 0.1 stack_reshape.12
  240.2 0.1 stack_reshape.15
  240.3 0.1 pad_maximum_fusion.2
  240.4 0.1 copy.65
  240.4 0.9 reshape.151
  241.3 0.1 stack_reshape.13
  241.4 0.1 pad_maximum_fusion.1
  241.5 0.1 copy.64
  241.6 0.9 reshape.150
  242.4 0.0 copy-done.1
  242.4 0.8 copy.120
  243.2 0.0 copy-done
  243.2 0.8 copy.121
  (48 shorter events, 0.4 us)
Async XLA Ops:
  0.6 9.8 %copy-start.4 = (bf16[7,896]{1,0:T(8,128)(2,1)S(1)}, bf16[7,896]{1,0:T(8,128)(2,1)}, u32[]{:S(2)}) copy-start(bf16[7,896]{1,0:T(8,128)(2,1)} %param.23) | copy-start | bytes 37636
  0.7 9.9 %copy-start.3 = (bf16[38,896]{1,0:T(8,128)(2,1)S(1)}, bf16[38,896]{1,0:T(8,128)(2,1)}, u32[]{:S(2)}) copy-start(bf16[38,896]{1,0:T(8,128)(2,1)} %param.26) | copy-start | bytes 204292
  9.4 4.0 %copy-start.5 = (f32[128]{0:T(128)S(1)}, f32[128]{0:T(128)}, u32[]{:S(2)}) copy-start(f32[128]{0:T(128)} %constant.77.clone) | copy-start | bytes 1540
  232.7 2.8 %copy-start.2 = (bf16[50,16,128]{2,1,0:T(8,128)(2,1)S(1)}, bf16[50,16,128]{2,1,0:T(8,128)(2,1)}, u32[]{:S(2)}) copy-start(bf16[50,16,128]{2,1,0:T(8,128)(2,1)} %get-tuple-element.18) | copy-start | bytes 614404
  235.6 6.9 %copy-start.1 = (bf16[256,896]{1,0:T(8,128)(2,1)S(1)}, bf16[256,896]{1,0:T(8,128)(2,1)}, u32[]{:S(2)}) copy-start(bf16[256,896]{1,0:T(8,128)(2,1)} %get-tuple-element.15) | copy-start | bytes 1376260
  239.8 3.4 %copy-start = (bf16[256,896]{1,0:T(8,128)(2,1)S(1)}, bf16[256,896]{1,0:T(8,128)(2,1)}, u32[]{:S(2)}) copy-start(bf16[256,896]{1,0:T(8,128)(2,1)} %get-tuple-element.16) | copy-start | bytes 1376260

commit v3 on v2

v3 whole, which is shorter than its diff:
```python
import functools

import jax
import jax.numpy as jnp
import numpy as np
from jax import lax
from jax.experimental import pallas as pl
from jax.experimental.pallas import tpu as pltpu
from jax.sharding import PartitionSpec as P

EPSILON = 1e-06
THETA = 1000000.0
NEG_FILL = -1e30
MESH = pl.DeviceIdType.MESH
AXES = ("dp", "fsdp")
BF = jnp.bfloat16
F32 = jnp.float32
GRAY = (0, 1, 3, 2)

BULK = ((0, 8), (8, 8), (16, 7), (23, 8), (31, 7), (38, 7))
TALLS = ((0, 4), (4, 3), (7, 4), (11, 3), (14, 4), (18, 3))
WAVES = (
    ((7, 1), (14, 2), (22, 1), (30, 1), (37, 1), (44, 1)),
    TALLS,
    ((0, 2), (8, 2), (16, 2), (23, 2), (31, 2), (38, 2)),
    ((2, 2), (10, 2), (18, 2), (25, 2), (33, 2), (40, 2)),
    ((4, 3), (12, 2), (20, 2), (27, 3), (35, 2), (42, 2)),
)
EARLY = ((0, 4), (8, 4), (16, 4), (23, 4), (31, 4), (38, 4))
LATE = ((4, 4), (12, 4), (20, 3), (27, 4), (35, 3), (42, 3))
OUT, DOWN, FFN = 0, 1, 2
OUT_UNITS = (7, 14, 15, 22, 30, 37, 44)
HEAD = ((45, 2), (47, 2), (49, 1))
UNITS, TALL, QKV = 50, 21, 45


def pair_units(starts, last):
    return tuple(starts[j % 6 // 2] + 2 * (j // 6) + j % 2 for j in range(18)) + (last,)


GATE_UNITS = pair_units((0, 8, 16), 6)
UP_UNITS = pair_units((23, 31, 38), 29)
GATE_AT, UP_AT, Q_AT, K_AT, V_AT, O_AT, S_AT, RAW = (
    0, 4864, 9728, 10624, 10752, 10880, 11776, 11904)
ORDER = tuple(
    tuple(2 * ((p % 3 + k // 2) % 3) + ((k % 2) ^ (p // 3)) for k in range(6)) for p in range(6)
)


def here():
    dp = lax.axis_index("dp")
    fs = lax.axis_index("fsdp")
    return (fs // 4) % 4, fs % 4, (dp // 2) * 2 + fs // 16, dp % 2


def device(x, y, z, core):
    return ((z // 2) * 2 + core, (z % 2) * 16 + x * 4 + y)


def gray_bits(v):
    high = v // 2
    low = (v % 2 + high) % 2
    return low, high


def flip(v, bit):
    if bit == 0:
        return v + 1 - 2 * (v % 2)
    return 3 - v


def partner(bit):
    x, y, z, core = here()
    axis, low = bit // 2, bit % 2
    place = [x, y, z]
    place[axis] = flip(place[axis], low)
    return device(*place, core)


def sibling():
    x, y, z, core = here()
    return device(x, y, z, 1 - core)


def my_bits():
    x, y, z, _ = here()
    bits = []
    for v in (x, y, z):
        low, high = gray_bits(v)
        bits += [low, high]
    return bits


DIMS = (1, 0, 3, 2, 5, 4)


def slot(bits, full):
    return tuple(slice(None) if b in full else bits[b] for b in DIMS)


def far(axis):
    x, y, z, core = here()
    place = [x, y, z]
    place[axis] = 3 - flip(place[axis], 0)
    return device(*place, core)


def dot(a, b):
    return lax.dot_general(a, b, (((1,), (0,)), ((), ())), preferred_element_type=F32)


def dot_t(a, b):
    return lax.dot_general(a, b, (((1,), (1,)), ((), ())), preferred_element_type=F32)


def layer_kernel(
    w_query, w_key, w_value, w_out_, w_gate, w_up, w_down, gains, biases, segments,
    x_own, e_own, spread_h, spread_o_h, pack_h, unpack_h, brow, freq,
    out_ref, gtok_ref, own_ref, sib_ref,
    u_buf, t_buf, u_got, t_got, wd, x_all, e_all, seg_all, stage, a1s, a2s, a2st, qkv, o_s,
    y1, ypart, yrec, da2, darec, mrec, arec, cosine, sine, gain, bias, slab,
    raw, last_rows, own_s, send_s, seg_own, spread, spread_o, pack, unpack,
    h_got0, h_got1, h_got2, ag_small_recv, rs_small_recv, small_send, ag_big_recv, rs_big_recv,
    big_send, ag_head_recv, rs_head_recv, head_send, credit, sib_send, sib_recv, loc_sem,
):
    _, _, _, core = here()
    bits = my_bits()
    flipped = [1 - b for b in bits]
    sib = sibling()
    peers = [partner(b) for b in range(6)]
    across_ = [far(a) for a in range(3)]

    barrier = pltpu.get_barrier_semaphore()
    for d in peers + across_ + [sib]:
        pl.semaphore_signal(barrier, inc=1, device_id=d, device_id_type=MESH)

    def to_sibling(src, dst, i):
        return pltpu.make_async_remote_copy(
            src_ref=src, dst_ref=dst, send_sem=sib_send.at[i], recv_sem=sib_recv.at[i],
            device_id=sib, device_id_type=MESH)

    own = pl.ds(pl.multiple_of(core * 256, 256), 256)
    locals_ = [
        pltpu.make_async_copy(a, b, loc_sem.at[i]) for i, (a, b) in enumerate((
            (x_own, x_all.at[own]), (e_own, e_all.at[own]), (spread_h, spread),
            (spread_o_h, spread_o), (pack_h, pack), (unpack_h, unpack)))]
    for c in locals_:
        c.start()

    raw[...] = jnp.zeros((8, RAW), F32)
    for ref, a in ((w_gate, GATE_AT), (w_up, UP_AT), (w_query, Q_AT), (w_key, K_AT),
                   (w_value, V_AT), (w_out_, O_AT), (gains, S_AT)):
        raw[0:7, a:a + ref.shape[1]] = ref[...].astype(F32)
    raw[0:1, S_AT + 16:S_AT + 25] = biases[...].astype(F32)
    seg_own[...] = jnp.zeros((8, 128), F32)
    seg_own[0:2, :] = segments[...].astype(F32)
    last_rows[...] = jnp.zeros((16, 896), F32)
    last_rows[0:6, :] = w_down[32:38, :].astype(F32)

    def lanes(first, second):
        if second == first + 64:
            return raw[:, first:first + 128]
        return jnp.concatenate([raw[:, first:first + 64], raw[:, second:second + 64]], axis=1)

    def hidden_at(base, c, h):
        return base + 1216 * (2 * (h // 19) + c) + 64 * (h % 19)

    def head_at(c, h):
        return (Q_AT + 448 * c + 64 * h, K_AT + 64 * c, V_AT + 64 * c, S_AT)[max(0, h - 6)]

    def units_of(c):
        for table, base in ((GATE_UNITS, GATE_AT), (UP_UNITS, UP_AT)):
            for j, place in enumerate(table):
                yield place, lanes(hidden_at(base, c, 2 * j), hidden_at(base, c, 2 * j + 1))
        for j in range(5):
            yield QKV + j, lanes(head_at(c, 2 * j), head_at(c, 2 * j + 1))
        for j, place in enumerate(OUT_UNITS):
            yield place, raw[:, O_AT + 128 * j:O_AT + 128 * j + 128]

    def fill(dst, other):
        for c in range(2):
            @pl.when(core == c)
            def _():
                zero = jnp.zeros((8, 128), F32)
                for place, v in units_of(1 - c if other else c):
                    tile = jnp.concatenate([zero, v] if c else [v, zero], axis=0)
                    dst[place] = tile.astype(BF)

    fill(send_s, True)
    pl.semaphore_wait(barrier, 10)
    swap_pair = to_sibling(send_s, stage, 0)
    swap_pair.start()
    swap_seg = to_sibling(seg_own, seg_all.at[core], 1)
    swap_x = to_sibling(x_own, x_all.at[own], 2)
    swap_e = to_sibling(e_own, e_all.at[own], 3)
    for c in (swap_seg, swap_x, swap_e):
        c.start()
    fill(own_s, False)
    seg_all[core] = seg_own[...]

    def remote(src, dst, send, recv, to):
        return pltpu.make_async_remote_copy(
            src_ref=src, dst_ref=dst, send_sem=send, recv_sem=recv, device_id=to,
            device_id_type=MESH)

    BOTH = ((u_buf, BULK), (t_buf, TALLS))

    def bufs(w):
        return (t_buf, t_got) if w == DOWN else (u_buf, u_got)

    def small_copy(k, p, i):
        buf, parts = BOTH[i]
        ref = buf.at[(pl.ds(*parts[p]),) + slot(bits, ORDER[p][:k])]
        return remote(ref, ref, small_send.at[k, p, i], ag_small_recv.at[k, p, i],
                      peers[ORDER[p][k]])

    def ag_small(k):
        for i in range(2):
            for p in range(6):
                if k > 0:
                    small_copy(k - 1, p, i).wait_recv()
                small_copy(k, p, i).start()

    def ag_small_end():
        for i in range(2):
            for p in range(6):
                small_copy(3, p, i).wait_recv()
        for i in range(2):
            for p in range(6):
                for k in range(4):
                    small_copy(k, p, i).wait_send()

    def ag_copy(w, k, p):
        order = ORDER[p]
        ref = bufs(w)[0].at[(pl.ds(*WAVES[w][p]),) + slot(bits, order[:k])]
        return remote(ref, ref, big_send.at[w, k - 4, p], ag_big_recv.at[w, k - 4, p],
                      peers[order[k]])

    def ag(w, k):
        for p in range(6):
            if k == 5:
                ag_copy(w, 4, p).wait_recv()
            ag_copy(w, k, p).start()

    def ag_done(w):
        for p in range(6):
            ag_copy(w, 5, p).wait_recv()
        for p in range(6):
            for k in (4, 5):
                ag_copy(w, k, p).wait_send()

    def given(k, p, *more):
        b = list(bits)
        for j in (k,) + more:
            b[ORDER[p][j]] = flipped[ORDER[p][j]]
        return slot(b, ORDER[p][:k])

    def rs_copy(w, k, p):
        acc, got = bufs(w)
        units = pl.ds(*WAVES[w][p])
        dst = got.at[units]
        if k < 5:
            b = list(bits)
            b[ORDER[p][5]] = flipped[ORDER[p][5]]
            dst = acc.at[(units,) + slot(b, ORDER[p][:k])]
        return remote(acc.at[(units,) + given(k, p)], dst, big_send.at[w, k - 4, p],
                      rs_big_recv.at[w, k - 4, p], peers[ORDER[p][k]])

    def rs_add(acc, got, part, k, p):
        start, n = part
        mine_ = slot(bits, ORDER[p][:k])

        def one(u):
            add = got[u] if k == 5 else acc[(u,) + given(k, p, 5)]
            acc[(u,) + mine_] = acc[(u,) + mine_] + add

        if k >= 2:
            @pl.loop(0, n)
            def _(i):
                one(start + i)
        else:
            for i in range(n):
                one(start + i)

    def rs(w, k):
        acc, got = bufs(w)
        if k == 4:
            for p in range(6):
                rs_copy(w, 5, p).wait_send()
            for b in range(6):
                pl.semaphore_signal(credit.at[w, b], inc=1, device_id=peers[b],
                                    device_id_type=MESH)
        for p in range(6):
            if k == 4:
                rs_copy(w, 5, p).wait_recv()
                rs_add(acc, got, WAVES[w][p], 5, p)
                pl.semaphore_wait(credit.at[w, ORDER[p][4]], 1)
            rs_copy(w, k, p).start()

    def rs_fold(w):
        acc, got = bufs(w)
        for p in range(6):
            rs_copy(w, 4, p).wait_recv()
            rs_add(acc, got, WAVES[w][p], 4, p)

    GROUPS = (((u_buf, EARLY),), ((u_buf, LATE), (t_buf, TALLS)))

    def rs_small_copy(g, k, p, i):
        buf, parts = GROUPS[g][i]
        units = pl.ds(*parts[p])
        b = list(bits)
        b[ORDER[p][5]] = flipped[ORDER[p][5]]
        return remote(buf.at[(units,) + given(k, p)], buf.at[(units,) + slot(b, ORDER[p][:k])],
                      small_send.at[k, p, g + i], rs_small_recv.at[k, p, g + i],
                      peers[ORDER[p][k]])

    def rs_small(g, k):
        if k == 3:
            for b in range(6):
                pl.semaphore_signal(credit.at[5 + g, b], inc=1, device_id=peers[b],
                                    device_id_type=MESH)
        for i in range(len(GROUPS[g])):
            for p in range(6):
                if k == 3:
                    if i == 0:
                        pl.semaphore_wait(credit.at[5 + g, ORDER[p][3]], 1)
                else:
                    rs_small_copy(g, k + 1, p, i).wait_recv()
                    rs_add(GROUPS[g][i][0], None, GROUPS[g][i][1][p], k + 1, p)
                rs_small_copy(g, k, p, i).start()

    def rs_small_end(g):
        for i, (buf, parts) in enumerate(GROUPS[g]):
            for p in range(6):
                start, n = parts[p]
                units = pl.ds(start, n)
                rs_small_copy(g, 0, p, i).wait_recv()
                total = (buf[(units,) + slot(bits, ())].astype(F32)
                         + buf[(units,) + given(0, p, 5)].astype(F32))
                own_ref[pl.ds(start + i * UNITS, n)] = total
                if i == 0:
                    slab[units] = total.astype(BF)

    def rs_sent():
        for p in range(6):
            for w in range(5):
                rs_copy(w, 4, p).wait_send()
            for g, i in ((0, 0), (1, 0), (1, 1)):
                for k in range(4):
                    rs_small_copy(g, k, p, i).wait_send()

    def turned_bits(axis, j):
        b = list(bits)
        for i in ((0,), (1,), (0, 1))[j]:
            b[2 * axis + i] = flipped[2 * axis + i]
        return b

    def head_to(axis, j):
        return across_[axis] if j == 2 else peers[2 * axis + j]

    def head_full(r, stage):
        return [2 * ((r + i) % 3) + j for i in range(stage) for j in range(2)]

    def head_copy(stage, r, j):
        ref = u_buf.at[(pl.ds(*HEAD[r]),) + slot(bits, head_full(r, stage))]
        return remote(ref, ref, head_send.at[stage, r, j], ag_head_recv.at[stage, r, j],
                      head_to((r + stage) % 3, j))

    def ag_head(stage):
        for r in range(3):
            for j in range(3):
                if stage > 0:
                    head_copy(stage - 1, r, j).wait_recv()
            for j in range(3):
                head_copy(stage, r, j).start()

    def ag_head_done():
        for r in range(3):
            for j in range(3):
                head_copy(2, r, j).wait_recv()
        for r in range(3):
            for j in range(3):
                for stage in range(3):
                    head_copy(stage, r, j).wait_send()

    def head_rs_copy(stage, r, j):
        start, n = HEAD[r]
        axis = (r + stage) % 3
        src = u_buf.at[(pl.ds(start, n),) + slot(turned_bits(axis, j), head_full(r, stage))]
        dst = (h_got0, h_got1, h_got2)[stage].at[j, pl.ds(start - QKV, n)]
        return remote(src, dst, head_send.at[stage, r, j], rs_head_recv.at[stage, r, j],
                      head_to(axis, j))

    def head_sum(stage, r):
        start, n = HEAD[r]
        for j in range(3):
            head_rs_copy(stage, r, j).wait_recv()
        got = (h_got0, h_got1, h_got2)[stage]
        totals = []
        for i in range(n):
            at = (start + i,) + slot(bits, head_full(r, stage))
            total = u_buf[at].astype(F32)
            for j in range(3):
                total = total + got[j, start + i - QKV].astype(F32)
            if stage:
                u_buf[at] = total.astype(BF)
            else:
                own_ref[start + i] = total
                slab[start + i] = total.astype(BF)

    def rs_head(stage):
        for r in range(3):
            if stage < 2:
                head_sum(stage + 1, r)
            for j in range(3):
                head_rs_copy(stage, r, j).start()

    def rs_head_end():
        for r in range(3):
            head_sum(0, r)
        for r in range(3):
            for j in range(3):
                for stage in range(3):
                    head_rs_copy(stage, r, j).wait_send()

    def last_swap(i):
        at = pl.ds(0, QKV) if i == 0 else pl.ds(QKV, UNITS - QKV)
        return to_sibling(slab.at[at], sib_ref.at[at], 16 + i)

    def rows(s):
        return pl.ds(pl.multiple_of(s * 128, 128), 128)

    def unit(u):
        return u_buf[u].reshape(1024, 128)

    mine = slot(bits, ())
    for c in range(7):
        cols = slice(128 * c, 128 * c + 128)
        for r in range(2):
            t_buf[(3 * c + r,) + mine] = w_down[16 * r:16 * r + 16, cols]
        t_buf[(3 * c + 2,) + mine] = last_rows[:, cols].astype(BF)
    swap_pair.wait()
    u_buf[(slice(None),) + mine] = own_s[...] + stage[...]
    ag_head(0)
    ag_small(0)
    ag_head(1)
    ag_small(1)
    ag_head(2)
    for c in locals_:
        c.wait()
    for c in (swap_seg, swap_x, swap_e):
        c.wait()
    ag_small(2)

    causal = (lax.broadcasted_iota(jnp.int32, (128, 128), 1)
              <= lax.broadcasted_iota(jnp.int32, (128, 128), 0))

    def allowed(s):
        line = seg_all[s // 2, pl.ds(s % 2, 1), :]
        across = jnp.broadcast_to(line, (128, 128))
        return jnp.logical_and(causal, across == across.T)

    for s in range(4):
        place = jnp.sum(allowed(s).astype(F32), axis=1, keepdims=True) - 1.0
        angle = place * freq[0:1, :]
        cosine[rows(s), :] = jnp.cos(angle)
        sine[rows(s), :] = jnp.sin(angle)
    ag_small(3)
    ag_head_done()

    small = unit(49).T
    gain[...] = dot_t(small[64:80], spread[...])[0:8]
    hit = (lax.broadcasted_iota(jnp.int32, (1024, 640), 0) == brow[core, 0:1, :]).astype(BF)
    picked = dot(small[80:96], hit)
    choose = lax.broadcasted_iota(jnp.int32, (16, 640), 0) == brow[core, 1:2, :]
    bias[...] = jnp.broadcast_to(
        jnp.sum(jnp.where(choose, picked, 0.0), axis=0, keepdims=True), (8, 640))

    def inv_root(v):
        return lax.rsqrt(jnp.mean(v * v, axis=-1, keepdims=True) + EPSILON)

    @pl.loop(0, 4)
    def _(s):
        v = x_all[rows(s), :].astype(F32)
        a1 = (v * inv_root(v) * gain[0:1, :]).astype(BF)
        a1s[rows(s), :] = dot(a1, spread[...]).astype(BF)

    ag_small_end()
    ag(OUT, 4)
    ag(DOWN, 4)
    lane = lax.broadcasted_iota(jnp.int32, (128, 640), 1)
    first = lane % 64 < 32
    turns = lane < 512

    def wide(ref, s):
        return jnp.concatenate([ref[rows(s), :]] * 5, axis=1)

    w_qkv = jnp.concatenate([unit(QKV + i) for i in range(5)], axis=1)
    for s in range(4):
        raw = dot(a1s[rows(s), :], w_qkv) + bias[0:1, :]
        turned = jnp.where(first, -pltpu.roll(raw, 608, 1), pltpu.roll(raw, 32, 1))
        turned = raw * wide(cosine, s) + turned * wide(sine, s)
        qkv[rows(s), :] = jnp.where(turns, turned, raw).astype(BF)
    ag(OUT, 5)
    ag(FFN, 4)
    ag_done(OUT)
    ag(DOWN, 5)

    def heads(v):
        return jnp.concatenate([v[:, 64 * h:64 * h + 64] for h in range(7)], axis=0)

    def unheads(v):
        return jnp.concatenate([v[128 * h:128 * h + 128, :] for h in range(7)], axis=1)

    def attend(s):
        q7 = heads(qkv[rows(s), 0:448])
        k = qkv[rows(s), 448:512]
        v = qkv[rows(s), 512:576]
        score = dot_t(q7, k) * 0.125
        ok = allowed(s)
        score = jnp.where(jnp.concatenate([ok] * 7, axis=0), score, NEG_FILL)
        e = jnp.exp(score - jnp.max(score, axis=-1, keepdims=True))
        soft = e / jnp.sum(e, axis=-1, keepdims=True)
        return q7, k, v, soft

    def w_out():
        return jnp.concatenate(
            [u_buf[OUT_UNITS[i], :, :, :, :, core].reshape(512, 128) for i in range(7)], axis=1)

    def y_swap(s):
        return to_sibling(ypart.at[rows(s)], yrec.at[rows(s)], 4 + s)

    def tick(now, t, *acts):
        @pl.when(now == t)
        def _():
            for f, a in acts:
                f(*a)

    @pl.loop(0, 4)
    def _(s):
        tick(s, 1, (ag, (FFN, 5)))
        tick(s, 2, (ag, (FFN + 1, 4)))
        tick(s, 3, (ag, (FFN + 1, 5)))
        _, _, v, soft = attend(s)
        o = unheads(dot(soft.astype(BF), v)).astype(BF)
        os = dot(o, spread_o[core]).astype(BF)
        o_s[rows(s), :] = os
        ypart[rows(s), :] = dot(os, w_out())
        y_swap(s).start()

    ag_done(DOWN)
    ag(FFN + 2, 4)

    def slab_place(s):
        z, x, y = s // 16, s // 4 % 4, s % 4
        b = []
        for v in (x, y, z):
            low, high = gray_bits(v)
            b += [low, high]
        return slot(b, ())

    @pl.loop(0, 8)
    def _(g):
        lines = []
        for i in range(8):
            at = slab_place(g * 8 + i)
            for r in range(3):
                lines.append(jnp.concatenate(
                    [t_buf[(3 * c + r,) + at] for c in range(7)], axis=1))
        block = jnp.concatenate(lines, axis=0)
        wd[pl.ds(pl.multiple_of(g * 304, 16), 304), :] = dot(pack[...], block).astype(BF)

    ag(FFN + 2, 5)

    @pl.loop(0, 4)
    def _(s):
        y_swap(s).wait()
        v = x_all[rows(s), :].astype(F32) + (ypart[rows(s), :] + yrec[rows(s), :])
        y1[rows(s), :] = v
        a2 = (v * inv_root(v) * gain[1:2, :]).astype(BF)
        a2s[rows(s), :] = dot(a2, spread[...]).astype(BF)
        ypart[rows(s), :] = jnp.zeros((128, 896), F32)
        da2[rows(s), :] = jnp.zeros((128, 1024), F32)

    a2st[...] = a2s[...].T

    def ffn(gates, ups, row, n):
        width = 128 * n
        w = jnp.concatenate([unit(i) for i in gates + ups], axis=1)
        both = dot(a2s[...], w)
        g, u = both[:, :width], both[:, width:]
        at = pl.ds(pl.multiple_of(row, 128), width)
        w_d = wd[at, :]
        dm = dot_t(e_all[...], w_d)
        sig = 1.0 / (1.0 + jnp.exp(-g))
        silu = g * sig
        m = (silu * u).astype(BF)
        dg = (dm * u * sig * (1.0 + g * (1.0 - sig))).astype(BF)
        du = (dm * silu).astype(BF)
        dgu = jnp.concatenate([dg, du], axis=1)
        ypart[...] += dot(m, w_d)
        da2[...] += dot_t(dgu, w)
        wd[at, :] = dot(m.T, e_all[...]).astype(BF)
        for part, places in ((dg, gates), (du, ups)):
            grads = dot(a2st[...], part).astype(BF)
            for i, place in enumerate(places):
                u_buf[place] = grads[:, 128 * i:128 * i + 128].reshape((2,) * 6 + (16, 128))

    ag_done(FFN)

    @pl.loop(0, 9)
    def _(i):
        tick(i, 3, (rs, (FFN, 5)), (ag_done, (FFN + 1,)))
        tick(i, 6, (rs, (FFN + 1, 5)), (ag_done, (FFN + 2,)))
        tick(i, 7, (rs, (FFN, 4)))
        wave, q = i // 3, i % 3
        g = 8 * q + 2 * wave
        u = 23 + 8 * q - q // 2 + 2 * wave
        ffn([g, g + 1], [u, u + 1], i * 256, 2)

    ffn([6], [29], 2304, 1)
    rs(FFN + 2, 5)

    other = pl.ds(pl.multiple_of((1 - core) * 256, 256), 256)
    out_swap = to_sibling(ypart.at[other], mrec, 8)
    out_swap.start()

    def unspread(v):
        high = v.astype(BF)
        low = (v - high.astype(F32)).astype(BF)
        return dot_t(high, spread[...]) + dot_t(low, spread[...])

    def da_swap(s):
        return to_sibling(yrec.at[rows(s)], darec.at[rows(s)], 9 + s)

    @pl.loop(0, 4)
    def _(s):
        yrec[rows(s), :] = unspread(da2[rows(s), :])
        da_swap(s).start()

    rs(FFN + 1, 4)

    @pl.loop(0, 8)
    def _(g):
        block = dot(unpack[...], wd[pl.ds(pl.multiple_of(g * 304, 16), 304), :]).astype(BF)
        for i in range(8):
            at = slab_place(g * 8 + i)
            for r in range(3):
                for c in range(7):
                    t_buf[(3 * c + r,) + at] = block[48 * i + 16 * r:48 * i + 16 * r + 16,
                                                     128 * c:128 * c + 128]

    rs(DOWN, 5)
    rs_fold(FFN)
    out_swap.wait()
    for s in range(2):
        at = pl.ds(pl.multiple_of(core * 256 + 128 * s, 128), 128)
        out_ref[pl.ds(128 * s, 128), :] = (
            y1[at, :] + (ypart[at, :] + mrec[pl.ds(128 * s, 128), :])).astype(BF)

    rs(FFN + 2, 4)

    gain_grads = gain.at[pl.ds(2, 2)]
    gain_grads[...] = jnp.zeros((2, 896), F32)

    @pl.loop(0, 4)
    def _(s):
        da_swap(s).wait()
        da = yrec[rows(s), :] + darec[rows(s), :]
        v = y1[rows(s), :]
        r = inv_root(v)

        @pl.when(s // 2 == core)
        def _():
            gain[3:4, :] += jnp.sum(da * v * r, axis=0, keepdims=True)

        w = da * gain[1:2, :]
        dy = (e_all[rows(s), :].astype(F32) + r * w
              - v * (r * r * r) * jnp.mean(w * v, axis=-1, keepdims=True))
        darec[rows(s), :] = dy
        f = dy.astype(BF)
        a2s[rows(s), 0:896] = f
        ds_ = dot_t(f, w_out()).astype(BF)
        a2s[rows(s), 896:1024] = jnp.zeros((128, 128), BF)
        a2st[rows(s), 0:448] = dot_t(ds_, spread_o[core]).astype(BF)

    rs_fold(FFN + 1)
    rs_small(0, 3)
    o_grad = dot(o_s[...].T, a2s[:, 0:896]).astype(BF)
    for i in range(7):
        part = o_grad[:, 128 * i:128 * i + 128].reshape((2,) * 5 + (16, 128))
        u_buf[OUT_UNITS[i], :, :, :, :, core] = part
        u_buf[OUT_UNITS[i], :, :, :, :, 1 - core] = jnp.zeros_like(part)
    rs(OUT, 5)
    rs_small(0, 2)
    rs(DOWN, 4)

    bias[...] = jnp.zeros((8, 640), F32)

    @pl.loop(0, 4)
    def _(s):
        tick(s, 1, (rs_small, (0, 1)), (rs_fold, (FFN + 2,)))
        tick(s, 2, (rs, (OUT, 4)), (rs_small, (0, 0)))
        tick(s, 3, (rs_fold, (DOWN,)))
        q7, k, v, soft = attend(s)
        do7 = heads(a2st[rows(s), 0:448])
        dp = dot_t(do7, v)
        ds_ = (soft * (dp - jnp.sum(soft * dp, axis=-1, keepdims=True))).astype(BF)
        dq = unheads(dot(ds_, k)) * 0.125
        dk = dot(ds_.T, q7) * 0.125
        dv = dot(soft.astype(BF).T, do7)
        raw = jnp.concatenate([dq, dk, dv, jnp.zeros((128, 64), F32)], axis=1)
        scaled = raw * wide(sine, s)
        turned = jnp.where(first, pltpu.roll(scaled, 608, 1), -pltpu.roll(scaled, 32, 1))
        grad = jnp.where(turns, raw * wide(cosine, s) + turned, raw).astype(BF)
        qkv[rows(s), :] = grad
        bias[0:1, :] += jnp.sum(grad.astype(F32), axis=0, keepdims=True)

    rs_fold(OUT)
    rs_small(1, 3)
    w_qkv = jnp.concatenate([unit(QKV + i) for i in range(5)], axis=1)
    da2[...] = dot_t(qkv[...], w_qkv)

    @pl.loop(0, 4)
    def _(s):
        yrec[rows(s), :] = unspread(da2[rows(s), :])

    a_swap = to_sibling(yrec.at[other], arec, 13)
    a_swap.start()
    rs_small(1, 2)
    a2st[...] = a1s[...].T
    for i in range(4):
        part = dot(a2st[...], qkv[:, 128 * i:128 * i + 128])
        u_buf[QKV + i] = part.astype(BF).reshape((2,) * 6 + (16, 128))
    a_swap.wait()
    for s in range(2):
        at = pl.ds(pl.multiple_of(core * 256 + 128 * s, 128), 128)
        da = yrec[at, :] + arec[pl.ds(128 * s, 128), :]
        v = x_all[at, :].astype(F32)
        r = inv_root(v)
        gain[2:3, :] += jnp.sum(da * v * r, axis=0, keepdims=True)
        w = da * gain[0:1, :]
        gtok_ref[pl.ds(128 * s, 128), :] = (
            darec[at, :] + r * w
            - v * (r * r * r) * jnp.mean(w * v, axis=-1, keepdims=True)).astype(BF)
    top = dot(jnp.concatenate([gain[2:4, :], jnp.zeros((14, 896), F32)], axis=0).astype(BF),
              spread[...])
    spot = jnp.where(choose, jnp.broadcast_to(bias[0:1, :], (16, 640)), 0.0).astype(BF)
    hit = (lax.broadcasted_iota(jnp.int32, (1024, 640), 0) == brow[core, 0:1, :]).astype(BF)
    low = dot_t(spot, hit)
    small = jnp.concatenate(
        [jnp.zeros((64, 1024), F32), top, low, jnp.zeros((32, 1024), F32)], axis=0).T
    part = dot(a2st[...], qkv[:, 512:640]) + small
    u_buf[49] = part.astype(BF).reshape((2,) * 6 + (16, 128))
    rs_head(2)
    rs_small(1, 1)
    rs_small_end(0)
    rs_head(1)
    rs_small(1, 0)
    rs_head(0)
    rs_small_end(1)
    last_swap(0).start()
    rs_head_end()
    last_swap(1).start()
    rs_sent()
    for i in range(2):
        last_swap(i).wait()


def layer(*arrays):
    dma = pltpu.SemaphoreType.DMA
    vm = pltpu.VMEM
    return pl.pallas_call(
        layer_kernel,
        out_shape=(
            jax.ShapeDtypeStruct((256, 896), BF),
            jax.ShapeDtypeStruct((256, 896), BF),
            jax.ShapeDtypeStruct((UNITS + TALL, 16, 128), F32),
            jax.ShapeDtypeStruct((UNITS, 16, 128), BF),
        ),
        in_specs=[pl.BlockSpec(memory_space=vm)] * 10 + [pl.BlockSpec(memory_space=pl.ANY)] * 6
        + [pl.BlockSpec(memory_space=vm)] * 2,
        out_specs=[pl.BlockSpec(memory_space=vm)] * 4,
        scratch_shapes=[
            vm((UNITS,) + (2,) * 6 + (16, 128), BF), vm((TALL,) + (2,) * 6 + (16, 128), BF),
            vm((QKV,) + (2,) * 5 + (16, 128), BF), vm((TALL,) + (2,) * 5 + (16, 128), BF),
            vm((2432, 896), BF), vm((512, 896), BF), vm((512, 896), BF), vm((2, 8, 128), F32),
            vm((UNITS, 16, 128), BF), vm((512, 1024), BF), vm((512, 1024), BF),
            vm((1024, 512), BF), vm((512, 640), BF), vm((512, 512), BF),
            vm((512, 896), F32), vm((512, 896), F32), vm((512, 896), F32), vm((512, 1024), F32),
            vm((512, 896), F32), vm((256, 896), F32), vm((256, 896), F32), vm((512, 128), F32), vm((512, 128), F32),
            vm((8, 896), F32), vm((8, 640), F32), vm((UNITS, 16, 128), BF),
            vm((8, RAW), F32), vm((16, 896), F32), vm((UNITS, 16, 128), BF),
            vm((UNITS, 16, 128), BF), vm((8, 128), F32), vm((896, 1024), BF), vm((2, 448, 512), BF),
            vm((304, 384), BF), vm((384, 304), BF),
            vm((3, 5, 16, 128), BF), vm((3, 5) + (2,) * 2 + (16, 128), BF),
            vm((3, 5) + (2,) * 4 + (16, 128), BF),
            dma((4, 6, 2)), dma((4, 6, 3)), dma((4, 6, 3)), dma((5, 2, 6)), dma((5, 2, 6)),
            dma((5, 2, 6)), dma((3, 3, 3)), dma((3, 3, 3)), dma((3, 3, 3)),
            pltpu.SemaphoreType.REGULAR((7, 6)),
            dma((21,)), dma((21,)), dma((6,)),
        ],
        compiler_params=pltpu.CompilerParams(collective_id=0, has_side_effects=True,
                                             vmem_limit_bytes=60 * 2**20),
    )(*arrays)


def finish_kernel(own, sib, out, tok, out_ref, tok_ref, q_ref, k_ref, v_ref, o_ref, g_ref, u_ref,
                  d_ref, gain_ref, bias_ref):
    out_ref[...] = out[...]
    tok_ref[...] = tok[...]
    for c in range(7):
        for r in range(3):
            n = 16 if r < 2 else 6
            d_ref[16 * r:16 * r + n, 128 * c:128 * c + 128] = own[UNITS + 3 * c + r][0:n]
    core = lax.axis_index("dp") % 2
    for c in range(2):
        @pl.when(core == c)
        def _():
            def mine(u):
                return own[u, 8 * c:8 * c + 8, :]

            def theirs(u):
                return sib[u].astype(F32)[8 * c:8 * c + 8]

            def half(plane, u, h):
                return (mine if plane == c else theirs)(u)[:, 64 * h:64 * h + 64]

            def put(ref, count, where):
                for n in range(count):
                    (p0, u0, h0), (p1, u1, h1) = where(2 * n), where(2 * n + 1)
                    if (p0, u0, h0, h1) == (p1, u1, 0, 1):
                        v = (mine if p0 == c else theirs)(u0)
                    else:
                        v = jnp.concatenate([half(p0, u0, h0), half(p1, u1, h1)], axis=1)
                    ref[:, 128 * n:128 * n + 128] = v[0:7]

            def hidden(table):
                def where(h):
                    t = h // 38 * 19 + h % 19
                    return h // 19 % 2, table[t // 2], t % 2
                return where

            put(g_ref, 38, hidden(GATE_UNITS))
            put(u_ref, 38, hidden(UP_UNITS))
            put(q_ref, 7, lambda h: (h // 7, QKV + h % 7 // 2, h % 7 % 2))
            put(k_ref, 1, lambda h: (h, QKV + 3, 1))
            put(v_ref, 1, lambda h: (h, QKV + 4, 0))
            for j, u in enumerate(OUT_UNITS):
                o_ref[:, 128 * j:128 * j + 128] = (mine(u) + theirs(u))[0:7]
            small = mine(QKV + 4) + theirs(QKV + 4)
            gain_ref[...] = small[0:7, 64:66]
            bias_ref[...] = small[0:1, 80:89]


def finish(own, sib, out, tok):
    vm = pl.BlockSpec(memory_space=pltpu.VMEM)
    shapes = [((256, 896), BF), ((256, 896), BF), ((7, 896), F32), ((7, 128), F32),
              ((7, 128), F32), ((7, 896), F32), ((7, 4864), F32), ((7, 4864), F32),
              ((38, 896), F32), ((7, 2), F32), ((1, 9), F32)]
    return pl.pallas_call(
        finish_kernel,
        out_shape=tuple(jax.ShapeDtypeStruct(s, d) for s, d in shapes),
        in_specs=[vm] * 4, out_specs=[vm] * 11,
    )(own, sib, out, tok)


def constants():
    slots = np.zeros(128, np.int32)
    for n in range(128):
        dp, fs = n // 32, n % 32
        x, y, z, core = fs // 4 % 4, fs % 4, (dp // 2) * 2 + fs // 16, dp % 2
        slots[n] = ((GRAY[x] * 4 + GRAY[y]) * 4 + GRAY[z]) * 2 + core
    spread = np.zeros((896, 1024), np.float32)
    for d in range(896):
        spread[d, slots[d // 7] * 8 + d % 7] = 1.0
    spread_o = np.zeros((2, 448, 512), np.float32)
    for c in range(2):
        part = spread[448 * c:448 * c + 448].reshape(448, 16, 2, 32)
        spread_o[c] = part[:, :, c].reshape(448, 512)
    unpack = np.zeros((384, 304), np.float32)
    for a in range(8):
        for r in range(38):
            unpack[48 * a + r, 38 * a + r] = 1.0
    brow = np.full((2, 8, 640), -1, np.int32)
    for c in range(2):
        for i in range(576):
            if i < 448:
                nat = 448 * c + i
            elif i < 512:
                nat = 896 + 64 * c + i - 448
            else:
                nat = 1024 + 64 * c + i - 512
            brow[c, 0, i] = slots[nat // 9] * 8
            brow[c, 1, i] = nat % 9
    freq = THETA ** (-2.0 * (np.arange(128) % 32) / 64.0)
    freq = np.broadcast_to(freq.astype(np.float32), (8, 128))
    return (jnp.asarray(spread, BF), jnp.asarray(spread_o, BF), jnp.asarray(unpack.T, BF),
            jnp.asarray(unpack, BF), jnp.asarray(brow), jnp.asarray(freq))


def shards(tokens, segments, w_query, w_key, w_value, w_out, w_gate, w_up, w_down, gains, biases,
           cotangent):
    out, tok, own, sib = layer(
        w_query, w_key, w_value, w_out, w_gate, w_up, w_down, gains, biases.reshape(1, 9),
        segments.reshape(2, 128), tokens.reshape(256, 896), cotangent.reshape(256, 896),
        *constants())
    out, tok, *grads, bias = finish(own, sib, out, tok)
    return (out.reshape(tokens.shape), tok.reshape(tokens.shape), *grads, bias.reshape(9))


def solution(mesh):
    row = P(AXES, None)
    batch = P(None, AXES, None, None)
    return jax.shard_map(
        shards, mesh=mesh,
        in_specs=(batch, P(None, AXES, None)) + (row,) * 8 + (P(AXES), batch),
        out_specs=(batch, batch) + (row,) * 8 + (P(AXES),),
        check_vma=False,
    )
```

time: 244 us -> 207 us (0.85)
  Pallas kernels: 219 us -> 202 us
  local copies, waits for them, and re-layouts: 20.3 us -> 3.88 us
  other arithmetic: 3.82 us -> 0 us
    pallas_call x1, Pallas kernels: 219 us -> 200 us  [layer(): pl.pallas_call(layer_kernel, out_shape=(jax.ShapeDtypeStruct((256, 896),...]
    reshape x14 -> x0, local copies, waits for them, and re-layouts: 6.79 us -> none  [the longest x5 4.38 us: pick(): cut = w.reshape(7, -1, 2, w.shape[1] // (2 * parts))]
    slice x25 -> x0, local copies, waits for them, and re-layouts: 2.9 us -> none  [the longest x1 1.03 us: shards(): mine, theirs = (lines(own[:UNITS]), lines(sib))]
    pallas_call x0 -> x1, Pallas kernels: none -> 2.76 us  [finish(): pl.pallas_call(finish_kernel, out_shape=tuple((jax.ShapeDtypeStruct(s, d)...]
where the time goes in v3:
time: 207 us
  Pallas kernels  202 us (98%)
  local copies, waits for them, and re-layouts  3.88 us (2%)
    pallas_call x1, Pallas kernels, layer(): pl.pallas_call(layer_kernel, out_shape=(jax.ShapeDtypeStruct((256, 896),...  200 us

profile of v3, /device:TPU:1, one launch (start us, length us, event | category | flops | bytes accessed | tf_op | source)
XLA Modules:
  0.0 206.8 jit_solution(10924333468047995175)
XLA Ops:
  0.6 1.3 copy.29.gains
  2.0 1.2 jit_solution_.3.freq
  3.2 199.5 %shard_map.257 = (bf16[256,896]{1,0:T(8,128)(2,1)}, bf16[256,896]{1,0:T(8,128)(2,1)}, f32[71,16,128]{2,1,0:T(8,128)}, bf16[50,16,128]{2,1,0:T(8,128)(2,1)}) custom-call(bf16[7,896]{1,0:T(8,128)(2,1)} %w_query.1, bf16[7,128]{1,0:T(8,128)(2,1)} %w_key.1, bf16[7,128]{1,0:T(8,128)(2,1)} %w_value.1, bf16[7,896]{1,0:T(8,128)(2,1)} %w_out_.1, ...), custom_call_target="tpu_custom_call" | custom-call | tf_op jit(solution)/shard_map/pallas_call | solution.py:773
  202.7 2.8 %shard_map.258 = (bf16[256,896]{1,0:T(8,128)(2,1)}, bf16[256,896]{1,0:T(8,128)(2,1)}, f32[7,896]{1,0:T(8,128)}, f32[7,128]{1,0:T(8,128)}, f32[7,128]{1,0:T(8,128...) custom-call(f32[71,16,128]{2,1,0:T(8,128)} %get-tuple-element.26.own, ...), custom_call_target="tpu_custom_call" | custom-call | tf_op jit(solution)/shard_map/pallas_call | solution.py:861
  205.5 1.3 copy.32

commit v4 on v3

--- a/solution.py
+++ b/solution.py
@@ -18,7 +18,7 @@
 GRAY = (0, 1, 3, 2)
 
 BULK = ((0, 8), (8, 8), (16, 7), (23, 8), (31, 7), (38, 7))
-TALLS = ((0, 4), (4, 3), (7, 4), (11, 3), (14, 4), (18, 3))
+TALLS = ((0, 3), (3, 3), (6, 3), (9, 3), (12, 3), (15, 2))
 WAVES = (
     ((7, 1), (14, 2), (22, 1), (30, 1), (37, 1), (44, 1)),
     TALLS,
@@ -31,7 +31,7 @@
 OUT, DOWN, FFN = 0, 1, 2
 OUT_UNITS = (7, 14, 15, 22, 30, 37, 44)
 HEAD = ((45, 2), (47, 2), (49, 1))
-UNITS, TALL, QKV = 50, 21, 45
+UNITS, TALL, QKV = 50, 17, 45
 
 
 def pair_units(starts, last):
@@ -115,7 +115,7 @@
 
 def layer_kernel(
     w_query, w_key, w_value, w_out_, w_gate, w_up, w_down, gains, biases, segments,
-    x_own, e_own, spread_h, spread_o_h, pack_h, unpack_h, brow, freq,
+    x_own, e_own, spread_h, spread_o_h, pack_h, unpack_h, pick_in, pick_out, brow, freq,
     out_ref, gtok_ref, own_ref, sib_ref,
     u_buf, t_buf, u_got, t_got, wd, x_all, e_all, seg_all, stage, a1s, a2s, a2st, qkv, o_s,
     y1, ypart, yrec, da2, darec, mrec, arec, cosine, sine, gain, bias, slab,
@@ -154,8 +154,10 @@
     raw[0:1, S_AT + 16:S_AT + 25] = biases[...].astype(F32)
     seg_own[...] = jnp.zeros((8, 128), F32)
     seg_own[0:2, :] = segments[...].astype(F32)
-    last_rows[...] = jnp.zeros((16, 896), F32)
-    last_rows[0:6, :] = w_down[32:38, :].astype(F32)
+    last_rows[...] = jnp.zeros((48, 128), F32)
+    ends = w_down[32:38, :].astype(F32)
+    for c in range(7):
+        last_rows[6 * c:6 * c + 6, :] = ends[:, 128 * c:128 * c + 128]
 
     def lanes(first, second):
         if second == first + 64:
@@ -437,8 +439,9 @@
     for c in range(7):
         cols = slice(128 * c, 128 * c + 128)
         for r in range(2):
-            t_buf[(3 * c + r,) + mine] = w_down[16 * r:16 * r + 16, cols]
-        t_buf[(3 * c + 2,) + mine] = last_rows[:, cols].astype(BF)
+            t_buf[(2 * c + r,) + mine] = w_down[16 * r:16 * r + 16, cols]
+    for r in range(3):
+        t_buf[(14 + r,) + mine] = last_rows[16 * r:16 * r + 16, :].astype(BF)
     swap_pair.wait()
     u_buf[(slice(None),) + mine] = own_s[...] + stage[...]
     ag_head(0)
@@ -482,8 +485,14 @@
     @pl.loop(0, 4)
     def _(s):
         v = x_all[rows(s), :].astype(F32)
-        a1 = (v * inv_root(v) * gain[0:1, :]).astype(BF)
-        a1s[rows(s), :] = dot(a1, spread[...]).astype(BF)
+        a2s[rows(s), 0:896] = (v * inv_root(v) * gain[0:1, :]).astype(BF)
+
+    def spread_rows(dst):
+        for h in range(2):
+            at = pl.ds(256 * h, 256)
+            dst[at, :] = dot(a2s[at, 0:896], spread[...]).astype(BF)
+
+    spread_rows(a1s)
 
     ag_small_end()
     ag(OUT, 4)
@@ -496,8 +505,9 @@
         return jnp.concatenate([ref[rows(s), :]] * 5, axis=1)
 
     w_qkv = jnp.concatenate([unit(QKV + i) for i in range(5)], axis=1)
+    da2[:, 0:640] = dot(a1s[...], w_qkv)
     for s in range(4):
-        raw = dot(a1s[rows(s), :], w_qkv) + bias[0:1, :]
+        raw = da2[rows(s), 0:640] + bias[0:1, :]
         turned = jnp.where(first, -pltpu.roll(raw, 608, 1), pltpu.roll(raw, 32, 1))
         turned = raw * wide(cosine, s) + turned * wide(sine, s)
         qkv[rows(s), :] = jnp.where(turns, turned, raw).astype(BF)
@@ -542,11 +552,14 @@
         tick(s, 2, (ag, (FFN + 1, 4)))
         tick(s, 3, (ag, (FFN + 1, 5)))
         _, _, v, soft = attend(s)
-        o = unheads(dot(soft.astype(BF), v)).astype(BF)
-        os = dot(o, spread_o[core]).astype(BF)
-        o_s[rows(s), :] = os
-        ypart[rows(s), :] = dot(os, w_out())
-        y_swap(s).start()
+        a2s[rows(s), 0:448] = unheads(dot(soft.astype(BF), v)).astype(BF)
+
+    o_s[...] = dot(a2s[:, 0:448], spread_o[core]).astype(BF)
+    for h in range(2):
+        at = pl.ds(256 * h, 256)
+        ypart[at, :] = dot(o_s[at, :], w_out())
+        for s in (2 * h, 2 * h + 1):
+            y_swap(s).start()
 
     ag_done(DOWN)
     ag(FFN + 2, 4)
@@ -561,12 +574,15 @@
 
     @pl.loop(0, 8)
     def _(g):
-        lines = []
+        lines, ends = [], []
         for i in range(8):
             at = slab_place(g * 8 + i)
-            for r in range(3):
+            for r in range(2):
                 lines.append(jnp.concatenate(
-                    [t_buf[(3 * c + r,) + at] for c in range(7)], axis=1))
+                    [t_buf[(2 * c + r,) + at] for c in range(7)], axis=1))
+            ends += [t_buf[(14 + r,) + at] for r in range(3)]
+        ends = dot(pick_in[...], jnp.concatenate(ends, axis=0)).astype(BF)
+        lines.append(jnp.concatenate([ends[48 * c:48 * c + 48] for c in range(7)], axis=1))
         block = jnp.concatenate(lines, axis=0)
         wd[pl.ds(pl.multiple_of(g * 304, 16), 304), :] = dot(pack[...], block).astype(BF)
 
@@ -577,11 +593,11 @@
         y_swap(s).wait()
         v = x_all[rows(s), :].astype(F32) + (ypart[rows(s), :] + yrec[rows(s), :])
         y1[rows(s), :] = v
-        a2 = (v * inv_root(v) * gain[1:2, :]).astype(BF)
-        a2s[rows(s), :] = dot(a2, spread[...]).astype(BF)
+        a2s[rows(s), 0:896] = (v * inv_root(v) * gain[1:2, :]).astype(BF)
         ypart[rows(s), :] = jnp.zeros((128, 896), F32)
         da2[rows(s), :] = jnp.zeros((128, 1024), F32)
 
+    spread_rows(a2s)
     a2st[...] = a2s[...].T
 
     def ffn(gates, ups, row, n):
@@ -626,39 +642,46 @@
     out_swap.start()
 
     def unspread(v):
+        n = v.shape[0]
         high = v.astype(BF)
         low = (v - high.astype(F32)).astype(BF)
-        return dot_t(high, spread[...]) + dot_t(low, spread[...])
+        both = dot_t(jnp.concatenate([high, low], axis=0), spread[...])
+        return both[:n] + both[n:]
+
+    def unspread_rows(h):
+        at = pl.ds(256 * h, 256)
+        yrec[at, :] = unspread(da2[at, :])
 
     def da_swap(s):
         return to_sibling(yrec.at[rows(s)], darec.at[rows(s)], 9 + s)
 
-    @pl.loop(0, 4)
-    def _(s):
-        yrec[rows(s), :] = unspread(da2[rows(s), :])
-        da_swap(s).start()
+    for h in range(2):
+        unspread_rows(h)
+        for s in (2 * h, 2 * h + 1):
+            da_swap(s).start()
 
     rs(FFN + 1, 4)
 
     @pl.loop(0, 8)
     def _(g):
         block = dot(unpack[...], wd[pl.ds(pl.multiple_of(g * 304, 16), 304), :]).astype(BF)
+        ends = jnp.concatenate([block[256:304, 128 * c:128 * c + 128] for c in range(7)], axis=0)
+        ends = dot(pick_out[...], ends).astype(BF)
         for i in range(8):
             at = slab_place(g * 8 + i)
+            for r in range(2):
+                for c in range(7):
+                    t_buf[(2 * c + r,) + at] = block[32 * i + 16 * r:32 * i + 16 * r + 16,
+                                                     128 * c:128 * c + 128]
             for r in range(3):
-                for c in range(7):
-                    t_buf[(3 * c + r,) + at] = block[48 * i + 16 * r:48 * i + 16 * r + 16,
-                                                     128 * c:128 * c + 128]
+                t_buf[(14 + r,) + at] = ends[48 * i + 16 * r:48 * i + 16 * r + 16]
 
     rs(DOWN, 5)
-    rs_fold(FFN)
     out_swap.wait()
     for s in range(2):
         at = pl.ds(pl.multiple_of(core * 256 + 128 * s, 128), 128)
         out_ref[pl.ds(128 * s, 128), :] = (
             y1[at, :] + (ypart[at, :] + mrec[pl.ds(128 * s, 128), :])).astype(BF)
-
-    rs(FFN + 2, 4)
 
     gain_grads = gain.at[pl.ds(2, 2)]
     gain_grads[...] = jnp.zeros((2, 896), F32)
@@ -680,28 +703,27 @@
         darec[rows(s), :] = dy
         f = dy.astype(BF)
         a2s[rows(s), 0:896] = f
-        ds_ = dot_t(f, w_out()).astype(BF)
-        a2s[rows(s), 896:1024] = jnp.zeros((128, 128), BF)
-        a2st[rows(s), 0:448] = dot_t(ds_, spread_o[core]).astype(BF)
-
-    rs_fold(FFN + 1)
-    rs_small(0, 3)
+
+    rs(FFN + 2, 4)
+    w_o = w_out()
+    a2st[0:512, 0:448] = dot_t(dot_t(a2s[:, 0:896], w_o).astype(BF), spread_o[core]).astype(BF)
+
     o_grad = dot(o_s[...].T, a2s[:, 0:896]).astype(BF)
     for i in range(7):
         part = o_grad[:, 128 * i:128 * i + 128].reshape((2,) * 5 + (16, 128))
         u_buf[OUT_UNITS[i], :, :, :, :, core] = part
         u_buf[OUT_UNITS[i], :, :, :, :, 1 - core] = jnp.zeros_like(part)
     rs(OUT, 5)
-    rs_small(0, 2)
-    rs(DOWN, 4)
+    rs_fold(FFN)
+    rs_fold(FFN + 1)
+    rs_small(0, 3)
 
     bias[...] = jnp.zeros((8, 640), F32)
 
     @pl.loop(0, 4)
     def _(s):
-        tick(s, 1, (rs_small, (0, 1)), (rs_fold, (FFN + 2,)))
-        tick(s, 2, (rs, (OUT, 4)), (rs_small, (0, 0)))
-        tick(s, 3, (rs_fold, (DOWN,)))
+        tick(s, 2, (rs, (DOWN, 4)))
+        tick(s, 3, (rs, (OUT, 4)), (rs_fold, (FFN + 2,)))
         q7, k, v, soft = attend(s)
         do7 = heads(a2st[rows(s), 0:448])
         dp = dot_t(do7, v)
@@ -716,22 +738,22 @@
         qkv[rows(s), :] = grad
         bias[0:1, :] += jnp.sum(grad.astype(F32), axis=0, keepdims=True)
 
+    rs_small(0, 2)
+    w_qkv = jnp.concatenate([unit(QKV + i) for i in range(5)], axis=1)
+    da2[...] = dot_t(qkv[...], w_qkv)
+    rs_fold(DOWN)
     rs_fold(OUT)
     rs_small(1, 3)
-    w_qkv = jnp.concatenate([unit(QKV + i) for i in range(5)], axis=1)
-    da2[...] = dot_t(qkv[...], w_qkv)
-
-    @pl.loop(0, 4)
-    def _(s):
-        yrec[rows(s), :] = unspread(da2[rows(s), :])
-
+    for h in range(2):
+        unspread_rows(h)
     a_swap = to_sibling(yrec.at[other], arec, 13)
     a_swap.start()
-    rs_small(1, 2)
+    rs_small(0, 1)
     a2st[...] = a1s[...].T
     for i in range(4):
         part = dot(a2st[...], qkv[:, 128 * i:128 * i + 128])
         u_buf[QKV + i] = part.astype(BF).reshape((2,) * 6 + (16, 128))
+    rs_small(1, 2)
     a_swap.wait()
     for s in range(2):
         at = pl.ds(pl.multiple_of(core * 256 + 128 * s, 128), 128)
@@ -743,6 +765,7 @@
         gtok_ref[pl.ds(128 * s, 128), :] = (
             darec[at, :] + r * w
             - v * (r * r * r) * jnp.mean(w * v, axis=-1, keepdims=True)).astype(BF)
+    rs_small(0, 0)
     top = dot(jnp.concatenate([gain[2:4, :], jnp.zeros((14, 896), F32)], axis=0).astype(BF),
               spread[...])
     spot = jnp.where(choose, jnp.broadcast_to(bias[0:1, :], (16, 640)), 0.0).astype(BF)
@@ -779,7 +802,7 @@
             jax.ShapeDtypeStruct((UNITS, 16, 128), BF),
         ),
         in_specs=[pl.BlockSpec(memory_space=vm)] * 10 + [pl.BlockSpec(memory_space=pl.ANY)] * 6
-        + [pl.BlockSpec(memory_space=vm)] * 2,
+        + [pl.BlockSpec(memory_space=vm)] * 4,
         out_specs=[pl.BlockSpec(memory_space=vm)] * 4,
         scratch_shapes=[
             vm((UNITS,) + (2,) * 6 + (16, 128), BF), vm((TALL,) + (2,) * 6 + (16, 128), BF),
@@ -790,9 +813,9 @@
             vm((512, 896), F32), vm((512, 896), F32), vm((512, 896), F32), vm((512, 1024), F32),
             vm((512, 896), F32), vm((256, 896), F32), vm((256, 896), F32), vm((512, 128), F32), vm((512, 128), F32),
             vm((8, 896), F32), vm((8, 640), F32), vm((UNITS, 16, 128), BF),
-            vm((8, RAW), F32), vm((16, 896), F32), vm((UNITS, 16, 128), BF),
+            vm((8, RAW), F32), vm((48, 128), F32), vm((UNITS, 16, 128), BF),
             vm((UNITS, 16, 128), BF), vm((8, 128), F32), vm((896, 1024), BF), vm((2, 448, 512), BF),
-            vm((304, 384), BF), vm((384, 304), BF),
+            vm((304, 304), BF), vm((304, 304), BF),
             vm((3, 5, 16, 128), BF), vm((3, 5) + (2,) * 2 + (16, 128), BF),
             vm((3, 5) + (2,) * 4 + (16, 128), BF),
             dma((4, 6, 2)), dma((4, 6, 3)), dma((4, 6, 3)), dma((5, 2, 6)), dma((5, 2, 6)),
@@ -810,9 +833,11 @@
     out_ref[...] = out[...]
     tok_ref[...] = tok[...]
     for c in range(7):
-        for r in range(3):
-            n = 16 if r < 2 else 6
-            d_ref[16 * r:16 * r + n, 128 * c:128 * c + 128] = own[UNITS + 3 * c + r][0:n]
+        for r in range(2):
+            d_ref[16 * r:16 * r + 16, 128 * c:128 * c + 128] = own[UNITS + 2 * c + r]
+    ends = jnp.concatenate([own[UNITS + 14 + r] for r in range(3)], axis=0)
+    for c in range(7):
+        d_ref[32:38, 128 * c:128 * c + 128] = ends[6 * c:6 * c + 6]
     core = lax.axis_index("dp") % 2
     for c in range(2):
         @pl.when(core == c)
@@ -878,10 +903,14 @@
     for c in range(2):
         part = spread[448 * c:448 * c + 448].reshape(448, 16, 2, 32)
         spread_o[c] = part[:, :, c].reshape(448, 512)
-    unpack = np.zeros((384, 304), np.float32)
+    unpack = np.zeros((304, 304), np.float32)
+    pick_in = np.zeros((336, 384), np.float32)
     for a in range(8):
         for r in range(38):
-            unpack[48 * a + r, 38 * a + r] = 1.0
+            unpack[32 * a + r if r < 32 else 256 + 6 * a + r - 32, 38 * a + r] = 1.0
+        for r in range(6):
+            for c in range(7):
+                pick_in[48 * c + 6 * a + r, 48 * a + 6 * c + r] = 1.0
     brow = np.full((2, 8, 640), -1, np.int32)
     for c in range(2):
         for i in range(576):
@@ -896,7 +925,8 @@
     freq = THETA ** (-2.0 * (np.arange(128) % 32) / 64.0)
     freq = np.broadcast_to(freq.astype(np.float32), (8, 128))
     return (jnp.asarray(spread, BF), jnp.asarray(spread_o, BF), jnp.asarray(unpack.T, BF),
-            jnp.asarray(unpack, BF), jnp.asarray(brow), jnp.asarray(freq))
+            jnp.asarray(unpack, BF), jnp.asarray(pick_in, BF), jnp.asarray(pick_in.T, BF),
+            jnp.asarray(brow), jnp.asarray(freq))
 
 
 def shards(tokens, segments, w_query, w_key, w_value, w_out, w_gate, w_up, w_down, gains, biases,

time: 207 us -> 188 us (0.908)
  Pallas kernels: 202 us -> 184 us
    pallas_call x1, Pallas kernels: 200 us -> 181 us  [layer(): pl.pallas_call(layer_kernel, out_shape=(jax.ShapeDtypeStruct((256, 896),...]
where the time goes in v4:
time: 188 us
  Pallas kernels  184 us (98%)
  local copies, waits for them, and re-layouts  3.89 us (2%)
    pallas_call x1, Pallas kernels, layer(): pl.pallas_call(layer_kernel, out_shape=(jax.ShapeDtypeStruct((256, 896),...  181 us

profile of v4, /device:TPU:1, one launch (start us, length us, event | category | flops | bytes accessed | tf_op | source)
XLA Modules:
  0.0 188.1 jit_solution(13559853012030804585)
XLA Ops:
  0.6 1.3 copy.31.gains
  2.0 1.2 jit_solution_.3.freq
  3.2 180.8 %shard_map.275 = (bf16[256,896]{1,0:T(8,128)(2,1)}, bf16[256,896]{1,0:T(8,128)(2,1)}, f32[67,16,128]{2,1,0:T(8,128)}, bf16[50,16,128]{2,1,0:T(8,128)(2,1)}) custom-call(bf16[7,896]{1,0:T(8,128)(2,1)} %w_query.1, bf16[7,128]{1,0:T(8,128)(2,1)} %w_key.1, bf16[7,128]{1,0:T(8,128)(2,1)} %w_value.1, bf16[7,896]{1,0:T(8,128)(2,1)} %w_out_.1, ...), custom_call_target="tpu_custom_call" | custom-call | tf_op jit(solution)/shard_map/pallas_call | solution.py:796
  184.1 2.8 %shard_map.276 = (bf16[256,896]{1,0:T(8,128)(2,1)}, bf16[256,896]{1,0:T(8,128)(2,1)}, f32[7,896]{1,0:T(8,128)}, f32[7,128]{1,0:T(8,128)}, f32[7,128]{1,0:T(8,128...) custom-call(f32[67,16,128]{2,1,0:T(8,128)} %get-tuple-element.26.own, ...), custom_call_target="tpu_custom_call" | custom-call | tf_op jit(solution)/shard_map/pallas_call | solution.py:886
  186.8 1.3 copy.34

commit v5 on v4

--- a/solution.py
+++ b/solution.py
@@ -149,8 +149,11 @@
 
     raw[...] = jnp.zeros((8, RAW), F32)
     for ref, a in ((w_gate, GATE_AT), (w_up, UP_AT), (w_query, Q_AT), (w_key, K_AT),
-                   (w_value, V_AT), (w_out_, O_AT), (gains, S_AT)):
+                   (w_value, V_AT), (w_out_, O_AT)):
         raw[0:7, a:a + ref.shape[1]] = ref[...].astype(F32)
+    last_rows[0:8, :] = jnp.zeros((8, 128), F32)
+    last_rows[0:2, 0:7] = gains[...].astype(F32)
+    raw[0:7, S_AT:S_AT + 2] = last_rows[0:8, :].T[0:7, 0:2]
     raw[0:1, S_AT + 16:S_AT + 25] = biases[...].astype(F32)
     seg_own[...] = jnp.zeros((8, 128), F32)
     seg_own[0:2, :] = segments[...].astype(F32)
@@ -497,6 +500,7 @@
     ag_small_end()
     ag(OUT, 4)
     ag(DOWN, 4)
+    ag(FFN, 4)
     lane = lax.broadcasted_iota(jnp.int32, (128, 640), 1)
     first = lane % 64 < 32
     turns = lane < 512
@@ -512,8 +516,6 @@
         turned = raw * wide(cosine, s) + turned * wide(sine, s)
         qkv[rows(s), :] = jnp.where(turns, turned, raw).astype(BF)
     ag(OUT, 5)
-    ag(FFN, 4)
-    ag_done(OUT)
     ag(DOWN, 5)
 
     def heads(v):
@@ -548,12 +550,11 @@
 
     @pl.loop(0, 4)
     def _(s):
-        tick(s, 1, (ag, (FFN, 5)))
-        tick(s, 2, (ag, (FFN + 1, 4)))
-        tick(s, 3, (ag, (FFN + 1, 5)))
+        tick(s, 2, (ag, (FFN, 5)), (ag, (FFN + 1, 4)))
         _, _, v, soft = attend(s)
         a2s[rows(s), 0:448] = unheads(dot(soft.astype(BF), v)).astype(BF)
 
+    ag_done(OUT)
     o_s[...] = dot(a2s[:, 0:448], spread_o[core]).astype(BF)
     for h in range(2):
         at = pl.ds(256 * h, 256)
@@ -562,7 +563,6 @@
             y_swap(s).start()
 
     ag_done(DOWN)
-    ag(FFN + 2, 4)
 
     def slab_place(s):
         z, x, y = s // 16, s // 4 % 4, s % 4
@@ -586,7 +586,8 @@
         block = jnp.concatenate(lines, axis=0)
         wd[pl.ds(pl.multiple_of(g * 304, 16), 304), :] = dot(pack[...], block).astype(BF)
 
-    ag(FFN + 2, 5)
+    ag(FFN + 1, 5)
+    ag(FFN + 2, 4)
 
     @pl.loop(0, 4)
     def _(s):
@@ -626,15 +627,16 @@
 
     @pl.loop(0, 9)
     def _(i):
+        tick(i, 2, (ag, (FFN + 2, 5)))
         tick(i, 3, (rs, (FFN, 5)), (ag_done, (FFN + 1,)))
         tick(i, 6, (rs, (FFN + 1, 5)), (ag_done, (FFN + 2,)))
-        tick(i, 7, (rs, (FFN, 4)))
         wave, q = i // 3, i % 3
         g = 8 * q + 2 * wave
         u = 23 + 8 * q - q // 2 + 2 * wave
         ffn([g, g + 1], [u, u + 1], i * 256, 2)
 
     ffn([6], [29], 2304, 1)
+    rs(FFN, 4)
     rs(FFN + 2, 5)
 
     other = pl.ds(pl.multiple_of((1 - core) * 256, 256), 256)
@@ -874,7 +876,7 @@
             for j, u in enumerate(OUT_UNITS):
                 o_ref[:, 128 * j:128 * j + 128] = (mine(u) + theirs(u))[0:7]
             small = mine(QKV + 4) + theirs(QKV + 4)
-            gain_ref[...] = small[0:7, 64:66]
+            gain_ref[...] = small.T[64:66, 0:7]
             bias_ref[...] = small[0:1, 80:89]
 
 
@@ -882,7 +884,7 @@
     vm = pl.BlockSpec(memory_space=pltpu.VMEM)
     shapes = [((256, 896), BF), ((256, 896), BF), ((7, 896), F32), ((7, 128), F32),
               ((7, 128), F32), ((7, 896), F32), ((7, 4864), F32), ((7, 4864), F32),
-              ((38, 896), F32), ((7, 2), F32), ((1, 9), F32)]
+              ((38, 896), F32), ((2, 7), F32), ((1, 9), F32)]
     return pl.pallas_call(
         finish_kernel,
         out_shape=tuple(jax.ShapeDtypeStruct(s, d) for s, d in shapes),
@@ -923,7 +925,7 @@
             brow[c, 0, i] = slots[nat // 9] * 8
             brow[c, 1, i] = nat % 9
     freq = THETA ** (-2.0 * (np.arange(128) % 32) / 64.0)
-    freq = np.broadcast_to(freq.astype(np.float32), (8, 128))
+    freq = np.concatenate([freq[None], np.zeros((7, 128))]).astype(np.float32)
     return (jnp.asarray(spread, BF), jnp.asarray(spread_o, BF), jnp.asarray(unpack.T, BF),
             jnp.asarray(unpack, BF), jnp.asarray(pick_in, BF), jnp.asarray(pick_in.T, BF),
             jnp.asarray(brow), jnp.asarray(freq))
@@ -932,11 +934,12 @@
 def shards(tokens, segments, w_query, w_key, w_value, w_out, w_gate, w_up, w_down, gains, biases,
            cotangent):
     out, tok, own, sib = layer(
-        w_query, w_key, w_value, w_out, w_gate, w_up, w_down, gains, biases.reshape(1, 9),
+        w_query, w_key, w_value, w_out, w_gate, w_up, w_down, gains.T, biases.reshape(1, 9),
         segments.reshape(2, 128), tokens.reshape(256, 896), cotangent.reshape(256, 896),
         *constants())
-    out, tok, *grads, bias = finish(own, sib, out, tok)
-    return (out.reshape(tokens.shape), tok.reshape(tokens.shape), *grads, bias.reshape(9))
+    out, tok, *grads, gain, bias = finish(own, sib, out, tok)
+    return (out.reshape(tokens.shape), tok.reshape(tokens.shape), *grads, gain.T,
+            bias.reshape(9))
 
 
 def solution(mesh):

time: 188 us -> 179 us (0.952)
  Pallas kernels: 184 us -> 178 us
  local copies, waits for them, and re-layouts: 3.89 us -> 0 us
    pallas_call x1, Pallas kernels: 181 us -> 176 us  [layer(): pl.pallas_call(layer_kernel, out_shape=(jax.ShapeDtypeStruct((256, 896),...]
    unnamed x2 -> x0, local copies, waits for them, and re-layouts: 2.64 us -> none
where the time goes in v5:
time: 179 us
  Pallas kernels  178 us (99%)
    pallas_call x1, Pallas kernels, layer(): pl.pallas_call(layer_kernel, out_shape=(jax.ShapeDtypeStruct((256, 896),...  176 us

profile of v5, /device:TPU:1, one launch (start us, length us, event | category | flops | bytes accessed | tf_op | source)
XLA Modules:
  0.0 179.1 jit_solution(12029112300232490373)
XLA Ops:
  0.6 175.6 %shard_map.275 = (bf16[256,896]{1,0:T(8,128)(2,1)}, bf16[256,896]{1,0:T(8,128)(2,1)}, f32[67,16,128]{2,1,0:T(8,128)}, bf16[50,16,128]{2,1,0:T(8,128)(2,1)}) custom-call(bf16[7,896]{1,0:T(8,128)(2,1)} %w_query.1, bf16[7,128]{1,0:T(8,128)(2,1)} %w_key.1, bf16[7,128]{1,0:T(8,128)(2,1)} %w_value.1, bf16[7,896]{1,0:T(8,128)(2,1)} %w_out_.1, ...), custom_call_target="tpu_custom_call" | custom-call | tf_op jit(solution)/shard_map/pallas_call | solution.py:798
  176.2 2.8 %shard_map.276 = (bf16[256,896]{1,0:T(8,128)(2,1)}, bf16[256,896]{1,0:T(8,128)(2,1)}, f32[7,896]{1,0:T(8,128)}, f32[7,128]{1,0:T(8,128)}, f32[7,128]{1,0:T(8,128...) custom-call(f32[67,16,128]{2,1,0:T(8,128)} %get-tuple-element.26.own, ...), custom_call_target="tpu_custom_call" | custom-call | tf_op jit(solution)/shard_map/pallas_call | solution.py:888

commit v6 on v5

--- a/solution.py
+++ b/solution.py
@@ -22,12 +22,12 @@
 WAVES = (
     ((7, 1), (14, 2), (22, 1), (30, 1), (37, 1), (44, 1)),
     TALLS,
-    ((0, 2), (8, 2), (16, 2), (23, 2), (31, 2), (38, 2)),
-    ((2, 2), (10, 2), (18, 2), (25, 2), (33, 2), (40, 2)),
-    ((4, 3), (12, 2), (20, 2), (27, 3), (35, 2), (42, 2)),
+    ((0, 3), (8, 2), (16, 2), (23, 3), (31, 2), (38, 2)),
+    ((3, 2), (10, 2), (18, 2), (26, 2), (33, 2), (40, 2)),
+    ((5, 2), (12, 2), (20, 2), (28, 2), (35, 2), (42, 2)),
 )
-EARLY = ((0, 4), (8, 4), (16, 4), (23, 4), (31, 4), (38, 4))
-LATE = ((4, 4), (12, 4), (20, 3), (27, 4), (35, 3), (42, 3))
+EARLY = ((0, 5), (8, 4), (16, 4), (23, 5), (31, 4), (38, 4))
+LATE = ((5, 3), (12, 4), (20, 3), (28, 3), (35, 3), (42, 3))
 OUT, DOWN, FFN = 0, 1, 2
 OUT_UNITS = (7, 14, 15, 22, 30, 37, 44)
 HEAD = ((45, 2), (47, 2), (49, 1))
@@ -35,11 +35,12 @@
 
 
 def pair_units(starts, last):
-    return tuple(starts[j % 6 // 2] + 2 * (j // 6) + j % 2 for j in range(18)) + (last,)
-
-
-GATE_UNITS = pair_units((0, 8, 16), 6)
-UP_UNITS = pair_units((23, 31, 38), 29)
+    return tuple(starts[j % 6 // 2] + 2 * (j // 6) + j % 2 + (j > 5 and j % 6 < 2)
+                 for j in range(18)) + (last,)
+
+
+GATE_UNITS = pair_units((0, 8, 16), 2)
+UP_UNITS = pair_units((23, 31, 38), 25)
 GATE_AT, UP_AT, Q_AT, K_AT, V_AT, O_AT, S_AT, RAW = (
     0, 4864, 9728, 10624, 10752, 10880, 11776, 11904)
 ORDER = tuple(
@@ -191,18 +192,6 @@
                     tile = jnp.concatenate([zero, v] if c else [v, zero], axis=0)
                     dst[place] = tile.astype(BF)
 
-    fill(send_s, True)
-    pl.semaphore_wait(barrier, 10)
-    swap_pair = to_sibling(send_s, stage, 0)
-    swap_pair.start()
-    swap_seg = to_sibling(seg_own, seg_all.at[core], 1)
-    swap_x = to_sibling(x_own, x_all.at[own], 2)
-    swap_e = to_sibling(e_own, e_all.at[own], 3)
-    for c in (swap_seg, swap_x, swap_e):
-        c.start()
-    fill(own_s, False)
-    seg_all[core] = seg_own[...]
-
     def remote(src, dst, send, recv, to):
         return pltpu.make_async_remote_copy(
             src_ref=src, dst_ref=dst, send_sem=send, recv_sem=recv, device_id=to,
@@ -219,40 +208,67 @@
         return remote(ref, ref, small_send.at[k, p, i], ag_small_recv.at[k, p, i],
                       peers[ORDER[p][k]])
 
-    def ag_small(k):
-        for i in range(2):
-            for p in range(6):
-                if k > 0:
-                    small_copy(k - 1, p, i).wait_recv()
-                small_copy(k, p, i).start()
-
-    def ag_small_end():
-        for i in range(2):
-            for p in range(6):
-                small_copy(3, p, i).wait_recv()
+    def ag_small(k, i):
+        for p in range(6):
+            if k > 0:
+                small_copy(k - 1, p, i).wait_recv()
+            small_copy(k, p, i).start()
+
+    def ag_small_end(i):
+        for p in range(6):
+            small_copy(3, p, i).wait_recv()
+
+    def ag_small_sent():
         for i in range(2):
             for p in range(6):
                 for k in range(4):
                     small_copy(k, p, i).wait_send()
 
+    is_mine = bits[5] == core
+
+    def when(test, f):
+        if test is None:
+            f()
+        else:
+            pl.when(test)(f)
+
+    def open_bit(w, k, p):
+        return ORDER[p].index(5) - k if w == OUT else None
+
+    def ag_tests(w, k, p):
+        at = open_bit(w, k, p)
+        if at is None or at < 0:
+            return None, None
+        return is_mine, (jnp.logical_not(is_mine) if at == 0 else is_mine)
+
+    def rs_tests(w, k, p):
+        send, take = ag_tests(w, k, p)
+        return take, send
+
+    def cut(w, k, p, b, full):
+        if w == OUT and open_bit(w, k, p) < 0:
+            b, full = list(b), [i for i in full if i != 5]
+            b[5] = core
+        return slot(b, full)
+
     def ag_copy(w, k, p):
         order = ORDER[p]
-        ref = bufs(w)[0].at[(pl.ds(*WAVES[w][p]),) + slot(bits, order[:k])]
+        ref = bufs(w)[0].at[(pl.ds(*WAVES[w][p]),) + cut(w, k, p, bits, order[:k])]
         return remote(ref, ref, big_send.at[w, k - 4, p], ag_big_recv.at[w, k - 4, p],
                       peers[order[k]])
 
     def ag(w, k):
         for p in range(6):
             if k == 5:
-                ag_copy(w, 4, p).wait_recv()
-            ag_copy(w, k, p).start()
+                when(ag_tests(w, 4, p)[1], ag_copy(w, 4, p).wait_recv)
+            when(ag_tests(w, k, p)[0], ag_copy(w, k, p).start)
 
     def ag_done(w):
         for p in range(6):
-            ag_copy(w, 5, p).wait_recv()
+            when(ag_tests(w, 5, p)[1], ag_copy(w, 5, p).wait_recv)
         for p in range(6):
             for k in (4, 5):
-                ag_copy(w, k, p).wait_send()
+                when(ag_tests(w, k, p)[0], ag_copy(w, k, p).wait_send)
 
     def given(k, p, *more):
         b = list(bits)
@@ -260,23 +276,37 @@
             b[ORDER[p][j]] = flipped[ORDER[p][j]]
         return slot(b, ORDER[p][:k])
 
+    def flipped_at(p, *steps):
+        b = list(bits)
+        for j in steps:
+            b[ORDER[p][j]] = flipped[ORDER[p][j]]
+        return b
+
+    def got_at(w, p):
+        if w == OUT and ORDER[p][5] != 5:
+            return tuple(core if b == 5 else slice(None) for b in DIMS if b != ORDER[p][5])
+        return ()
+
     def rs_copy(w, k, p):
         acc, got = bufs(w)
         units = pl.ds(*WAVES[w][p])
-        dst = got.at[units]
-        if k < 5:
-            b = list(bits)
-            b[ORDER[p][5]] = flipped[ORDER[p][5]]
-            dst = acc.at[(units,) + slot(b, ORDER[p][:k])]
-        return remote(acc.at[(units,) + given(k, p)], dst, big_send.at[w, k - 4, p],
-                      rs_big_recv.at[w, k - 4, p], peers[ORDER[p][k]])
-
-    def rs_add(acc, got, part, k, p):
+        full = ORDER[p][:k]
+        src = acc.at[(units,) + cut(w, k, p, flipped_at(p, k), full)]
+        if k == 5:
+            dst = got.at[(units,) + got_at(w, p)]
+        else:
+            dst = acc.at[(units,) + cut(w, k, p, flipped_at(p, 5), full)]
+        return remote(src, dst, big_send.at[w, k - 4, p], rs_big_recv.at[w, k - 4, p],
+                      peers[ORDER[p][k]])
+
+    def rs_add(acc, got, part, k, p, w=None):
         start, n = part
-        mine_ = slot(bits, ORDER[p][:k])
+        full = ORDER[p][:k]
+        mine_ = cut(w, k, p, bits, full)
+        there = cut(w, k, p, flipped_at(p, 5, k), full)
 
         def one(u):
-            add = got[u] if k == 5 else acc[(u,) + given(k, p, 5)]
+            add = got[(u,) + got_at(w, p)] if k == 5 else acc[(u,) + there]
             acc[(u,) + mine_] = acc[(u,) + mine_] + add
 
         if k >= 2:
@@ -287,26 +317,31 @@
             for i in range(n):
                 one(start + i)
 
+    def rs_take(w, k, p):
+        acc, got = bufs(w)
+
+        def take():
+            rs_copy(w, k, p).wait_recv()
+            rs_add(acc, got, WAVES[w][p], k, p, w)
+
+        when(rs_tests(w, k, p)[1], take)
+
     def rs(w, k):
-        acc, got = bufs(w)
         if k == 4:
             for p in range(6):
-                rs_copy(w, 5, p).wait_send()
+                when(rs_tests(w, 5, p)[0], rs_copy(w, 5, p).wait_send)
             for b in range(6):
                 pl.semaphore_signal(credit.at[w, b], inc=1, device_id=peers[b],
                                     device_id_type=MESH)
         for p in range(6):
             if k == 4:
-                rs_copy(w, 5, p).wait_recv()
-                rs_add(acc, got, WAVES[w][p], 5, p)
+                rs_take(w, 5, p)
                 pl.semaphore_wait(credit.at[w, ORDER[p][4]], 1)
-            rs_copy(w, k, p).start()
+            when(rs_tests(w, k, p)[0], rs_copy(w, k, p).start)
 
     def rs_fold(w):
-        acc, got = bufs(w)
         for p in range(6):
-            rs_copy(w, 4, p).wait_recv()
-            rs_add(acc, got, WAVES[w][p], 4, p)
+            rs_take(w, 4, p)
 
     GROUPS = (((u_buf, EARLY),), ((u_buf, LATE), (t_buf, TALLS)))
 
@@ -349,7 +384,7 @@
     def rs_sent():
         for p in range(6):
             for w in range(5):
-                rs_copy(w, 4, p).wait_send()
+                when(rs_tests(w, 4, p)[0], rs_copy(w, 4, p).wait_send)
             for g, i in ((0, 0), (1, 0), (1, 1)):
                 for k in range(4):
                     rs_small_copy(g, k, p, i).wait_send()
@@ -432,12 +467,6 @@
         at = pl.ds(0, QKV) if i == 0 else pl.ds(QKV, UNITS - QKV)
         return to_sibling(slab.at[at], sib_ref.at[at], 16 + i)
 
-    def rows(s):
-        return pl.ds(pl.multiple_of(s * 128, 128), 128)
-
-    def unit(u):
-        return u_buf[u].reshape(1024, 128)
-
     mine = slot(bits, ())
     for c in range(7):
         cols = slice(128 * c, 128 * c + 128)
@@ -445,18 +474,40 @@
             t_buf[(2 * c + r,) + mine] = w_down[16 * r:16 * r + 16, cols]
     for r in range(3):
         t_buf[(14 + r,) + mine] = last_rows[16 * r:16 * r + 16, :].astype(BF)
+    fill(send_s, True)
+    pl.semaphore_wait(barrier, 10)
+    swap_pair = to_sibling(send_s, stage, 0)
+    swap_pair.start()
+    ag_small(0, 1)
+    swap_seg = to_sibling(seg_own, seg_all.at[core], 1)
+    swap_x = to_sibling(x_own, x_all.at[own], 2)
+    swap_e = to_sibling(e_own, e_all.at[own], 3)
+    for c in (swap_seg, swap_x, swap_e):
+        c.start()
+    fill(own_s, False)
+    seg_all[core] = seg_own[...]
+
+    def rows(s):
+        return pl.ds(pl.multiple_of(s * 128, 128), 128)
+
+    def unit(u):
+        return u_buf[u].reshape(1024, 128)
+
     swap_pair.wait()
     u_buf[(slice(None),) + mine] = own_s[...] + stage[...]
     ag_head(0)
-    ag_small(0)
+    ag_small(0, 0)
+    ag_small(1, 1)
     ag_head(1)
-    ag_small(1)
+    ag_small(1, 0)
+    ag_small(2, 1)
     ag_head(2)
     for c in locals_:
         c.wait()
     for c in (swap_seg, swap_x, swap_e):
         c.wait()
-    ag_small(2)
+    ag_small(3, 1)
+    ag_small(2, 0)
 
     causal = (lax.broadcasted_iota(jnp.int32, (128, 128), 1)
               <= lax.broadcasted_iota(jnp.int32, (128, 128), 0))
@@ -471,7 +522,9 @@
         angle = place * freq[0:1, :]
         cosine[rows(s), :] = jnp.cos(angle)
         sine[rows(s), :] = jnp.sin(angle)
-    ag_small(3)
+    ag_small_end(1)
+    ag(DOWN, 4)
+    ag_small(3, 0)
     ag_head_done()
 
     small = unit(49).T
@@ -497,9 +550,8 @@
 
     spread_rows(a1s)
 
-    ag_small_end()
+    ag_small_end(0)
     ag(OUT, 4)
-    ag(DOWN, 4)
     ag(FFN, 4)
     lane = lax.broadcasted_iota(jnp.int32, (128, 640), 1)
     first = lane % 64 < 32
@@ -555,6 +607,7 @@
         a2s[rows(s), 0:448] = unheads(dot(soft.astype(BF), v)).astype(BF)
 
     ag_done(OUT)
+    ag_small_sent()
     o_s[...] = dot(a2s[:, 0:448], spread_o[core]).astype(BF)
     for h in range(2):
         at = pl.ds(256 * h, 256)
@@ -624,6 +677,7 @@
                 u_buf[place] = grads[:, 128 * i:128 * i + 128].reshape((2,) * 6 + (16, 128))
 
     ag_done(FFN)
+    ffn([2], [25], 2304, 1)
 
     @pl.loop(0, 9)
     def _(i):
@@ -631,11 +685,11 @@
         tick(i, 3, (rs, (FFN, 5)), (ag_done, (FFN + 1,)))
         tick(i, 6, (rs, (FFN + 1, 5)), (ag_done, (FFN + 2,)))
         wave, q = i // 3, i % 3
-        g = 8 * q + 2 * wave
-        u = 23 + 8 * q - q // 2 + 2 * wave
+        odd = (2 - q) // 2 * ((wave + 1) // 2)
+        g = 8 * q + 2 * wave + odd
+        u = 23 + 8 * q - q // 2 + 2 * wave + odd
         ffn([g, g + 1], [u, u + 1], i * 256, 2)
 
-    ffn([6], [29], 2304, 1)
     rs(FFN, 4)
     rs(FFN + 2, 5)
 

time: 179 us -> 169 us (0.944)
  Pallas kernels: 178 us -> 168 us
    pallas_call x1, Pallas kernels: 176 us -> 166 us  [layer(): pl.pallas_call(layer_kernel, out_shape=(jax.ShapeDtypeStruct((256, 896),...]
where the time goes in v6:
time: 169 us
  Pallas kernels  168 us (99%)
    pallas_call x1, Pallas kernels, layer(): pl.pallas_call(layer_kernel, out_shape=(jax.ShapeDtypeStruct((256, 896),...  166 us

profile of v6, /device:TPU:1, one launch (start us, length us, event | category | flops | bytes accessed | tf_op | source)
XLA Modules:
  0.0 169.2 jit_solution(12174927006248041242)
XLA Ops:
  0.6 165.7 %shard_map.275 = (bf16[256,896]{1,0:T(8,128)(2,1)}, bf16[256,896]{1,0:T(8,128)(2,1)}, f32[67,16,128]{2,1,0:T(8,128)}, bf16[50,16,128]{2,1,0:T(8,128)(2,1)}) custom-call(bf16[7,896]{1,0:T(8,128)(2,1)} %w_query.1, bf16[7,128]{1,0:T(8,128)(2,1)} %w_key.1, bf16[7,128]{1,0:T(8,128)(2,1)} %w_value.1, bf16[7,896]{1,0:T(8,128)(2,1)} %w_out_.1, ...), custom_call_target="tpu_custom_call" | custom-call | tf_op jit(solution)/shard_map/pallas_call | solution.py:852
  166.4 2.8 %shard_map.276 = (bf16[256,896]{1,0:T(8,128)(2,1)}, bf16[256,896]{1,0:T(8,128)(2,1)}, f32[7,896]{1,0:T(8,128)}, f32[7,128]{1,0:T(8,128)}, f32[7,128]{1,0:T(8,128...) custom-call(f32[67,16,128]{2,1,0:T(8,128)} %get-tuple-element.26.own, ...), custom_call_target="tpu_custom_call" | custom-call | tf_op jit(solution)/shard_map/pallas_call | solution.py:942

commit v7 on v6

--- a/solution.py
+++ b/solution.py
@@ -202,10 +202,15 @@
     def bufs(w):
         return (t_buf, t_got) if w == DOWN else (u_buf, u_got)
 
+    def sent(buf, parts, k, sem):
+        count = sum(n for _, n in parts)
+        ref = buf.at[(pl.ds(0, count),) + slot(bits, ORDER[0][:k])]
+        remote(ref, ref, sem, sem, peers[0]).wait_send()
+
     def small_copy(k, p, i):
         buf, parts = BOTH[i]
         ref = buf.at[(pl.ds(*parts[p]),) + slot(bits, ORDER[p][:k])]
-        return remote(ref, ref, small_send.at[k, p, i], ag_small_recv.at[k, p, i],
+        return remote(ref, ref, small_send.at[k, 2 * i], ag_small_recv.at[k, p, i],
                       peers[ORDER[p][k]])
 
     def ag_small(k, i):
@@ -220,9 +225,9 @@
 
     def ag_small_sent():
         for i in range(2):
-            for p in range(6):
-                for k in range(4):
-                    small_copy(k, p, i).wait_send()
+            buf, parts = BOTH[i]
+            for k in range(4):
+                sent(buf, parts, k, small_send.at[k, 2 * i])
 
     is_mine = bits[5] == core
 
@@ -351,7 +356,7 @@
         b = list(bits)
         b[ORDER[p][5]] = flipped[ORDER[p][5]]
         return remote(buf.at[(units,) + given(k, p)], buf.at[(units,) + slot(b, ORDER[p][:k])],
-                      small_send.at[k, p, g + i], rs_small_recv.at[k, p, g + i],
+                      small_send.at[k, g + i], rs_small_recv.at[k, p, g + i],
                       peers[ORDER[p][k]])
 
     def rs_small(g, k):
@@ -385,9 +390,9 @@
         for p in range(6):
             for w in range(5):
                 when(rs_tests(w, 4, p)[0], rs_copy(w, 4, p).wait_send)
-            for g, i in ((0, 0), (1, 0), (1, 1)):
-                for k in range(4):
-                    rs_small_copy(g, k, p, i).wait_send()
+        for g, i in ((0, 0), (1, 0), (1, 1)):
+            for k in range(4):
+                sent(*GROUPS[g][i], k, small_send.at[k, g + i])
 
     def turned_bits(axis, j):
         b = list(bits)
@@ -403,8 +408,13 @@
 
     def head_copy(stage, r, j):
         ref = u_buf.at[(pl.ds(*HEAD[r]),) + slot(bits, head_full(r, stage))]
-        return remote(ref, ref, head_send.at[stage, r, j], ag_head_recv.at[stage, r, j],
+        return remote(ref, ref, head_send.at[stage], ag_head_recv.at[stage, r, j],
                       head_to((r + stage) % 3, j))
+
+    def head_sent():
+        for stage in range(3):
+            ref = u_buf.at[(pl.ds(0, 15),) + slot(bits, head_full(0, stage))]
+            remote(ref, ref, head_send.at[stage], head_send.at[stage], peers[0]).wait_send()
 
     def ag_head(stage):
         for r in range(3):
@@ -418,17 +428,14 @@
         for r in range(3):
             for j in range(3):
                 head_copy(2, r, j).wait_recv()
-        for r in range(3):
-            for j in range(3):
-                for stage in range(3):
-                    head_copy(stage, r, j).wait_send()
+        head_sent()
 
     def head_rs_copy(stage, r, j):
         start, n = HEAD[r]
         axis = (r + stage) % 3
         src = u_buf.at[(pl.ds(start, n),) + slot(turned_bits(axis, j), head_full(r, stage))]
         dst = (h_got0, h_got1, h_got2)[stage].at[j, pl.ds(start - QKV, n)]
-        return remote(src, dst, head_send.at[stage, r, j], rs_head_recv.at[stage, r, j],
+        return remote(src, dst, head_send.at[stage], rs_head_recv.at[stage, r, j],
                       head_to(axis, j))
 
     def head_sum(stage, r):
@@ -458,10 +465,7 @@
     def rs_head_end():
         for r in range(3):
             head_sum(0, r)
-        for r in range(3):
-            for j in range(3):
-                for stage in range(3):
-                    head_rs_copy(stage, r, j).wait_send()
+        head_sent()
 
     def last_swap(i):
         at = pl.ds(0, QKV) if i == 0 else pl.ds(QKV, UNITS - QKV)
@@ -874,8 +878,8 @@
             vm((304, 304), BF), vm((304, 304), BF),
             vm((3, 5, 16, 128), BF), vm((3, 5) + (2,) * 2 + (16, 128), BF),
             vm((3, 5) + (2,) * 4 + (16, 128), BF),
-            dma((4, 6, 2)), dma((4, 6, 3)), dma((4, 6, 3)), dma((5, 2, 6)), dma((5, 2, 6)),
-            dma((5, 2, 6)), dma((3, 3, 3)), dma((3, 3, 3)), dma((3, 3, 3)),
+            dma((4, 6, 2)), dma((4, 6, 3)), dma((4, 3)), dma((5, 2, 6)), dma((5, 2, 6)),
+            dma((5, 2, 6)), dma((3, 3, 3)), dma((3, 3, 3)), dma((3,)),
             pltpu.SemaphoreType.REGULAR((7, 6)),
             dma((21,)), dma((21,)), dma((6,)),
         ],

time: 169 us -> 169 us (level)
  no operation moved by 1% of the time
where the time goes in v7:
time: 169 us; the launch traced here: 168 us
  Pallas kernels  168 us (99%)
    pallas_call x1, Pallas kernels, layer(): pl.pallas_call(layer_kernel, out_shape=(jax.ShapeDtypeStruct((256, 896),...  165 us

profile of v7, /device:TPU:1, one launch (start us, length us, event | category | flops | bytes accessed | tf_op | source)
XLA Modules:
  0.0 168.5 jit_solution(18392648187475639480)
XLA Ops:
  0.6 164.9 %shard_map.275 = (bf16[256,896]{1,0:T(8,128)(2,1)}, bf16[256,896]{1,0:T(8,128)(2,1)}, f32[67,16,128]{2,1,0:T(8,128)}, bf16[50,16,128]{2,1,0:T(8,128)(2,1)}) custom-call(bf16[7,896]{1,0:T(8,128)(2,1)} %w_query.1, bf16[7,128]{1,0:T(8,128)(2,1)} %w_key.1, bf16[7,128]{1,0:T(8,128)(2,1)} %w_value.1, bf16[7,896]{1,0:T(8,128)(2,1)} %w_out_.1, ...), custom_call_target="tpu_custom_call" | custom-call | tf_op jit(solution)/shard_map/pallas_call | solution.py:856
  165.6 2.8 %shard_map.276 = (bf16[256,896]{1,0:T(8,128)(2,1)}, bf16[256,896]{1,0:T(8,128)(2,1)}, f32[7,896]{1,0:T(8,128)}, f32[7,128]{1,0:T(8,128)}, f32[7,128]{1,0:T(8,128...) custom-call(f32[67,16,128]{2,1,0:T(8,128)} %get-tuple-element.26.own, ...), custom_call_target="tpu_custom_call" | custom-call | tf_op jit(solution)/shard_map/pallas_call | solution.py:946

commit v8 on v7

--- a/solution.py
+++ b/solution.py
@@ -18,7 +18,7 @@
 GRAY = (0, 1, 3, 2)
 
 BULK = ((0, 8), (8, 8), (16, 7), (23, 8), (31, 7), (38, 7))
-TALLS = ((0, 3), (3, 3), (6, 3), (9, 3), (12, 3), (15, 2))
+TALLS = ((0, 2), (2, 3), (5, 3), (8, 3), (11, 3), (14, 3))
 WAVES = (
     ((7, 1), (14, 2), (22, 1), (30, 1), (37, 1), (44, 1)),
     TALLS,

time: 169 us -> 169 us (level)
  no operation moved by 1% of the time
where the time goes in v8:
time: 169 us
  Pallas kernels  168 us (99%)
    pallas_call x1, Pallas kernels, layer(): pl.pallas_call(layer_kernel, out_shape=(jax.ShapeDtypeStruct((256, 896),...  165 us

profile of v8, /device:TPU:1, one launch (start us, length us, event | category | flops | bytes accessed | tf_op | source)
XLA Modules:
  0.0 168.6 jit_solution(149657972303896189)
XLA Ops:
  0.6 165.0 %shard_map.275 = (bf16[256,896]{1,0:T(8,128)(2,1)}, bf16[256,896]{1,0:T(8,128)(2,1)}, f32[67,16,128]{2,1,0:T(8,128)}, bf16[50,16,128]{2,1,0:T(8,128)(2,1)}) custom-call(bf16[7,896]{1,0:T(8,128)(2,1)} %w_query.1, bf16[7,128]{1,0:T(8,128)(2,1)} %w_key.1, bf16[7,128]{1,0:T(8,128)(2,1)} %w_value.1, bf16[7,896]{1,0:T(8,128)(2,1)} %w_out_.1, ...), custom_call_target="tpu_custom_call" | custom-call | tf_op jit(solution)/shard_map/pallas_call | solution.py:856
  165.7 2.8 %shard_map.276 = (bf16[256,896]{1,0:T(8,128)(2,1)}, bf16[256,896]{1,0:T(8,128)(2,1)}, f32[7,896]{1,0:T(8,128)}, f32[7,128]{1,0:T(8,128)}, f32[7,128]{1,0:T(8,128...) custom-call(f32[67,16,128]{2,1,0:T(8,128)} %get-tuple-element.26.own, ...), custom_call_target="tpu_custom_call" | custom-call | tf_op jit(solution)/shard_map/pallas_call | solution.py:946
